TPU v7x, 32 devices: a whole 2x2x4 slice. The times are simulated.
32 devices in a mesh: gx: 8 (over y, x, core), yz: 4 (over z).
Axes of the slice: x: 2, y: 2, z: 4, core: 2. Of those that a mesh axis runs over, the one named last changes fastest.
Arguments:
- positions: float32 [3, 1536], P(None, ('gx', 'yz')), may hold values from -6 to 6
- velocities: float32 [3, 1536], P(None, ('gx', 'yz')), may hold values from -6 to 6
- forces_start: float32 [3, 1536], P(None, ('gx', 'yz')), may hold values from -6 to 6
- species: int32 [1536], P(('gx', 'yz')), may hold values from 0 to 7
- live_atoms: int32 [32], P(('gx', 'yz')), may hold values from 12 to 48, as said below
- send_list: int32 [8, 384], P(None, ('gx', 'yz')), may hold values from 0 to 47, as said below
- neighbours: int32 [1536, 128], P(('gx', 'yz')), may hold values from 0 to 143, as said below
- neighbour_count: int32 [1536], P(('gx', 'yz')), may hold values from 64 to 128
- radial_weight: bfloat16 [8, 512], replicated, may hold values from -4 to 4
- species_embed: bfloat16 [2, 8, 512], replicated, may hold values from -2 to 2
- env_weight: bfloat16 [1, 512, 64], replicated, may hold values from -0.25 to 0.25
- latent_weight: bfloat16 [1, 576, 512], replicated, may hold values from -0.25 to 0.25
- readout: bfloat16 [512], replicated, may hold values from -0.0625 to 0.0625
Outputs:
- positions_end: float32 [3, 1536], P(None, ('gx', 'yz'))
- velocities_end: float32 [3, 1536], P(None, ('gx', 'yz'))
- forces_end: float32 [3, 1536], P(None, ('gx', 'yz'))
Inputs may be any that keep to these rules, and one draw needn't show every extreme that they name: `live_atoms`: atoms in use are the first ones of a domain's slots; some domain uses all 48 in every draw. `send_list`: each row names distinct atoms in use of the sending domain. `neighbours`: each entry names an own atom in use or a ghost slot.
All inputs are finite; a program needn't handle non-finite values.
Results may differ from a plain program's by a relative error of at most 0.038.
Values sent between devices are 32-bit elements; how exact they have to be, the bound alone decides.
No kernel may reach another device: no remote copies, remote signals or barrier semaphores. Data moves between devices by JAX's collectives and lax.ppermute only.
A program may use at most 64 MiB of HBM per device.

v0:
```python
import functools

import jax
import jax.numpy as jnp
from jax import lax
from jax.experimental import pallas as pl
from jax.experimental.pallas import tpu as pltpu
from jax.sharding import PartitionSpec as P

SPECIES = 8
SLOTS = 128
RADIUS = 6.0
STEP = 0.25
COUPLING = 4.0
MASSES = (1.008, 12.011, 14.007, 15.999, 32.06, 22.99, 35.45, 30.97)

LANES = 1664
DIRECTIONS = ((-1, -1), (-1, 0), (-1, 1), (0, -1), (0, 1), (1, -1), (1, 0), (1, 1))
BASIS_PAD = 16

F32 = jnp.float32
BF16 = jnp.bfloat16


def mm(left, right):
    return jnp.dot(left, right, preferred_element_type=F32)


def mm_nt(left, right):
    return lax.dot_general(left, right, (((1,), (1,)), ((), ())), preferred_element_type=F32)


def split3(values):
    high = values.astype(BF16)
    rest = values - high.astype(F32)
    mid = rest.astype(BF16)
    low = (rest - mid.astype(F32)).astype(BF16)
    return jnp.concatenate([high.astype(F32), mid.astype(F32), low.astype(F32)], axis=0).astype(BF16)


def one_hot(ids, rows):
    row_ids = lax.broadcasted_iota(jnp.int32, (rows, ids.shape[1]), 0)
    return jnp.where(row_ids == ids, 1.0, 0.0).astype(BF16)


SMEM = pl.BlockSpec(memory_space=pltpu.SMEM)
VMEM = pl.BlockSpec(memory_space=pltpu.VMEM)


def identity(size):
    row = lax.broadcasted_iota(jnp.int32, (size, size), 0)
    col = lax.broadcasted_iota(jnp.int32, (size, size), 1)
    return jnp.where(row == col, 1.0, 0.0).astype(BF16)


def padded_rows(values, rows):
    have, lanes = values.shape
    return jnp.concatenate([values, jnp.zeros((rows - have, lanes), values.dtype)], axis=0)


def sum_parts(parts):
    rows = parts.shape[0] // 3
    return parts[:rows] + parts[rows : 2 * rows] + parts[2 * rows :]


def by_direction(rows):
    return jnp.concatenate([rows[k : k + 1] for k in range(len(DIRECTIONS))], axis=1)


def put(out_ref, place_ref, blocks):
    ghost_n = blocks.shape[1] // len(DIRECTIONS)
    out_ref[...] = jnp.zeros_like(out_ref)
    for k in range(len(DIRECTIONS)):
        out_ref[place_ref[k]] = blocks[:, k * ghost_n : (k + 1) * ghost_n]


def take(in_ref, place_ref):
    return jnp.concatenate([in_ref[place_ref[k]] for k in range(len(DIRECTIONS))], axis=1)


def pick_ghosts(values, send_ref, atom_n):
    return sum_parts(mm(split3(values), one_hot(by_direction(send_ref[...]), atom_n)))


def start_kernel(
    place_ref, pos_ref, vel_ref, force_ref, species_ref, send_ref, moved_ref, half_ref, inv_ref, out_ref
):
    species = species_ref[...]
    inverse = jnp.zeros(species.shape, F32)
    for spec_id, mass in enumerate(MASSES):
        inverse = jnp.where(species == spec_id, F32(1.0 / mass), inverse)
    half = vel_ref[...] + 0.5 * STEP * inverse * force_ref[...]
    moved = pos_ref[...] + STEP * half
    inv_ref[...] = inverse
    half_ref[...] = half
    moved_ref[...] = moved
    sources = padded_rows(jnp.concatenate([moved, species.astype(F32)], axis=0), 8)
    put(out_ref, place_ref, pick_ghosts(sources, send_ref, species.shape[1])[0:4])


def total_force(place_ref, own_ref, send_ref, in_ref):
    own = own_ref[...]
    back = padded_rows(take(in_ref, place_ref), 8)
    pick = one_hot(by_direction(send_ref[...]), own.shape[1])
    return own + sum_parts(mm_nt(split3(back), pick))[0:3]


def middle_kernel(
    back_ref, place_ref, own_ref, send_ref, half_ref, moved_ref, inv_ref, in_ref, half_two_ref, end_ref, out_ref
):
    forces = total_force(back_ref, own_ref, send_ref, in_ref)
    kick = 0.5 * STEP * inv_ref[...] * forces
    half_two = half_ref[...] + kick + kick
    end = moved_ref[...] + STEP * half_two
    half_two_ref[...] = half_two
    end_ref[...] = end
    put(out_ref, place_ref, pick_ghosts(padded_rows(end, 8), send_ref, end.shape[1])[0:3])


def last_kernel(back_ref, own_ref, send_ref, half_two_ref, inv_ref, in_ref, vel_ref, force_ref):
    forces = total_force(back_ref, own_ref, send_ref, in_ref)
    force_ref[...] = forces
    vel_ref[...] = half_two_ref[...] + 0.5 * STEP * inv_ref[...] * forces


def prepare_kernel(
    live_ref,
    count_ref,
    slots_ref,
    radial_ref,
    embed_ref,
    env_t_ref,
    latent_ref,
    readout_ref,
    neigh_ref,
    centre_ref,
    total_ref,
    embed_t_ref,
    radial_t_ref,
    on_hidden_ref,
    on_inner_ref,
    on_bent_ref,
    on_weight_ref,
    readout_t_ref,
    radial_back_ref,
):
    features, latent = env_t_ref.shape
    slots_t = mm_nt(identity(slots_ref.shape[1]), slots_ref[...].astype(F32).astype(BF16)).astype(BF16)
    list_pairs(live_ref, count_ref, slots_t, neigh_ref, centre_ref, total_ref)

    eye = identity(latent)
    half = BF16(0.5)
    latent_w = latent_ref[...]
    readout = readout_ref[...]
    none = jnp.zeros((BASIS_PAD - 8, latent), BF16)
    readout16 = padded_rows(readout.astype(F32), BASIS_PAD).astype(BF16)
    radial16 = jnp.concatenate([radial_ref[...] * half, none], axis=0)
    latent_t = mm_nt(eye, latent_w * half).astype(BF16)
    on_hidden_ref[...] = jnp.concatenate([latent_t[:, :latent], env_t_ref[...], readout16], axis=0)
    on_inner_ref[...] = latent_t[:, latent:]
    on_bent_ref[...] = (latent_w.astype(F32) * (0.5 * readout.astype(F32))).astype(BF16)
    on_weight_ref[...] = mm_nt(eye, jnp.concatenate([env_t_ref[...], readout16], axis=0)).astype(BF16)
    readout_t_ref[...] = mm_nt(eye, jnp.broadcast_to(readout.astype(F32), (128, latent)).astype(BF16))
    radial_back_ref[...] = radial16
    radial_t_ref[...] = mm_nt(eye, radial16).astype(BF16)
    embed_t_ref[...] = mm_nt(eye, jnp.concatenate([embed_ref[1], embed_ref[0]], axis=0) * half).astype(BF16)


def list_pairs(live_ref, count_ref, slots_t, neigh_ref, centre_ref, total_ref):
    atom_n = count_ref.shape[1]
    slot_n = slots_t.shape[0]
    blocks, lanes = neigh_ref.shape
    atom_row = lax.broadcasted_iota(jnp.int32, (1, atom_n), 1)
    used = jnp.where(atom_row < live_ref[0], count_ref[...], 0).astype(F32)
    row_i = lax.broadcasted_iota(jnp.int32, (atom_n, atom_n), 0)
    col_i = lax.broadcasted_iota(jnp.int32, (atom_n, atom_n), 1)
    end = jnp.sum(jnp.where(col_i <= row_i, used, 0.0), axis=1, keepdims=True)
    own = jnp.sum(jnp.where(col_i == row_i, used, 0.0), axis=1, keepdims=True)
    total = jnp.sum(used)
    total_ref[0] = total.astype(jnp.int32)
    lane = lax.broadcasted_iota(jnp.int32, (1, lanes), 1)

    def one_block(block, carry):
        place = (lane + block * lanes).astype(F32)
        past = end <= place
        centre = jnp.sum(jnp.where(past, 1.0, 0.0), axis=0, keepdims=True)
        start = jnp.sum(jnp.where(past, own, 0.0), axis=0, keepdims=True)
        slot = (place - start).astype(jnp.int32)
        centre_id = centre.astype(jnp.int32)
        rows = mm(slots_t, one_hot(centre_id, atom_n))
        slot_ids = lax.broadcasted_iota(jnp.int32, (slot_n, lanes), 0)
        neigh = jnp.sum(jnp.where(slot_ids == slot, rows, 0.0), axis=0, keepdims=True)
        valid = place < total
        neigh_ref[pl.ds(block, 1), :] = jnp.where(valid, neigh.astype(jnp.int32), -1)
        centre_ref[pl.ds(block, 1), :] = jnp.where(valid, centre_id, -1)
        return carry

    lax.fori_loop(0, blocks, one_block, 0)


def prepare(live_atoms, neighbour_count, neighbours, radial_weight, species_embed, env_weight, latent_weight, readout):
    atom_n, slot_n = neighbours.shape
    latent, features = env_weight.shape[1:]
    blocks = pl.cdiv(atom_n * slot_n, LANES)
    shapes = (
        ((blocks, LANES), jnp.int32),
        ((blocks, LANES), jnp.int32),
        ((1,), jnp.int32),
        ((latent, 16), BF16),
        ((latent, BASIS_PAD), BF16),
        ((latent + features + BASIS_PAD, latent), BF16),
        ((latent, features), BF16),
        ((latent + features, latent), BF16),
        ((latent, features + BASIS_PAD), BF16),
        ((latent, 128), F32),
        ((BASIS_PAD, latent), BF16),
    )
    out = pl.pallas_call(
        prepare_kernel,
        out_shape=[jax.ShapeDtypeStruct(*shape) for shape in shapes],
        in_specs=[SMEM] + [VMEM] * 7,
        out_specs=[VMEM, VMEM, SMEM] + [VMEM] * 8,
        compiler_params=pltpu.CompilerParams(vmem_limit_bytes=24 * 2**20),
        cost_estimate=pl.CostEstimate(flops=2 * 10**9, bytes_accessed=4 * 2**20, transcendentals=0),
        name="prepare",
    )(
        live_atoms,
        neighbour_count.reshape(1, atom_n),
        neighbours,
        radial_weight,
        species_embed,
        env_weight[0].T,
        latent_weight[0],
        readout[None, :],
    )
    return out[:3], out[3:]


def silu_pair(half_in):
    bent = jnp.tanh(half_in)
    part = half_in * bent
    return half_in + part, (1.0 + bent) * (1.0 + (half_in - part))


def force_kernel(
    place_ref,
    back_ref,
    total_ref,
    neigh_ref,
    centre_ref,
    own_ref,
    own_kind_ref,
    embed_ref,
    radial_ref,
    on_hidden_ref,
    on_inner_ref,
    on_bent_ref,
    on_weight_ref,
    readout_ref,
    radial_back_ref,
    in_ref,
    *refs,
    first_call,
):
    kind_ref, own_out_ref, out_ref, *scratch = refs
    hot_s, use_s, u_s, slope_s, raw_s, part_s, ain_s, energy_s, c_s, dc_s, f_s = scratch
    blocks, lanes = neigh_ref.shape
    atom_n = own_ref.shape[1]
    ghosts = take(in_ref, place_ref)
    ext_n = atom_n + ghosts.shape[1]
    if first_call:
        ghost_kind = ghosts[3:4].astype(jnp.int32)
        kind_ref[...] = ghost_kind
    else:
        ghost_kind = kind_ref[...]
    kind = jnp.concatenate([own_kind_ref[...], ghost_kind], axis=1)
    pos = jnp.concatenate([own_ref[...], ghosts[0:3]], axis=1)
    basis_n = SPECIES
    latent, features = on_inner_ref.shape
    count = (total_ref[0] + lanes - 1) // lanes
    scale = COUPLING * SLOTS ** (-0.5)

    pos8 = padded_rows(pos, 8) * (1.0 / RADIUS)
    pos_parts = split3(jnp.concatenate([pos8, -pos8[:, :atom_n]], axis=1))
    row8 = lax.broadcasted_iota(jnp.int32, (SPECIES, ext_n), 0)
    kinds = jnp.where(row8 == kind, 1.0, 0.0)
    none = jnp.zeros((SPECIES, ext_n), F32)
    neigh_embed = mm(embed_ref[...], jnp.concatenate([kinds, none], axis=0).astype(BF16))
    own_embed = mm(
        embed_ref[...],
        jnp.concatenate([none, kinds], axis=0)[:, :atom_n].astype(BF16),
    )
    weight_in = jnp.concatenate(
        [neigh_embed, own_embed, radial_ref[...].astype(F32)], axis=1
    ).astype(BF16)

    mid_row = lax.broadcasted_iota(jnp.int32, (BASIS_PAD, lanes), 0).astype(F32)
    mids = (mid_row + 0.5) / basis_n
    sharp = 2.0 * basis_n * basis_n

    c_s[...] = jnp.zeros_like(c_s)
    dc_s[...] = jnp.zeros_like(dc_s)
    f_s[...] = jnp.zeros_like(f_s)

    def geometry(block):
        vec = u_s[block]
        square = jnp.sum(vec * vec, axis=0, keepdims=True)
        inside = jnp.maximum(1.0 - square, 0.0)
        inside = jnp.where(centre_ref[pl.ds(block, 1), :] >= 0, inside, 0.0)
        apart = square - mids
        return vec, inside, apart, jnp.exp(-sharp * apart * apart)

    def first(block, carry):
        hot_j = one_hot(neigh_ref[pl.ds(block, 1), :], ext_n)
        hot_c = one_hot(centre_ref[pl.ds(block, 1), :], atom_n)
        hot = jnp.concatenate([hot_j, hot_c], axis=0)
        hot_s[block] = hot
        u_s[block] = sum_parts(mm(pos_parts, hot))
        vec, inside, _, basis = geometry(block)
        use = jnp.concatenate([hot_c * vec[k : k + 1].astype(BF16) for k in range(3)], axis=0)
        use_s[block] = use
        pre = mm(weight_in, jnp.concatenate([hot, basis.astype(BF16)], axis=0))
        hidden, slope = silu_pair(pre)
        slope_s[block] = slope.astype(BF16)
        taken = mm(on_hidden_ref[...], hidden.astype(BF16))
        part_s[block] = taken[:latent]
        raw = taken[latent : latent + features]
        raw_s[block] = raw
        energy_s[block] = taken[latent + features : latent + features + 8]
        c_s[...] += mm_nt((raw * (inside * inside)).astype(BF16), use)
        return carry

    lax.fori_loop(0, count, first, 0)
    c_all = c_s[...] * scale
    c_b = c_all.astype(BF16)

    def second(block, carry):
        _, inside, _, _ = geometry(block)
        use = use_s[block]
        env = inside * inside
        weight = raw_s[block] * env
        inner = weight * mm(c_b, use)
        later = part_s[block] + mm(on_inner_ref[...], inner.astype(BF16))
        gain, bent = silu_pair(later)
        readout = jnp.concatenate([readout_ref[...]] * (lanes // 128), axis=1)
        energy_s[block] += jnp.sum(gain * readout, axis=0, keepdims=True)
        taken = mm(on_bent_ref[...], bent.astype(BF16))
        part_s[block] = taken[:latent]
        a_in = taken[latent:] * env
        ain_s[block] = a_in
        dc_s[...] += mm_nt((a_in * weight).astype(BF16), use)
        return carry

    lax.fori_loop(0, count, second, 0)
    c_dc = jnp.concatenate([c_all, dc_s[...] * scale], axis=0).astype(BF16)
    both = jnp.concatenate([c_all.T, dc_s[...].T * scale], axis=1).astype(BF16)

    def third(block, carry):
        vec, inside, apart, basis = geometry(block)
        use = use_s[block]
        hot = hot_s[block]
        env = inside * inside
        raw = raw_s[block]
        weight = raw * env
        a_in = ain_s[block]
        along = mm(c_dc, use)
        d_weight = a_in * along[:features] + along[features:]
        d_env = jnp.sum(d_weight * raw, axis=0, keepdims=True) + energy_s[block][0:1]
        ones = jnp.ones((BASIS_PAD, lanes), BF16)
        d_hidden = part_s[block] + mm(
            on_weight_ref[...], jnp.concatenate([d_weight.astype(BF16), ones], axis=0)
        )
        d_pre = (d_hidden * slope_s[block].astype(F32)).astype(BF16)
        d_basis = mm(radial_back_ref[...], d_pre)
        d_square = env * jnp.sum(d_basis * basis * apart, axis=0, keepdims=True) * (-2.0 * sharp)
        d_square = d_square - 2.0 * inside * d_env
        d_all = mm(both, jnp.concatenate([a_in * weight, weight], axis=0).astype(BF16))
        hot_c = hot[ext_n:].astype(F32)
        picked = [
            jnp.sum(d_all[k * atom_n : (k + 1) * atom_n] * hot_c, axis=0, keepdims=True)
            for k in range(3)
        ]
        d_vec = jnp.concatenate(picked + [jnp.zeros((5, lanes), F32)], axis=0)
        d_vec = (d_vec + 2.0 * d_square * vec) * (1.0 / RADIUS)
        f_s[...] += mm_nt(split3(d_vec), hot)
        return carry

    lax.fori_loop(0, count, third, 0)
    summed = f_s[0:8] + f_s[8:16] + f_s[16:24]
    on_centre = summed[0:3, ext_n:]
    on_neigh = summed[0:3, :ext_n]
    own_out_ref[...] = on_centre - on_neigh[:, :atom_n]
    put(out_ref, back_ref, -on_neigh[:, atom_n:])


def exchange_shape(devices, rows, ghost_n):
    return [jax.ShapeDtypeStruct((devices, rows, ghost_n), F32)]


def pair_forces(places, pairs, own_pos, own_kind, ghost_kind, incoming, weights, devices):
    neigh, centre, total = pairs
    blocks, lanes = neigh.shape
    latent, features = weights[3].shape
    atom_n = own_pos.shape[1]
    ghost_n = incoming.shape[-1]
    ghost_all = ghost_n * len(DIRECTIONS)
    ext_n = atom_n + ghost_all
    first_call = ghost_kind is None
    operands = [*places, total, neigh, centre, own_pos, own_kind, *weights, incoming]
    out_shape = [jax.ShapeDtypeStruct((3, atom_n), F32)] + exchange_shape(devices, 3, ghost_n)
    if first_call:
        out_shape = [jax.ShapeDtypeStruct((1, ghost_all), jnp.int32)] + out_shape
    else:
        operands.append(ghost_kind)
    pair_rows = blocks * lanes
    return pl.pallas_call(
        functools.partial(force_kernel, first_call=first_call),
        out_shape=out_shape,
        in_specs=[SMEM] * 3 + [VMEM] * (len(operands) - 3),
        out_specs=[VMEM] * len(out_shape),
        scratch_shapes=[
            pltpu.VMEM((blocks, ext_n + atom_n, lanes), BF16),
            pltpu.VMEM((blocks, 3 * atom_n, lanes), BF16),
            pltpu.VMEM((blocks, 8, lanes), F32),
            pltpu.VMEM((blocks, latent, lanes), BF16),
            pltpu.VMEM((blocks, features, lanes), F32),
            pltpu.VMEM((blocks, latent, lanes), F32),
            pltpu.VMEM((blocks, features, lanes), F32),
            pltpu.VMEM((blocks, 8, lanes), F32),
            pltpu.VMEM((features, 3 * atom_n), F32),
            pltpu.VMEM((features, 3 * atom_n), F32),
            pltpu.VMEM((24, ext_n + atom_n), F32),
        ],
        compiler_params=pltpu.CompilerParams(vmem_limit_bytes=48 * 2**20),
        cost_estimate=pl.CostEstimate(
            flops=pair_rows * latent * 2700, bytes_accessed=4 * 2**20, transcendentals=0
        ),
        name="pair_forces",
    )(*operands)


def small_call(kernel, name, smem_n, operands, out_shape):
    return pl.pallas_call(
        kernel,
        out_shape=out_shape,
        in_specs=[SMEM] * smem_n + [VMEM] * (len(operands) - smem_n),
        out_specs=[VMEM] * len(out_shape),
        compiler_params=pltpu.CompilerParams(vmem_limit_bytes=16 * 2**20),
        name=name,
    )(*operands)


def neighbour_devices(step):
    gx_n, yz_n = lax.axis_size("gx"), lax.axis_size("yz")
    gx, yz = lax.axis_index("gx"), lax.axis_index("yz")
    step_gx = jnp.array([a for a, _ in DIRECTIONS], jnp.int32) * step
    step_yz = jnp.array([b for _, b in DIRECTIONS], jnp.int32) * step
    return ((gx + step_gx + gx_n) % gx_n) * yz_n + (yz + step_yz + yz_n) % yz_n


def exchange(blocks):
    return lax.all_to_all(blocks, ("gx", "yz"), 0, 0, tiled=True)


def body(
    positions,
    velocities,
    forces_start,
    species,
    live_atoms,
    send_list,
    neighbours,
    neighbour_count,
    radial_weight,
    species_embed,
    env_weight,
    latent_weight,
    readout,
):
    atom_n = positions.shape[1]
    ghost_n = send_list.shape[1]
    devices = lax.axis_size("gx") * lax.axis_size("yz")
    ahead, behind = neighbour_devices(1), neighbour_devices(-1)
    kinds = species.reshape(1, atom_n)
    atoms = jax.ShapeDtypeStruct((3, atom_n), F32)
    row = jax.ShapeDtypeStruct((1, atom_n), F32)

    moved, half, inverse, sent = small_call(
        start_kernel,
        "start",
        1,
        [ahead, positions, velocities, forces_start, kinds, send_list],
        [atoms, atoms, row] + exchange_shape(devices, 4, ghost_n),
    )
    got = exchange(sent)
    pairs, weights = prepare(
        live_atoms, neighbour_count, neighbours, radial_weight, species_embed, env_weight, latent_weight, readout
    )
    places = (behind, behind)
    ghost_kind, own, sent = pair_forces(
        places, pairs, moved, kinds, None, got, weights, devices
    )
    got = exchange(sent)
    half_two, positions_end, sent = small_call(
        middle_kernel,
        "middle",
        2,
        [ahead, ahead, own, send_list, half, moved, inverse, got],
        [atoms, atoms] + exchange_shape(devices, 3, ghost_n),
    )
    got = exchange(sent)
    own, sent = pair_forces(
        places, pairs, positions_end, kinds, ghost_kind, got, weights, devices
    )
    got = exchange(sent)
    velocities_end, forces_end = small_call(
        last_kernel, "last", 1, [ahead, own, send_list, half_two, inverse, got], [atoms, atoms]
    )
    return (positions_end, velocities_end, forces_end)


def solution(mesh):
    placed = (
        P(None, ("gx", "yz")),
        P(None, ("gx", "yz")),
        P(None, ("gx", "yz")),
        P(("gx", "yz")),
        P(("gx", "yz")),
        P(None, ("gx", "yz")),
        P(("gx", "yz"), None),
        P(("gx", "yz")),
        P(),
        P(),
        P(),
        P(),
        P(),
    )
    return jax.shard_map(
        body,
        mesh=mesh,
        in_specs=placed,
        out_specs=(P(None, ("gx", "yz")), P(None, ("gx", "yz")), P(None, ("gx", "yz"))),
        check_vma=False,
    )
```

profile of v0, /device:TPU:0, one launch (start us, length us, event | category | flops | bytes accessed | tf_op | source)
XLA Modules:
  0.0 93.5 jit_solution(9737883591943648636)
XLA Ops:
  0.6 0.0 copy-start.15
  0.6 0.0 copy-start.16
  0.7 0.0 copy-start.4
  0.7 0.0 copy-start.3
  0.7 0.0 copy-start
  0.7 0.6 copy-done.15
  1.3 0.0 copy-done.16
  1.3 0.0 copy-start.1
  1.3 0.0 copy-start.2
  1.3 0.0 copy-done.4
  1.3 0.0 copy-done.3
  1.4 0.0 copy-done
  1.4 0.6 copy-done.1
  2.0 0.0 copy-done.2
  2.0 1.4 %start.1 = (f32[3,48]{1,0:T(4,128)S(1)}, f32[3,48]{1,0:T(4,128)S(1)}, f32[1,48]{1,0:T(1,128)S(1)}, f32[32,4,12]{2,1,0:T(4,128)}) custom-call(s32[8]{0:T(128)S(1)} %fusion.place_ref.back_ref, f32[3,48]{1,0:T(4,128)S(1)} %copy-done.1, f32[3,48]{1,0:T(4,128)S(1)} %copy-done.2, f32[3,48]{1,0:T(4,128)S(1)} %copy-done.3, s32[1,48]{1,0:T(1,128)S(1)} %bitcast.6, ...), custom_call_target="tpu_custom_call" | custom-call | tf_op jit(solution)/shard_map/start/pallas_call | solution.py:443
  3.4 0.0 copy-start.12
  3.4 0.0 copy-start.13
  3.5 0.0 copy-start.14
  3.5 0.0 copy-start.6
  3.5 0.0 copy-start.7
  3.5 0.0 copy-start.8
  3.5 7.3 %all-to-all-start = ((f32[32,4,12]{2,1,0:T(4,128)}), f32[32,4,12]{2,1,0:T(4,128)S(1)}, u32[]{:S(2)}, u32[]{:S(2)}) async-start(f32[32,4,12]{2,1,0:T(4,128)} %get-tuple-element.40), calls=%async_computation | async-start | bytes 131072 | tf_op jit(solution)/shard_map/all_to_all | solution.py:462
  10.8 0.0 copy-start.9
  11.5 0.0 copy-done.12
  11.5 0.0 copy-done.13
  11.5 0.0 copy-done.14
  11.5 0.0 copy-start.11
  11.5 0.0 copy-done.6
  11.6 0.0 copy-done.7
  11.6 0.0 copy-done.8
  11.6 0.0 copy-done.9
  11.6 0.6 copy-done.11
  12.2 0.0 copy-start.5
  12.2 1.1 %copy-done.5 = bf16[1,576,512]{2,1,0:T(8,128)(2,1)S(1)} copy-done((bf16[1,576,512]{2,1,0:T(8,128)(2,1)S(1)}, bf16[1,576,512]{2,1,0:T(8,128)(2,1)}, u32[]{:S(2)}) %copy-start.5) | copy-done | bytes 589848
  13.3 2.6 %prepare.1 = (s32[4,1664]{1,0:T(4,128)S(1)}, s32[4,1664]{1,0:T(4,128)S(1)}, s32[1]{0:T(128)}, bf16[512,16]{1,0:T(8,128)(2,1)S(1)}, bf16[512,16]{1,0:T(8,128)(2,1...) custom-call(s32[1]{0:T(128)S(6)} %copy.20.live_ref, ...), custom_call_target="tpu_custom_call" | custom-call | flops 2000000000 | bytes 4194304 | tf_op jit(solution)/shard_map/prepare/pallas_call | solution.py:218
  15.9 2.4 %all-to-all-done.in_ref = f32[32,4,12]{2,1,0:T(4,128)S(1)} async-done(((f32[32,4,12]{2,1,0:T(4,128)}), f32[32,4,12]{2,1,0:T(4,128)S(1)}, u32[]{:S(2)}, u32[]{:S(2)}) %all-to-all-start) | async-done | bytes 6176 | tf_op jit(solution)/shard_map/all_to_all | solution.py:462
  18.3 8.8 %pair_forces.2 = (s32[1,96]{1,0:T(1,128)S(1)}, f32[3,48]{1,0:T(4,128)S(1)}, f32[32,3,12]{2,1,0:T(4,128)S(1)}) custom-call(s32[8]{0:T(128)S(1)} %fusion.1.place_ref.back_ref, s32[8]{0:T(128)S(1)} %fusion.1.place_ref.back_ref, s32[1]{0:T(128)} %get-tuple-element.28.total_ref, s32[4,1664]{1,0:T(4,128)S(1)} %get-tuple-element.29.neigh_ref, ...), custom_call_target="tpu_custom_call" | custom-call | flops 9201254400 | bytes 4194304 | tf_op jit(solution)/shard_map/pair_forces/pallas_call | solution.py:416
  27.1 23.2 %all_to_all.20.in_ref = f32[32,3,12]{2,1,0:T(4,128)S(1)} all-to-all(f32[32,3,12]{2,1,0:T(4,128)S(1)} %get-tuple-element.44), channel_id=1, replica_groups=mesh['gx'=8,'yz'=4] {'gx','yz'}, dimensions={0} | all-to-all | bytes 9216 | tf_op jit(solution)/shard_map/all_to_all | solution.py:462
  50.3 1.3 %middle.1 = (f32[3,48]{1,0:T(4,128)S(1)}, f32[3,48]{1,0:T(4,128)}, f32[32,3,12]{2,1,0:T(4,128)S(1)}) custom-call(s32[8]{0:T(128)S(1)} %fusion.place_ref.back_ref, s32[8]{0:T(128)S(1)} %fusion.place_ref.back_ref, f32[3,48]{1,0:T(4,128)S(1)} %get-tuple-element.41.own_ref, s32[8,12]{1,0:T(8,128)S(1)} %copy-done, f32[3,48]{1,0:T(4,128)S(1)} %get-tuple-element.42.half_ref, ...), custom_call_target="tpu_custom_call" | custom-call | tf_op jit(solution)/shard_map/middle/pallas_call | solution.py:443
  51.6 9.2 %all_to_all.21.in_ref = f32[32,3,12]{2,1,0:T(4,128)S(1)} all-to-all(f32[32,3,12]{2,1,0:T(4,128)S(1)} %get-tuple-element.46), channel_id=1, replica_groups=mesh['gx'=8,'yz'=4] {'gx','yz'}, dimensions={0} | all-to-all | bytes 9216 | tf_op jit(solution)/shard_map/all_to_all | solution.py:462
  60.8 0.0 copy-start.10
  60.8 0.7 copy-done.10
  61.5 8.9 %pair_forces.3 = (f32[3,48]{1,0:T(4,128)S(1)}, f32[32,3,12]{2,1,0:T(4,128)S(1)}) custom-call(s32[8]{0:T(128)S(1)} %fusion.1.place_ref.back_ref, s32[8]{0:T(128)S(1)} %fusion.1.place_ref.back_ref, s32[1]{0:T(128)} %get-tuple-element.28.total_ref, s32[4,1664]{1,0:T(4,128)S(1)} %get-tuple-element.29.neigh_ref, s32[4,1664]{1,0:T(4,128)S(1)} %get-tuple-element.30.centre_ref, ...), custom_call_target="tpu_custom_call" | custom-call | flops 9201254400 | bytes 4194304 | tf_op jit(solution)/shard_map/pair_forces/pallas_call | solution.py:416
  70.3 21.8 %all_to_all.22.in_ref = f32[32,3,12]{2,1,0:T(4,128)S(1)} all-to-all(f32[32,3,12]{2,1,0:T(4,128)S(1)} %get-tuple-element.50), channel_id=1, replica_groups=mesh['gx'=8,'yz'=4] {'gx','yz'}, dimensions={0} | all-to-all | bytes 9216 | tf_op jit(solution)/shard_map/all_to_all | solution.py:462
  92.1 1.3 %last.1 = (f32[3,48]{1,0:T(4,128)}, f32[3,48]{1,0:T(4,128)}) custom-call(s32[8]{0:T(128)S(1)} %fusion.place_ref.back_ref, f32[3,48]{1,0:T(4,128)S(1)} %get-tuple-element.48.own_ref, s32[8,12]{1,0:T(8,128)S(1)} %copy-done, f32[3,48]{1,0:T(4,128)S(1)} %get-tuple-element.49.half_two_ref, f32[1,48]{1,0:T(1,128)S(1)} %get-tuple-element.43.inv_ref, ...), custom_call_target="tpu_custom_call" | custom-call | tf_op jit(solution)/shard_map/last/pallas_call | solution.py:443
  (3 shorter events, 0.0 us)
Async XLA Ops:
  0.6 0.7 copy-start.15
  0.6 0.7 copy-start.16
  0.7 0.7 copy-start.4
  0.7 0.7 copy-start.3
  0.7 0.7 copy-start
  1.3 0.7 copy-start.1
  1.3 0.7 copy-start.2
  3.4 8.0 %copy-start.12 = (bf16[512]{0:T(512)(128)(2,1)S(1)}, bf16[512]{0:T(512)(128)(2,1)}, u32[]{:S(2)}) copy-start(bf16[512]{0:T(512)(128)(2,1)} %param.29) | copy-start | bytes 3076
  3.4 8.0 %copy-start.13 = (s32[8]{0:T(128)S(1)}, s32[8]{0:T(128)}, u32[]{:S(2)}) copy-start(s32[8]{0:T(128)} %constant.64) | copy-start | bytes 100
  3.5 8.0 %copy-start.14 = (s32[8]{0:T(128)S(1)}, s32[8]{0:T(128)}, u32[]{:S(2)}) copy-start(s32[8]{0:T(128)} %constant.63) | copy-start | bytes 100
  3.5 8.1 %copy-start.6 = (bf16[1,512,64]{1,2,0:T(8,128)(2,1)S(1)}, bf16[1,512,64]{1,2,0:T(8,128)(2,1)}, u32[]{:S(2)}) copy-start(bf16[1,512,64]{1,2,0:T(8,128)(2,1)} %param.27) | copy-start | bytes 196612
  3.5 8.1 %copy-start.7 = (s32[48,128]{1,0:T(8,128)S(1)}, s32[48,128]{1,0:T(8,128)}, u32[]{:S(2)}) copy-start(s32[48,128]{1,0:T(8,128)} %slots_ref.1) | copy-start | bytes 73732
  3.5 8.1 %copy-start.8 = (bf16[2,8,512]{2,1,0:T(8,128)(2,1)S(1)}, bf16[2,8,512]{2,1,0:T(8,128)(2,1)}, u32[]{:S(2)}) copy-start(bf16[2,8,512]{2,1,0:T(8,128)(2,1)} %embed_ref.1) | copy-start | bytes 49156
  3.5 14.8 %all-to-all-start = ((f32[32,4,12]{2,1,0:T(4,128)}), f32[32,4,12]{2,1,0:T(4,128)S(1)}, u32[]{:S(2)}, u32[]{:S(2)}) async-start(f32[32,4,12]{2,1,0:T(4,128)} %get-tuple-element.40), calls=%async_computation | async-start | bytes 131072 | tf_op jit(solution)/shard_map/all_to_all | solution.py:462
  10.8 0.8 copy-start.9
  11.5 0.7 copy-start.11
  12.2 1.1 %copy-start.5 = (bf16[1,576,512]{2,1,0:T(8,128)(2,1)S(1)}, bf16[1,576,512]{2,1,0:T(8,128)(2,1)}, u32[]{:S(2)}) copy-start(bf16[1,576,512]{2,1,0:T(8,128)(2,1)} %param.28) | copy-start | bytes 1769476
  60.8 0.7 copy-start.10
where the time goes:
time: 93.6 us; the launch traced here: 93.5 us
  blocking collectives  54.2 us (58%)
  Pallas kernels  24.4 us (26%)
  starting transfers between devices  7.3 us (8%)
  local copies, waits for them, and re-layouts  3.7 us (4%)
  waiting for transfers between devices  2.42 us (3%)
  between operations  1.48 us (2%)
    all_to_all x3, blocking collectives, exchange(): return lax.all_to_all(blocks, ('gx', 'yz'), 0, 0, tiled=True)  54.2 us
    pallas_call x2, Pallas kernels, pair_forces(): pl.pallas_call(functools.partial(force_kernel, first_call=first_call), ou...  17.7 us
    all_to_all x1, starting transfers between devices, exchange(): return lax.all_to_all(blocks, ('gx', 'yz'), 0, 0, tiled=True)  7.3 us
    pallas_call x3, Pallas kernels, small_call(): pl.pallas_call(kernel, out_shape=out_shape, in_specs=[SMEM] * smem_n + [V...  4.11 us
    unnamed x34, local copies, waits for them, and re-layouts  3.7 us
    pallas_call x1, Pallas kernels, prepare(): pl.pallas_call(prepare_kernel, out_shape=[jax.ShapeDtypeStruct(*shape) fo...  2.61 us
    all_to_all x1, waiting for transfers between devices, exchange(): return lax.all_to_all(blocks, ('gx', 'yz'), 0, 0, tiled=True)  2.42 us
  transfers between devices with their start and end apart: 1, of which 1 were waited for; matrix products, arithmetic and copies ran while one was open for 0% of the time, Pallas kernels for 3%

commit v1 on v0

--- a/solution.py
+++ b/solution.py
@@ -14,7 +14,7 @@
 COUPLING = 4.0
 MASSES = (1.008, 12.011, 14.007, 15.999, 32.06, 22.99, 35.45, 30.97)
 
-LANES = 1664
+LANES = 1024
 DIRECTIONS = ((-1, -1), (-1, 0), (-1, 1), (0, -1), (0, 1), (1, -1), (1, 0), (1, 1))
 BASIS_PAD = 16
 
@@ -82,45 +82,53 @@
     return sum_parts(mm(split3(values), one_hot(by_direction(send_ref[...]), atom_n)))
 
 
-def start_kernel(
-    place_ref, pos_ref, vel_ref, force_ref, species_ref, send_ref, moved_ref, half_ref, inv_ref, out_ref
-):
-    species = species_ref[...]
+def inverse_mass(species):
     inverse = jnp.zeros(species.shape, F32)
     for spec_id, mass in enumerate(MASSES):
         inverse = jnp.where(species == spec_id, F32(1.0 / mass), inverse)
+    return inverse
+
+
+def start_kernel(
+    place_ref, pos_ref, vel_ref, force_ref, species_ref, send_ref, moved_ref, half_ref, out_ref
+):
+    species = species_ref[...]
+    inverse = inverse_mass(species)
     half = vel_ref[...] + 0.5 * STEP * inverse * force_ref[...]
     moved = pos_ref[...] + STEP * half
-    inv_ref[...] = inverse
     half_ref[...] = half
     moved_ref[...] = moved
-    sources = padded_rows(jnp.concatenate([moved, species.astype(F32)], axis=0), 8)
-    put(out_ref, place_ref, pick_ghosts(sources, send_ref, species.shape[1])[0:4])
-
-
-def total_force(place_ref, own_ref, send_ref, in_ref):
-    own = own_ref[...]
-    back = padded_rows(take(in_ref, place_ref), 8)
-    pick = one_hot(by_direction(send_ref[...]), own.shape[1])
-    return own + sum_parts(mm_nt(split3(back), pick))[0:3]
-
-
-def middle_kernel(
-    back_ref, place_ref, own_ref, send_ref, half_ref, moved_ref, inv_ref, in_ref, half_two_ref, end_ref, out_ref
-):
-    forces = total_force(back_ref, own_ref, send_ref, in_ref)
-    kick = 0.5 * STEP * inv_ref[...] * forces
-    half_two = half_ref[...] + kick + kick
-    end = moved_ref[...] + STEP * half_two
-    half_two_ref[...] = half_two
-    end_ref[...] = end
-    put(out_ref, place_ref, pick_ghosts(padded_rows(end, 8), send_ref, end.shape[1])[0:3])
-
-
-def last_kernel(back_ref, own_ref, send_ref, half_two_ref, inv_ref, in_ref, vel_ref, force_ref):
-    forces = total_force(back_ref, own_ref, send_ref, in_ref)
+    spare = jnp.zeros((1, species.shape[1]), F32)
+    sources = jnp.concatenate([moved, species.astype(F32), half, spare], axis=0)
+    picked = pick_ghosts(sources, send_ref, species.shape[1])
+    sends = jnp.concatenate([send_ref[...].astype(F32)] * len(DIRECTIONS), axis=1)
+    put(out_ref, place_ref, jnp.concatenate([picked, sends], axis=0))
+
+
+def total_force(own, back, sends):
+    pick = one_hot(by_direction(sends), own.shape[1])
+    return own + sum_parts(mm_nt(split3(padded_rows(back, 8)), pick))[0:3]
+
+
+def domain_force(all_ref, owner, around_ref, first, sends, atom_n):
+    ghost_n = sends.shape[1]
+    back = []
+    for k in range(len(DIRECTIONS)):
+        start = atom_n + k * ghost_n
+        back.append(all_ref[around_ref[first + k]][:, start : start + ghost_n])
+    return total_force(all_ref[owner][:, :atom_n], jnp.concatenate(back, axis=1), sends)
+
+
+def step_on(moved, half, kinds, forces):
+    kick = 0.5 * STEP * inverse_mass(kinds) * forces
+    half_two = half + kick + kick
+    return half_two, moved + STEP * half_two
+
+
+def last_kernel(place_ref, own_ref, send_ref, half_two_ref, species_ref, in_ref, vel_ref, force_ref):
+    forces = total_force(own_ref[...], take(in_ref, place_ref), send_ref[...])
     force_ref[...] = forces
-    vel_ref[...] = half_two_ref[...] + 0.5 * STEP * inv_ref[...] * forces
+    vel_ref[...] = half_two_ref[...] + 0.5 * STEP * inverse_mass(species_ref[...]) * forces
 
 
 def prepare_kernel(
@@ -244,11 +252,11 @@
 
 def force_kernel(
     place_ref,
-    back_ref,
     total_ref,
+    around_ref,
     neigh_ref,
     centre_ref,
-    own_ref,
+    moved_ref,
     own_kind_ref,
     embed_ref,
     radial_ref,
@@ -260,21 +268,38 @@
     radial_back_ref,
     in_ref,
     *refs,
-    first_call,
+    second_call,
 ):
-    kind_ref, own_out_ref, out_ref, *scratch = refs
-    hot_s, use_s, u_s, slope_s, raw_s, part_s, ain_s, energy_s, c_s, dc_s, f_s = scratch
+    *refs, hot_s, use_s, u_s, slope_s, raw_s, part_s, ain_s, energy_s, c_s, dc_s, f_s = refs
     blocks, lanes = neigh_ref.shape
-    atom_n = own_ref.shape[1]
+    atom_n = moved_ref.shape[1]
     ghosts = take(in_ref, place_ref)
+    ghost_n = ghosts.shape[1] // len(DIRECTIONS)
     ext_n = atom_n + ghosts.shape[1]
-    if first_call:
-        ghost_kind = ghosts[3:4].astype(jnp.int32)
-        kind_ref[...] = ghost_kind
+    ghost_kind = ghosts[3:4].astype(jnp.int32)
+    own_kind = own_kind_ref[...]
+    if second_call:
+        half_ref, send_ref, all_ref, half_two_ref, end_ref, own_out_ref, out_ref = refs
+        on_ghosts = []
+        for k in range(len(DIRECTIONS)):
+            owner = place_ref[k]
+            sends = ghosts[8:16, k * ghost_n : (k + 1) * ghost_n].astype(jnp.int32)
+            whole = domain_force(all_ref, owner, around_ref, k * 8, sends, atom_n)
+            picked = mm(split3(padded_rows(whole, 8)), one_hot(sends[k : k + 1], atom_n))
+            on_ghosts.append(sum_parts(picked)[0:3])
+        _, ghost_pos = step_on(
+            ghosts[0:3], ghosts[4:7], ghost_kind, jnp.concatenate(on_ghosts, axis=1)
+        )
+        here = len(DIRECTIONS)
+        whole = domain_force(all_ref, place_ref[here], around_ref, here * 8, send_ref[...], atom_n)
+        half_two, own_pos = step_on(moved_ref[...], half_ref[...], own_kind, whole)
+        half_two_ref[...] = half_two
+        end_ref[...] = own_pos
     else:
-        ghost_kind = kind_ref[...]
-    kind = jnp.concatenate([own_kind_ref[...], ghost_kind], axis=1)
-    pos = jnp.concatenate([own_ref[...], ghosts[0:3]], axis=1)
+        (out_ref,) = refs
+        own_pos, ghost_pos = moved_ref[...], ghosts[0:3]
+    kind = jnp.concatenate([own_kind, ghost_kind], axis=1)
+    pos = jnp.concatenate([own_pos, ghost_pos], axis=1)
     basis_n = SPECIES
     latent, features = on_inner_ref.shape
     count = (total_ref[0] + lanes - 1) // lanes
@@ -320,9 +345,9 @@
         use = jnp.concatenate([hot_c * vec[k : k + 1].astype(BF16) for k in range(3)], axis=0)
         use_s[block] = use
         pre = mm(weight_in, jnp.concatenate([hot, basis.astype(BF16)], axis=0))
-        hidden, slope = silu_pair(pre)
-        slope_s[block] = slope.astype(BF16)
-        taken = mm(on_hidden_ref[...], hidden.astype(BF16))
+        hidden, slope = silu_pair(pre.astype(BF16))
+        slope_s[block] = slope
+        taken = mm(on_hidden_ref[...], hidden)
         part_s[block] = taken[:latent]
         raw = taken[latent : latent + features]
         raw_s[block] = raw
@@ -341,10 +366,10 @@
         weight = raw_s[block] * env
         inner = weight * mm(c_b, use)
         later = part_s[block] + mm(on_inner_ref[...], inner.astype(BF16))
-        gain, bent = silu_pair(later)
+        gain, bent = silu_pair(later.astype(BF16))
         readout = jnp.concatenate([readout_ref[...]] * (lanes // 128), axis=1)
-        energy_s[block] += jnp.sum(gain * readout, axis=0, keepdims=True)
-        taken = mm(on_bent_ref[...], bent.astype(BF16))
+        energy_s[block] += jnp.sum(gain.astype(F32) * readout, axis=0, keepdims=True)
+        taken = mm(on_bent_ref[...], bent)
         part_s[block] = taken[:latent]
         a_in = taken[latent:] * env
         ain_s[block] = a_in
@@ -370,7 +395,7 @@
         d_hidden = part_s[block] + mm(
             on_weight_ref[...], jnp.concatenate([d_weight.astype(BF16), ones], axis=0)
         )
-        d_pre = (d_hidden * slope_s[block].astype(F32)).astype(BF16)
+        d_pre = d_hidden.astype(BF16) * slope_s[block]
         d_basis = mm(radial_back_ref[...], d_pre)
         d_square = env * jnp.sum(d_basis * basis * apart, axis=0, keepdims=True) * (-2.0 * sharp)
         d_square = d_square - 2.0 * inside * d_env
@@ -389,32 +414,32 @@
     summed = f_s[0:8] + f_s[8:16] + f_s[16:24]
     on_centre = summed[0:3, ext_n:]
     on_neigh = summed[0:3, :ext_n]
-    own_out_ref[...] = on_centre - on_neigh[:, :atom_n]
-    put(out_ref, back_ref, -on_neigh[:, atom_n:])
-
-
-def exchange_shape(devices, rows, ghost_n):
-    return [jax.ShapeDtypeStruct((devices, rows, ghost_n), F32)]
-
-
-def pair_forces(places, pairs, own_pos, own_kind, ghost_kind, incoming, weights, devices):
+    own = on_centre - on_neigh[:, :atom_n]
+    if second_call:
+        own_out_ref[...] = own
+        put(out_ref, place_ref, -on_neigh[:, atom_n:])
+    else:
+        every = jnp.concatenate([own, -on_neigh[:, atom_n:]], axis=1)
+        out_ref[...] = jnp.broadcast_to(every[None], out_ref.shape)
+
+
+def pair_forces(places, pairs, own_pos, own_kind, weights, incoming, second=()):
+    place, around = places
     neigh, centre, total = pairs
     blocks, lanes = neigh.shape
     latent, features = weights[3].shape
     atom_n = own_pos.shape[1]
-    ghost_n = incoming.shape[-1]
-    ghost_all = ghost_n * len(DIRECTIONS)
-    ext_n = atom_n + ghost_all
-    first_call = ghost_kind is None
-    operands = [*places, total, neigh, centre, own_pos, own_kind, *weights, incoming]
-    out_shape = [jax.ShapeDtypeStruct((3, atom_n), F32)] + exchange_shape(devices, 3, ghost_n)
-    if first_call:
-        out_shape = [jax.ShapeDtypeStruct((1, ghost_all), jnp.int32)] + out_shape
+    devices, _, ghost_n = incoming.shape
+    ext_n = atom_n + ghost_n * len(DIRECTIONS)
+    operands = [place, total, around, neigh, centre, own_pos, own_kind, *weights, incoming, *second]
+    if second:
+        out_shape = [jax.ShapeDtypeStruct((3, atom_n), F32)] * 3
+        out_shape.append(jax.ShapeDtypeStruct((devices, 3, ghost_n), F32))
     else:
-        operands.append(ghost_kind)
+        out_shape = [jax.ShapeDtypeStruct((devices, 3, ext_n), F32)]
     pair_rows = blocks * lanes
     return pl.pallas_call(
-        functools.partial(force_kernel, first_call=first_call),
+        functools.partial(force_kernel, second_call=bool(second)),
         out_shape=out_shape,
         in_specs=[SMEM] * 3 + [VMEM] * (len(operands) - 3),
         out_specs=[VMEM] * len(out_shape),
@@ -450,12 +475,11 @@
     )(*operands)
 
 
-def neighbour_devices(step):
+def devices_at(shift_gx, shift_yz):
     gx_n, yz_n = lax.axis_size("gx"), lax.axis_size("yz")
-    gx, yz = lax.axis_index("gx"), lax.axis_index("yz")
-    step_gx = jnp.array([a for a, _ in DIRECTIONS], jnp.int32) * step
-    step_yz = jnp.array([b for _, b in DIRECTIONS], jnp.int32) * step
-    return ((gx + step_gx + gx_n) % gx_n) * yz_n + (yz + step_yz + yz_n) % yz_n
+    gx = (lax.axis_index("gx") + jnp.asarray(shift_gx, jnp.int32) + gx_n) % gx_n
+    yz = (lax.axis_index("yz") + jnp.asarray(shift_yz, jnp.int32) + yz_n) % yz_n
+    return gx * yz_n + yz
 
 
 def exchange(blocks):
@@ -480,41 +504,35 @@
     atom_n = positions.shape[1]
     ghost_n = send_list.shape[1]
     devices = lax.axis_size("gx") * lax.axis_size("yz")
-    ahead, behind = neighbour_devices(1), neighbour_devices(-1)
+    ahead = devices_at([a for a, _ in DIRECTIONS], [b for _, b in DIRECTIONS])
+    sources = [(-a, -b) for a, b in DIRECTIONS] + [(0, 0)]
+    behind = devices_at([a for a, _ in sources], [b for _, b in sources])
+    around = devices_at(
+        [a + c for a, _ in sources for c, _ in DIRECTIONS], [b + d for _, b in sources for _, d in DIRECTIONS]
+    )
     kinds = species.reshape(1, atom_n)
     atoms = jax.ShapeDtypeStruct((3, atom_n), F32)
-    row = jax.ShapeDtypeStruct((1, atom_n), F32)
-
-    moved, half, inverse, sent = small_call(
+
+    moved, half, sent = small_call(
         start_kernel,
         "start",
         1,
         [ahead, positions, velocities, forces_start, kinds, send_list],
-        [atoms, atoms, row] + exchange_shape(devices, 4, ghost_n),
+        [atoms, atoms, jax.ShapeDtypeStruct((devices, 16, ghost_n), F32)],
     )
     got = exchange(sent)
     pairs, weights = prepare(
         live_atoms, neighbour_count, neighbours, radial_weight, species_embed, env_weight, latent_weight, readout
     )
-    places = (behind, behind)
-    ghost_kind, own, sent = pair_forces(
-        places, pairs, moved, kinds, None, got, weights, devices
-    )
-    got = exchange(sent)
-    half_two, positions_end, sent = small_call(
-        middle_kernel,
-        "middle",
-        2,
-        [ahead, ahead, own, send_list, half, moved, inverse, got],
-        [atoms, atoms] + exchange_shape(devices, 3, ghost_n),
-    )
-    got = exchange(sent)
-    own, sent = pair_forces(
-        places, pairs, positions_end, kinds, ghost_kind, got, weights, devices
-    )
-    got = exchange(sent)
+    places = (behind, around)
+    (sent,) = pair_forces(places, pairs, moved, kinds, weights, got)
+    every = exchange(sent)
+    half_two, positions_end, own, sent = pair_forces(
+        places, pairs, moved, kinds, weights, got, (half, send_list, every)
+    )
+    back = exchange(sent)
     velocities_end, forces_end = small_call(
-        last_kernel, "last", 1, [ahead, own, send_list, half_two, inverse, got], [atoms, atoms]
+        last_kernel, "last", 1, [ahead, own, send_list, half_two, kinds, back], [atoms, atoms]
     )
     return (positions_end, velocities_end, forces_end)
 

time: 93.6 us -> 87.6 us (0.936)
  blocking collectives: 54.2 us -> 43 us
  Pallas kernels: 24.4 us -> 27.2 us
  other arithmetic: 0.03 us -> 1.56 us
  local copies, waits for them, and re-layouts: 3.7 us -> 4.87 us
    all_to_all x3 -> x2, blocking collectives: 54.2 us -> 43 us  [exchange(): return lax.all_to_all(blocks, ('gx', 'yz'), 0, 0, tiled=True)]
    pallas_call x2, Pallas kernels: 17.7 us -> 22.2 us  [pair_forces(): pl.pallas_call(functools.partial(force_kernel, second_call=bool(second)),...]
    pallas_call x3 -> x2, Pallas kernels: 4.11 us -> 2.15 us  [small_call(): pl.pallas_call(kernel, out_shape=out_shape, in_specs=[SMEM] * smem_n + [V...]
    all_to_all x0 -> x2, other arithmetic: none -> 1.52 us  [exchange(): return lax.all_to_all(blocks, ('gx', 'yz'), 0, 0, tiled=True)]
    unnamed x34 -> x40, local copies, waits for them, and re-layouts: 3.7 us -> 4.35 us
where the time goes in v1:
time: 87.6 us; the launch traced here: 87.5 us
  blocking collectives  43 us (49%)
  Pallas kernels  27.2 us (31%)
  starting transfers between devices  7.3 us (8%)
  local copies, waits for them, and re-layouts  4.87 us (6%)
  waiting for transfers between devices  1.95 us (2%)
  between operations  1.58 us (2%)
  other arithmetic  1.56 us (2%)
    all_to_all x2, blocking collectives, exchange(): return lax.all_to_all(blocks, ('gx', 'yz'), 0, 0, tiled=True)  43 us
    pallas_call x2, Pallas kernels, pair_forces(): pl.pallas_call(functools.partial(force_kernel, second_call=bool(second)),...  22.2 us
    all_to_all x1, starting transfers between devices, exchange(): return lax.all_to_all(blocks, ('gx', 'yz'), 0, 0, tiled=True)  7.3 us
    unnamed x40, local copies, waits for them, and re-layouts  4.35 us
    pallas_call x1, Pallas kernels, prepare(): pl.pallas_call(prepare_kernel, out_shape=[jax.ShapeDtypeStruct(*shape) fo...  2.84 us
    pallas_call x2, Pallas kernels, small_call(): pl.pallas_call(kernel, out_shape=out_shape, in_specs=[SMEM] * smem_n + [V...  2.15 us
    all_to_all x1, waiting for transfers between devices, exchange(): return lax.all_to_all(blocks, ('gx', 'yz'), 0, 0, tiled=True)  1.95 us
  transfers between devices with their start and end apart: 1, of which 1 were waited for; matrix products, arithmetic and copies ran while one was open for 0% of the time, Pallas kernels for 3%

profile of v1, /device:TPU:0, one launch (start us, length us, event | category | flops | bytes accessed | tf_op | source)
XLA Modules:
  0.0 87.5 jit_solution(12925728842874520619)
XLA Ops:
  0.6 0.0 copy-start.4
  0.6 0.0 copy-start.16
  0.7 0.0 copy-start.17
  0.7 0.0 copy-start.3
  0.7 0.0 copy-start
  0.7 0.6 copy-done.16
  1.3 0.0 copy-done.17
  1.3 0.0 copy-start.2
  1.3 0.0 copy-start.1
  1.4 0.0 copy-done.4
  1.4 0.0 copy-done.3
  1.4 0.0 copy-done
  1.4 0.6 copy-done.2
  2.0 0.0 copy-done.1
  2.0 0.8 start.1
  2.8 0.0 copy-start.7
  2.8 0.0 copy-start.8
  2.9 0.8 reshape.14
  3.7 0.0 copy-start.11
  3.7 0.0 copy-start.13
  3.7 0.0 copy-start.6
  3.7 7.3 %all-to-all-start = ((f32[32,1,192]{2,1,0:T(1,128)}), f32[32,1,192]{2,1,0:T(1,128)S(1)}, u32[]{:S(2)}, u32[]{:S(2)}) async-start(f32[32,1,192]{2,1,0:T(1,128)} %reshape.14), calls=%async_computation | async-start | bytes 65536 | tf_op jit(solution)/shard_map/all_to_all | solution.py:486
  11.0 0.0 copy-start.9
  11.7 0.0 copy-done.11
  11.7 0.0 copy-done.14
  11.7 0.0 copy-done.15
  11.8 0.0 copy-done.12
  11.8 0.0 copy-done.13
  11.8 0.0 copy-start.10
  11.8 0.0 copy-done.7
  11.8 0.0 copy-done.8
  11.8 0.0 copy-done.6
  11.9 0.0 copy-done.9
  11.9 0.6 copy-done.10
  12.5 1.1 %copy-done.5 = bf16[1,576,512]{2,1,0:T(8,128)(2,1)S(1)} copy-done((bf16[1,576,512]{2,1,0:T(8,128)(2,1)S(1)}, bf16[1,576,512]{2,1,0:T(8,128)(2,1)}, u32[]{:S(2)}) %copy-start.5) | copy-done | bytes 589848
  13.5 2.8 %prepare.1 = (s32[6,1024]{1,0:T(8,128)S(1)}, s32[6,1024]{1,0:T(8,128)S(1)}, s32[1]{0:T(128)}, bf16[512,16]{1,0:T(8,128)(2,1)S(1)}, bf16[512,16]{1,0:T(8,128)(2,1...) custom-call(s32[1]{0:T(128)S(6)} %copy.22.live_ref, ...), custom_call_target="tpu_custom_call" | custom-call | flops 2000000000 | bytes 4194304 | tf_op jit(solution)/shard_map/prepare/pallas_call | solution.py:226
  16.4 1.9 %all-to-all-done = f32[32,1,192]{2,1,0:T(1,128)S(1)} async-done(((f32[32,1,192]{2,1,0:T(1,128)}), f32[32,1,192]{2,1,0:T(1,128)S(1)}, u32[]{:S(2)}, u32[]{:S(2)}) %all-to-all-start) | async-done | bytes 24608 | tf_op jit(solution)/shard_map/all_to_all | solution.py:486
  18.3 0.5 broadcast.58
  18.8 0.7 reduce
  19.6 0.2 reshape.15.in_ref
  19.7 10.3 %pair_forces.2 = f32[32,3,144]{2,1,0:T(4,128)S(1)} custom-call(s32[9]{0:T(128)S(1)} %fusion.place_ref, s32[1]{0:T(128)} %get-tuple-element.23.total_ref, s32[72]{0:T(128)S(1)} %fusion.1.around_ref, s32[6,1024]{1,0:T(8,128)S(1)} %get-tuple-element.24.neigh_ref, s32[6,1024]{1,0:T(8,128)S(1)} %get-tuple-element.25.centre_ref, ...), custom_call_target="tpu_custom_call" | custom-call | flops 8493465600 | bytes 4194304 | tf_op jit(solution)/shard_map/pair_forces/pallas_call | solution.py:441
  30.0 0.2 reshape.16
  30.3 22.4 %all_to_all.15 = f32[32,1,432]{2,1,0:T(1,128)S(1)} all-to-all(f32[32,1,432]{2,1,0:T(1,128)S(1)} %reshape.16), channel_id=1, replica_groups=mesh['gx'=8,'yz'=4] {'gx','yz'}, dimensions={0} | all-to-all | bytes 110592 | tf_op jit(solution)/shard_map/all_to_all | solution.py:486
  52.7 0.8 reduce.1
  53.5 0.1 reshape.17.refs_2_
  53.6 12.0 %pair_forces.3 = (f32[3,48]{1,0:T(4,128)S(1)}, f32[3,48]{1,0:T(4,128)}, f32[3,48]{1,0:T(4,128)S(1)}, f32[32,3,12]{2,1,0:T(4,128)S(1)}) custom-call(s32[9]{0:T(128)S(1)} %fusion.place_ref, s32[1]{0:T(128)} %get-tuple-element.23.total_ref, s32[72]{0:T(128)S(1)} %fusion.1.around_ref, s32[6,1024]{1,0:T(8,128)S(1)} %get-tuple-element.24.neigh_ref, ...), custom_call_target="tpu_custom_call" | custom-call | flops 8493465600 | bytes 4194304 | tf_op jit(solution)/shard_map/pair_forces/pallas_call | solution.py:441
  65.6 20.6 %all_to_all.16.in_ref = f32[32,3,12]{2,1,0:T(4,128)S(1)} all-to-all(f32[32,3,12]{2,1,0:T(4,128)S(1)} %get-tuple-element.40), channel_id=1, replica_groups=mesh['gx'=8,'yz'=4] {'gx','yz'}, dimensions={0} | all-to-all | bytes 9216 | tf_op jit(solution)/shard_map/all_to_all | solution.py:486
  86.1 1.3 %last.1 = (f32[3,48]{1,0:T(4,128)}, f32[3,48]{1,0:T(4,128)}) custom-call(s32[8]{0:T(128)S(1)} %fusion.2.place_ref, f32[3,48]{1,0:T(4,128)S(1)} %get-tuple-element.38.own_ref, s32[8,12]{1,0:T(8,128)S(1)} %copy-done, f32[3,48]{1,0:T(4,128)S(1)} %get-tuple-element.39.half_two_ref, s32[1,48]{1,0:T(1,128)S(1)} %bitcast.9, f32[32,3,12]{2,1,0:T(4,128)S(1)} %all_to_all.16.in_ref), custom_call_target="tpu_custom_call" | custom-call | tf_op jit(solution)/shard_map/last/pallas_call | solution.py:468
  (8 shorter events, 0.1 us)
Async XLA Ops:
  0.6 0.7 copy-start.4
  0.6 0.7 copy-start.16
  0.7 0.7 copy-start.17
  0.7 0.7 copy-start.3
  0.7 0.7 copy-start
  1.3 0.7 copy-start.2
  1.3 0.7 copy-start.1
  2.8 9.0 %copy-start.7 = (s32[48,128]{1,0:T(8,128)S(1)}, s32[48,128]{1,0:T(8,128)}, u32[]{:S(2)}) copy-start(s32[48,128]{1,0:T(8,128)} %slots_ref.1) | copy-start | bytes 73732
  2.8 9.0 %copy-start.8 = (bf16[2,8,512]{2,1,0:T(8,128)(2,1)S(1)}, bf16[2,8,512]{2,1,0:T(8,128)(2,1)}, u32[]{:S(2)}) copy-start(bf16[2,8,512]{2,1,0:T(8,128)(2,1)} %embed_ref.1) | copy-start | bytes 49156
  3.7 8.0 %copy-start.11 = (bf16[512]{0:T(512)(128)(2,1)S(1)}, bf16[512]{0:T(512)(128)(2,1)}, u32[]{:S(2)}) copy-start(bf16[512]{0:T(512)(128)(2,1)} %param.31) | copy-start | bytes 3076
  3.7 8.0 %copy-start.14 = (s32[9]{0:T(128)S(1)}, s32[9]{0:T(128)}, u32[]{:S(2)}) copy-start(s32[9]{0:T(128)} %constant.82.clone) | copy-start | bytes 112
  3.7 8.0 %copy-start.15 = (s32[9]{0:T(128)S(1)}, s32[9]{0:T(128)}, u32[]{:S(2)}) copy-start(s32[9]{0:T(128)} %constant.81.clone) | copy-start | bytes 112
  3.7 8.1 %copy-start.12 = (s32[72]{0:T(128)S(1)}, s32[72]{0:T(128)}, u32[]{:S(2)}) copy-start(s32[72]{0:T(128)} %constant.84.clone) | copy-start | bytes 868
  3.7 8.1 %copy-start.13 = (s32[72]{0:T(128)S(1)}, s32[72]{0:T(128)}, u32[]{:S(2)}) copy-start(s32[72]{0:T(128)} %constant.83.clone) | copy-start | bytes 868
  3.7 8.1 %copy-start.6 = (bf16[1,512,64]{1,2,0:T(8,128)(2,1)S(1)}, bf16[1,512,64]{1,2,0:T(8,128)(2,1)}, u32[]{:S(2)}) copy-start(bf16[1,512,64]{1,2,0:T(8,128)(2,1)} %param.29) | copy-start | bytes 196612
  3.7 14.6 %all-to-all-start = ((f32[32,1,192]{2,1,0:T(1,128)}), f32[32,1,192]{2,1,0:T(1,128)S(1)}, u32[]{:S(2)}, u32[]{:S(2)}) async-start(f32[32,1,192]{2,1,0:T(1,128)} %reshape.14), calls=%async_computation | async-start | bytes 65536 | tf_op jit(solution)/shard_map/all_to_all | solution.py:486
  11.0 0.8 copy-start.9
  11.8 0.7 copy-start.10
  12.5 1.1 %copy-start.5 = (bf16[1,576,512]{2,1,0:T(8,128)(2,1)S(1)}, bf16[1,576,512]{2,1,0:T(8,128)(2,1)}, u32[]{:S(2)}) copy-start(bf16[1,576,512]{2,1,0:T(8,128)(2,1)} %param.30) | copy-start | bytes 1769476

commit v2 on v1

--- a/solution.py
+++ b/solution.py
@@ -78,10 +78,6 @@
     return jnp.concatenate([in_ref[place_ref[k]] for k in range(len(DIRECTIONS))], axis=1)
 
 
-def pick_ghosts(values, send_ref, atom_n):
-    return sum_parts(mm(split3(values), one_hot(by_direction(send_ref[...]), atom_n)))
-
-
 def inverse_mass(species):
     inverse = jnp.zeros(species.shape, F32)
     for spec_id, mass in enumerate(MASSES):
@@ -89,9 +85,7 @@
     return inverse
 
 
-def start_kernel(
-    place_ref, pos_ref, vel_ref, force_ref, species_ref, send_ref, moved_ref, half_ref, out_ref
-):
+def start_kernel(pos_ref, vel_ref, force_ref, species_ref, send_ref, moved_ref, half_ref, out_ref):
     species = species_ref[...]
     inverse = inverse_mass(species)
     half = vel_ref[...] + 0.5 * STEP * inverse * force_ref[...]
@@ -99,10 +93,9 @@
     half_ref[...] = half
     moved_ref[...] = moved
     spare = jnp.zeros((1, species.shape[1]), F32)
-    sources = jnp.concatenate([moved, species.astype(F32), half, spare], axis=0)
-    picked = pick_ghosts(sources, send_ref, species.shape[1])
-    sends = jnp.concatenate([send_ref[...].astype(F32)] * len(DIRECTIONS), axis=1)
-    put(out_ref, place_ref, jnp.concatenate([picked, sends], axis=0))
+    sends = send_ref[...].astype(F32)
+    sends = jnp.concatenate([sends, jnp.zeros((8, species.shape[1] - sends.shape[1]), F32)], axis=1)
+    out_ref[...] = jnp.concatenate([moved, species.astype(F32), half, spare, sends], axis=0)
 
 
 def total_force(own, back, sends):
@@ -143,8 +136,7 @@
     neigh_ref,
     centre_ref,
     total_ref,
-    embed_t_ref,
-    radial_t_ref,
+    into_ref,
     on_hidden_ref,
     on_inner_ref,
     on_bent_ref,
@@ -170,8 +162,8 @@
     on_weight_ref[...] = mm_nt(eye, jnp.concatenate([env_t_ref[...], readout16], axis=0)).astype(BF16)
     readout_t_ref[...] = mm_nt(eye, jnp.broadcast_to(readout.astype(F32), (128, latent)).astype(BF16))
     radial_back_ref[...] = radial16
-    radial_t_ref[...] = mm_nt(eye, radial16).astype(BF16)
-    embed_t_ref[...] = mm_nt(eye, jnp.concatenate([embed_ref[1], embed_ref[0]], axis=0) * half).astype(BF16)
+    into = jnp.concatenate([embed_ref[1] * half, embed_ref[0] * half, radial16], axis=0)
+    into_ref[...] = mm_nt(eye, into).astype(BF16)
 
 
 def list_pairs(live_ref, count_ref, slots_t, neigh_ref, centre_ref, total_ref):
@@ -214,8 +206,7 @@
         ((blocks, LANES), jnp.int32),
         ((blocks, LANES), jnp.int32),
         ((1,), jnp.int32),
-        ((latent, 16), BF16),
-        ((latent, BASIS_PAD), BF16),
+        ((latent, 2 * SPECIES + BASIS_PAD), BF16),
         ((latent + features + BASIS_PAD, latent), BF16),
         ((latent, features), BF16),
         ((latent + features, latent), BF16),
@@ -227,7 +218,7 @@
         prepare_kernel,
         out_shape=[jax.ShapeDtypeStruct(*shape) for shape in shapes],
         in_specs=[SMEM] + [VMEM] * 7,
-        out_specs=[VMEM, VMEM, SMEM] + [VMEM] * 8,
+        out_specs=[VMEM, VMEM, SMEM] + [VMEM] * 7,
         compiler_params=pltpu.CompilerParams(vmem_limit_bytes=24 * 2**20),
         cost_estimate=pl.CostEstimate(flops=2 * 10**9, bytes_accessed=4 * 2**20, transcendentals=0),
         name="prepare",
@@ -258,8 +249,7 @@
     centre_ref,
     moved_ref,
     own_kind_ref,
-    embed_ref,
-    radial_ref,
+    into_ref,
     on_hidden_ref,
     on_inner_ref,
     on_bent_ref,
@@ -269,24 +259,27 @@
     in_ref,
     *refs,
     second_call,
+    out_ghost_n,
 ):
     *refs, hot_s, use_s, u_s, slope_s, raw_s, part_s, ain_s, energy_s, c_s, dc_s, f_s = refs
     blocks, lanes = neigh_ref.shape
     atom_n = moved_ref.shape[1]
-    ghosts = take(in_ref, place_ref)
-    ghost_n = ghosts.shape[1] // len(DIRECTIONS)
-    ext_n = atom_n + ghosts.shape[1]
+    ghost_n = out_ghost_n
+    ext_n = atom_n + ghost_n * len(DIRECTIONS)
+    own_kind = own_kind_ref[...]
+    from_owners = [in_ref[place_ref[k]] for k in range(len(DIRECTIONS))]
+    sends = [owner[8:16, :ghost_n].astype(jnp.int32) for owner in from_owners]
+    picks = [one_hot(sends[k][k : k + 1], atom_n) for k in range(len(DIRECTIONS))]
+    ghosts = jnp.concatenate(
+        [sum_parts(mm(split3(owner[0:8]), pick)) for owner, pick in zip(from_owners, picks)], axis=1
+    )
     ghost_kind = ghosts[3:4].astype(jnp.int32)
-    own_kind = own_kind_ref[...]
     if second_call:
         half_ref, send_ref, all_ref, half_two_ref, end_ref, own_out_ref, out_ref = refs
         on_ghosts = []
         for k in range(len(DIRECTIONS)):
-            owner = place_ref[k]
-            sends = ghosts[8:16, k * ghost_n : (k + 1) * ghost_n].astype(jnp.int32)
-            whole = domain_force(all_ref, owner, around_ref, k * 8, sends, atom_n)
-            picked = mm(split3(padded_rows(whole, 8)), one_hot(sends[k : k + 1], atom_n))
-            on_ghosts.append(sum_parts(picked)[0:3])
+            whole = domain_force(all_ref, place_ref[k], around_ref, k * 8, sends[k], atom_n)
+            on_ghosts.append(sum_parts(mm(split3(padded_rows(whole, 8)), picks[k]))[0:3])
         _, ghost_pos = step_on(
             ghosts[0:3], ghosts[4:7], ghost_kind, jnp.concatenate(on_ghosts, axis=1)
         )
@@ -309,15 +302,18 @@
     pos_parts = split3(jnp.concatenate([pos8, -pos8[:, :atom_n]], axis=1))
     row8 = lax.broadcasted_iota(jnp.int32, (SPECIES, ext_n), 0)
     kinds = jnp.where(row8 == kind, 1.0, 0.0)
-    none = jnp.zeros((SPECIES, ext_n), F32)
-    neigh_embed = mm(embed_ref[...], jnp.concatenate([kinds, none], axis=0).astype(BF16))
-    own_embed = mm(
-        embed_ref[...],
-        jnp.concatenate([none, kinds], axis=0)[:, :atom_n].astype(BF16),
-    )
-    weight_in = jnp.concatenate(
-        [neigh_embed, own_embed, radial_ref[...].astype(F32)], axis=1
-    ).astype(BF16)
+    basis_in = identity(BASIS_PAD).astype(F32)
+    selected = jnp.concatenate(
+        [
+            jnp.concatenate([kinds, jnp.zeros((SPECIES + BASIS_PAD, ext_n), F32)], axis=0),
+            jnp.concatenate(
+                [jnp.zeros((SPECIES, atom_n), F32), kinds[:, :atom_n], jnp.zeros((BASIS_PAD, atom_n), F32)], axis=0
+            ),
+            jnp.concatenate([jnp.zeros((2 * SPECIES, BASIS_PAD), F32), basis_in], axis=0),
+        ],
+        axis=1,
+    )
+    weight_in = mm(into_ref[...], selected.astype(BF16)).astype(BF16)
 
     mid_row = lax.broadcasted_iota(jnp.int32, (BASIS_PAD, lanes), 0).astype(F32)
     mids = (mid_row + 0.5) / basis_n
@@ -345,9 +341,9 @@
         use = jnp.concatenate([hot_c * vec[k : k + 1].astype(BF16) for k in range(3)], axis=0)
         use_s[block] = use
         pre = mm(weight_in, jnp.concatenate([hot, basis.astype(BF16)], axis=0))
-        hidden, slope = silu_pair(pre.astype(BF16))
-        slope_s[block] = slope
-        taken = mm(on_hidden_ref[...], hidden)
+        hidden, slope = silu_pair(pre)
+        slope_s[block] = slope.astype(BF16)
+        taken = mm(on_hidden_ref[...], hidden.astype(BF16))
         part_s[block] = taken[:latent]
         raw = taken[latent : latent + features]
         raw_s[block] = raw
@@ -366,10 +362,10 @@
         weight = raw_s[block] * env
         inner = weight * mm(c_b, use)
         later = part_s[block] + mm(on_inner_ref[...], inner.astype(BF16))
-        gain, bent = silu_pair(later.astype(BF16))
+        gain, bent = silu_pair(later)
         readout = jnp.concatenate([readout_ref[...]] * (lanes // 128), axis=1)
-        energy_s[block] += jnp.sum(gain.astype(F32) * readout, axis=0, keepdims=True)
-        taken = mm(on_bent_ref[...], bent)
+        energy_s[block] += jnp.sum(gain * readout, axis=0, keepdims=True)
+        taken = mm(on_bent_ref[...], bent.astype(BF16))
         part_s[block] = taken[:latent]
         a_in = taken[latent:] * env
         ain_s[block] = a_in
@@ -395,7 +391,7 @@
         d_hidden = part_s[block] + mm(
             on_weight_ref[...], jnp.concatenate([d_weight.astype(BF16), ones], axis=0)
         )
-        d_pre = d_hidden.astype(BF16) * slope_s[block]
+        d_pre = (d_hidden * slope_s[block].astype(F32)).astype(BF16)
         d_basis = mm(radial_back_ref[...], d_pre)
         d_square = env * jnp.sum(d_basis * basis * apart, axis=0, keepdims=True) * (-2.0 * sharp)
         d_square = d_square - 2.0 * inside * d_env
@@ -419,27 +415,26 @@
         own_out_ref[...] = own
         put(out_ref, place_ref, -on_neigh[:, atom_n:])
     else:
-        every = jnp.concatenate([own, -on_neigh[:, atom_n:]], axis=1)
-        out_ref[...] = jnp.broadcast_to(every[None], out_ref.shape)
-
-
-def pair_forces(places, pairs, own_pos, own_kind, weights, incoming, second=()):
+        out_ref[...] = jnp.concatenate([own, -on_neigh[:, atom_n:]], axis=1)
+
+
+def pair_forces(places, pairs, own_pos, own_kind, weights, incoming, ghost_n, second=()):
     place, around = places
     neigh, centre, total = pairs
     blocks, lanes = neigh.shape
-    latent, features = weights[3].shape
+    latent, features = weights[2].shape
     atom_n = own_pos.shape[1]
-    devices, _, ghost_n = incoming.shape
+    devices = incoming.shape[0]
     ext_n = atom_n + ghost_n * len(DIRECTIONS)
     operands = [place, total, around, neigh, centre, own_pos, own_kind, *weights, incoming, *second]
     if second:
         out_shape = [jax.ShapeDtypeStruct((3, atom_n), F32)] * 3
         out_shape.append(jax.ShapeDtypeStruct((devices, 3, ghost_n), F32))
     else:
-        out_shape = [jax.ShapeDtypeStruct((devices, 3, ext_n), F32)]
+        out_shape = [jax.ShapeDtypeStruct((3, ext_n), F32)]
     pair_rows = blocks * lanes
     return pl.pallas_call(
-        functools.partial(force_kernel, second_call=bool(second)),
+        functools.partial(force_kernel, second_call=bool(second), out_ghost_n=ghost_n),
         out_shape=out_shape,
         in_specs=[SMEM] * 3 + [VMEM] * (len(operands) - 3),
         out_specs=[VMEM] * len(out_shape),
@@ -482,6 +477,10 @@
     return gx * yz_n + yz
 
 
+def gather_all(block):
+    return lax.all_gather(block, ("gx", "yz"))
+
+
 def exchange(blocks):
     return lax.all_to_all(blocks, ("gx", "yz"), 0, 0, tiled=True)
 
@@ -503,7 +502,6 @@
 ):
     atom_n = positions.shape[1]
     ghost_n = send_list.shape[1]
-    devices = lax.axis_size("gx") * lax.axis_size("yz")
     ahead = devices_at([a for a, _ in DIRECTIONS], [b for _, b in DIRECTIONS])
     sources = [(-a, -b) for a, b in DIRECTIONS] + [(0, 0)]
     behind = devices_at([a for a, _ in sources], [b for _, b in sources])
@@ -516,19 +514,19 @@
     moved, half, sent = small_call(
         start_kernel,
         "start",
-        1,
-        [ahead, positions, velocities, forces_start, kinds, send_list],
-        [atoms, atoms, jax.ShapeDtypeStruct((devices, 16, ghost_n), F32)],
-    )
-    got = exchange(sent)
+        0,
+        [positions, velocities, forces_start, kinds, send_list],
+        [atoms, atoms, jax.ShapeDtypeStruct((16, atom_n), F32)],
+    )
+    got = gather_all(sent)
     pairs, weights = prepare(
         live_atoms, neighbour_count, neighbours, radial_weight, species_embed, env_weight, latent_weight, readout
     )
     places = (behind, around)
-    (sent,) = pair_forces(places, pairs, moved, kinds, weights, got)
-    every = exchange(sent)
+    (sent,) = pair_forces(places, pairs, moved, kinds, weights, got, ghost_n)
+    every = gather_all(sent)
     half_two, positions_end, own, sent = pair_forces(
-        places, pairs, moved, kinds, weights, got, (half, send_list, every)
+        places, pairs, moved, kinds, weights, got, ghost_n, (half, send_list, every)
     )
     back = exchange(sent)
     velocities_end, forces_end = small_call(

time: 87.6 us -> 189 us (2.16)
  blocking collectives: 43 us -> 140 us
  waiting for transfers between devices: 1.95 us -> 7.45 us
  starting transfers between devices: 7.3 us -> 9.9 us
  local copies, waits for them, and re-layouts: 4.87 us -> 2.4 us
    all_gather x0 -> x2, blocking collectives: none -> 140 us  [gather_all(): return lax.all_gather(block, ('gx', 'yz'))]
    all_to_all x2 -> x0, blocking collectives: 43 us -> none  [exchange(): return lax.all_to_all(blocks, ('gx', 'yz'), 0, 0, tiled=True)]
    all_to_all x1, waiting for transfers between devices: 1.95 us -> 7.45 us  [exchange(): return lax.all_to_all(blocks, ('gx', 'yz'), 0, 0, tiled=True)]
    all_to_all x1, starting transfers between devices: 7.3 us -> 9.9 us  [exchange(): return lax.all_to_all(blocks, ('gx', 'yz'), 0, 0, tiled=True)]
    unnamed x40 -> x36, local copies, waits for them, and re-layouts: 4.35 us -> 2.4 us
  transfers between devices with their start and end apart: 1 -> 1, of which waited for: 1 -> 1; matrix products, arithmetic and copies ran while one was open for 0% -> 0% of each run, Pallas kernels for 3% -> 0%
where the time goes in v2:
time: 189 us; the launch traced here: 188 us
  blocking collectives  140 us (74%)
  Pallas kernels  27.6 us (15%)
  starting transfers between devices  9.9 us (5%)
  waiting for transfers between devices  7.45 us (4%)
  local copies, waits for them, and re-layouts  2.4 us (1%)
    all_gather x2, blocking collectives, gather_all(): return lax.all_gather(block, ('gx', 'yz'))  140 us
    pallas_call x2, Pallas kernels, pair_forces(): pl.pallas_call(functools.partial(force_kernel, second_call=bool(second),...  23.4 us
    all_to_all x1, starting transfers between devices, exchange(): return lax.all_to_all(blocks, ('gx', 'yz'), 0, 0, tiled=True)  9.9 us
    all_to_all x1, waiting for transfers between devices, exchange(): return lax.all_to_all(blocks, ('gx', 'yz'), 0, 0, tiled=True)  7.45 us
  transfers between devices with their start and end apart: 1, of which 1 were waited for; matrix products, arithmetic and copies ran while one was open for 0% of the time, Pallas kernels for 0%

profile of v2, /device:TPU:0, one launch (start us, length us, event | category | flops | bytes accessed | tf_op | source)
XLA Modules:
  0.0 188.5 jit_solution(8084162033921225858)
XLA Ops:
  0.6 0.0 copy-start.11
  0.6 0.0 copy-start.4
  0.7 0.0 copy-start
  1.3 0.0 copy-done.11
  1.3 0.0 copy-start.2
  1.4 0.0 copy-start.3
  1.4 0.0 copy-start.1
  1.4 0.0 copy-done.4
  1.4 0.0 copy-done
  1.4 0.6 copy-done.2
  2.0 0.0 copy-done.3
  2.0 0.0 copy-done.1
  2.1 0.0 copy-start.16
  2.1 0.0 copy-start.17
  2.1 0.0 copy-start.14
  2.1 0.0 copy-start.15
  2.1 0.0 copy-start.6
  2.1 0.0 copy-start.7
  2.1 0.0 copy-start.8
  2.1 72.0 %all-gather = f32[512,48]{1,0:T(8,128)S(1)} all-gather(f32[16,48]{1,0:T(8,128)S(1)} %get-tuple-element.33), channel_id=2, replica_groups=mesh['gx'=8,'yz'=4] {'gx','yz'}, dimensions={0}, use_global_device_ids=true | all-gather | bytes 101376 | tf_op jit(solution)/shard_map/all_gather | solution.py:481
  74.1 0.0 copy-done.16
  74.1 0.0 copy-done.17
  74.1 0.0 copy-start.9
  74.1 0.0 copy-done.14
  74.1 0.0 copy-done.15
  74.2 0.0 copy-start.10
  74.2 0.0 copy-done.6
  74.2 0.0 copy-done.7
  74.2 0.0 copy-done.8
  74.2 0.6 copy-done.9
  74.8 0.0 copy-done.10
  74.8 0.0 copy-start.5
  74.8 1.1 copy-done.5
  75.9 2.8 %prepare.1 = (s32[6,1024]{1,0:T(8,128)S(1)}, s32[6,1024]{1,0:T(8,128)S(1)}, s32[1]{0:T(128)}, bf16[512,32]{1,0:T(8,128)(2,1)S(1)}, bf16[592,512]{1,0:T(8,128)(2,...) custom-call(s32[1]{0:T(128)S(6)} %copy.22.live_ref, ...), custom_call_target="tpu_custom_call" | custom-call | flops 2000000000 | bytes 4194304 | tf_op jit(solution)/shard_map/prepare/pallas_call | solution.py:217
  78.7 10.9 %pair_forces.2 = f32[3,144]{1,0:T(4,128)S(1)} custom-call(s32[9]{0:T(128)S(1)} %fusion.place_ref, s32[1]{0:T(128)} %get-tuple-element.22.total_ref, s32[72]{0:T(128)S(1)} %fusion.1.around_ref, s32[6,1024]{1,0:T(8,128)S(1)} %get-tuple-element.23.neigh_ref, s32[6,1024]{1,0:T(8,128)S(1)} %get-tuple-element.24.centre_ref, ...), custom_call_target="tpu_custom_call" | custom-call | flops 8493465600 | bytes 4194304 | tf_op jit(solution)/shard_map/pair_forces/pallas_call | solution.py:436
  89.6 67.6 %all-gather.2.refs_2_ = f32[32,3,144]{2,1,0:T(4,128)S(1)} all-gather(f32[1,3,144]{2,1,0:T(4,128)S(1)} %bitcast.10), channel_id=3, replica_groups=mesh['gx'=8,'yz'=4] {'gx','yz'}, dimensions={0}, use_global_device_ids=true | all-gather | bytes 57024 | tf_op jit(solution)/shard_map/all_gather | solution.py:481
  157.3 12.5 %pair_forces.3 = (f32[3,48]{1,0:T(4,128)S(1)}, f32[3,48]{1,0:T(4,128)}, f32[3,48]{1,0:T(4,128)S(1)}, f32[32,3,12]{2,1,0:T(4,128)}) custom-call(s32[9]{0:T(128)S(1)} %fusion.place_ref, s32[1]{0:T(128)} %get-tuple-element.22.total_ref, s32[72]{0:T(128)S(1)} %fusion.1.around_ref, s32[6,1024]{1,0:T(8,128)S(1)} %get-tuple-element.23.neigh_ref, ...), custom_call_target="tpu_custom_call" | custom-call | flops 8493465600 | bytes 4194304 | tf_op jit(solution)/shard_map/pair_forces/pallas_call | solution.py:436
  169.8 0.0 copy-start.12
  169.8 0.0 copy-start.13
  169.8 9.9 %all-to-all-start = ((f32[32,3,12]{2,1,0:T(4,128)}), f32[32,3,12]{2,1,0:T(4,128)S(1)}, u32[]{:S(2)}, u32[]{:S(2)}) async-start(f32[32,3,12]{2,1,0:T(4,128)} %get-tuple-element.38), calls=%async_computation | async-start | bytes 131072 | tf_op jit(solution)/shard_map/all_to_all | solution.py:485
  179.7 0.0 copy-done.12
  179.7 0.0 copy-done.13
  179.7 7.5 %all-to-all-done.in_ref = f32[32,3,12]{2,1,0:T(4,128)S(1)} async-done(((f32[32,3,12]{2,1,0:T(4,128)}), f32[32,3,12]{2,1,0:T(4,128)S(1)}, u32[]{:S(2)}, u32[]{:S(2)}) %all-to-all-start) | async-done | bytes 4640 | tf_op jit(solution)/shard_map/all_to_all | solution.py:485
  187.2 1.3 last.1
  (5 shorter events, 0.1 us)
Async XLA Ops:
  0.6 0.7 copy-start.11
  0.6 0.7 copy-start.4
  0.7 0.7 copy-start
  1.3 0.7 copy-start.2
  1.4 0.7 copy-start.3
  1.4 0.7 copy-start.1
  2.1 72.1 %copy-start.16 = (s32[9]{0:T(128)S(1)}, s32[9]{0:T(128)}, u32[]{:S(2)}) copy-start(s32[9]{0:T(128)} %constant.82.clone) | copy-start | bytes 112
  2.1 72.0 %copy-start.17 = (s32[9]{0:T(128)S(1)}, s32[9]{0:T(128)}, u32[]{:S(2)}) copy-start(s32[9]{0:T(128)} %constant.81.clone) | copy-start | bytes 112
  2.1 72.1 %copy-start.14 = (s32[72]{0:T(128)S(1)}, s32[72]{0:T(128)}, u32[]{:S(2)}) copy-start(s32[72]{0:T(128)} %constant.84.clone) | copy-start | bytes 868
  2.1 72.0 %copy-start.15 = (s32[72]{0:T(128)S(1)}, s32[72]{0:T(128)}, u32[]{:S(2)}) copy-start(s32[72]{0:T(128)} %constant.83.clone) | copy-start | bytes 868
  2.1 72.1 %copy-start.6 = (bf16[1,512,64]{1,2,0:T(8,128)(2,1)S(1)}, bf16[1,512,64]{1,2,0:T(8,128)(2,1)}, u32[]{:S(2)}) copy-start(bf16[1,512,64]{1,2,0:T(8,128)(2,1)} %param.29) | copy-start | bytes 196612
  2.1 72.1 %copy-start.7 = (s32[48,128]{1,0:T(8,128)S(1)}, s32[48,128]{1,0:T(8,128)}, u32[]{:S(2)}) copy-start(s32[48,128]{1,0:T(8,128)} %slots_ref.1) | copy-start | bytes 73732
  2.1 72.1 %copy-start.8 = (bf16[2,8,512]{2,1,0:T(8,128)(2,1)S(1)}, bf16[2,8,512]{2,1,0:T(8,128)(2,1)}, u32[]{:S(2)}) copy-start(bf16[2,8,512]{2,1,0:T(8,128)(2,1)} %embed_ref.1) | copy-start | bytes 49156
  74.1 0.7 copy-start.9
  74.2 0.7 copy-start.10
  74.8 1.1 copy-start.5
  169.8 9.9 %copy-start.12 = (s32[8]{0:T(128)S(1)}, s32[8]{0:T(128)}, u32[]{:S(2)}) copy-start(s32[8]{0:T(128)} %constant.80.clone) | copy-start | bytes 100
  169.8 9.9 %copy-start.13 = (s32[8]{0:T(128)S(1)}, s32[8]{0:T(128)}, u32[]{:S(2)}) copy-start(s32[8]{0:T(128)} %constant.79.clone) | copy-start | bytes 100
  169.8 17.4 %all-to-all-start = ((f32[32,3,12]{2,1,0:T(4,128)}), f32[32,3,12]{2,1,0:T(4,128)S(1)}, u32[]{:S(2)}, u32[]{:S(2)}) async-start(f32[32,3,12]{2,1,0:T(4,128)} %get-tuple-element.38), calls=%async_computation | async-start | bytes 131072 | tf_op jit(solution)/shard_map/all_to_all | solution.py:485

commit v3 on v2

--- a/solution.py
+++ b/solution.py
@@ -16,6 +16,7 @@
 
 LANES = 1024
 DIRECTIONS = ((-1, -1), (-1, 0), (-1, 1), (0, -1), (0, 1), (1, -1), (1, 0), (1, 1))
+TILE = (8, 128)
 BASIS_PAD = 16
 
 F32 = jnp.float32
@@ -85,17 +86,45 @@
     return inverse
 
 
-def start_kernel(pos_ref, vel_ref, force_ref, species_ref, send_ref, moved_ref, half_ref, out_ref):
+def fetch(pairs, sems):
+    copies = [pltpu.make_async_copy(src, dst, sems.at[n]) for n, (src, dst) in enumerate(pairs)]
+    for copy in copies:
+        copy.start()
+    return copies
+
+
+def start_kernel(
+    place_ref, pos_hbm, vel_hbm, force_hbm, species_hbm, send_hbm, moved_ref, half_ref, out_ref, *scratch
+):
+    pos_ref, vel_ref, force_ref, species_ref, send_ref, sems = scratch
+    copies = fetch(
+        [
+            (pos_hbm, pos_ref),
+            (vel_hbm, vel_ref),
+            (force_hbm, force_ref),
+            (species_hbm, species_ref),
+            (send_hbm, send_ref),
+        ],
+        sems,
+    )
+    out_ref[...] = jnp.zeros_like(out_ref)
+    for copy in copies:
+        copy.wait()
     species = species_ref[...]
-    inverse = inverse_mass(species)
-    half = vel_ref[...] + 0.5 * STEP * inverse * force_ref[...]
+    half = vel_ref[...] + 0.5 * STEP * inverse_mass(species) * force_ref[...]
     moved = pos_ref[...] + STEP * half
     half_ref[...] = half
     moved_ref[...] = moved
     spare = jnp.zeros((1, species.shape[1]), F32)
-    sends = send_ref[...].astype(F32)
-    sends = jnp.concatenate([sends, jnp.zeros((8, species.shape[1] - sends.shape[1]), F32)], axis=1)
-    out_ref[...] = jnp.concatenate([moved, species.astype(F32), half, spare, sends], axis=0)
+    sources = split3(jnp.concatenate([moved, species.astype(F32), half, spare], axis=0))
+    sends = send_ref[...]
+    picked = sum_parts(mm(sources, one_hot(by_direction(sends), species.shape[1])))
+    sent = sends.astype(F32)
+    ghost_n = sent.shape[1]
+    rest = jnp.zeros((TILE[0], TILE[1] - 2 * ghost_n), F32)
+    for k in range(len(DIRECTIONS)):
+        block = picked[:, k * ghost_n : (k + 1) * ghost_n]
+        out_ref[place_ref[k]] = jnp.concatenate([block, sent, rest], axis=1)
 
 
 def total_force(own, back, sends):
@@ -107,9 +136,9 @@
     ghost_n = sends.shape[1]
     back = []
     for k in range(len(DIRECTIONS)):
-        start = atom_n + k * ghost_n
-        back.append(all_ref[around_ref[first + k]][:, start : start + ghost_n])
-    return total_force(all_ref[owner][:, :atom_n], jnp.concatenate(back, axis=1), sends)
+        start = k * ghost_n
+        back.append(all_ref[around_ref[first + k]][0:3, start : start + ghost_n])
+    return total_force(all_ref[owner][3:6, :atom_n], jnp.concatenate(back, axis=1), sends)
 
 
 def step_on(moved, half, kinds, forces):
@@ -126,13 +155,13 @@
 
 def prepare_kernel(
     live_ref,
-    count_ref,
-    slots_ref,
     radial_ref,
     embed_ref,
-    env_t_ref,
-    latent_ref,
     readout_ref,
+    count_hbm,
+    slots_hbm,
+    env_t_hbm,
+    latent_hbm,
     neigh_ref,
     centre_ref,
     total_ref,
@@ -143,10 +172,28 @@
     on_weight_ref,
     readout_t_ref,
     radial_back_ref,
+    count_ref,
+    slots_ref,
+    env_t_ref,
+    latent_ref,
+    sems,
 ):
+    copies = fetch(
+        [
+            (count_hbm, count_ref),
+            (slots_hbm, slots_ref),
+            (env_t_hbm, env_t_ref),
+            (latent_hbm, latent_ref),
+        ],
+        sems,
+    )
     features, latent = env_t_ref.shape
+    for copy in copies[:2]:
+        copy.wait()
     slots_t = mm_nt(identity(slots_ref.shape[1]), slots_ref[...].astype(F32).astype(BF16)).astype(BF16)
     list_pairs(live_ref, count_ref, slots_t, neigh_ref, centre_ref, total_ref)
+    for copy in copies[2:]:
+        copy.wait()
 
     eye = identity(latent)
     half = BF16(0.5)
@@ -214,24 +261,18 @@
         ((latent, 128), F32),
         ((BASIS_PAD, latent), BF16),
     )
+    small = [radial_weight, species_embed, readout[None, :]]
+    large = [neighbour_count.reshape(1, atom_n), neighbours, env_weight[0].T, latent_weight[0]]
     out = pl.pallas_call(
         prepare_kernel,
         out_shape=[jax.ShapeDtypeStruct(*shape) for shape in shapes],
-        in_specs=[SMEM] + [VMEM] * 7,
+        in_specs=[SMEM] + [VMEM] * len(small) + [pl.BlockSpec(memory_space=pl.ANY)] * len(large),
         out_specs=[VMEM, VMEM, SMEM] + [VMEM] * 7,
-        compiler_params=pltpu.CompilerParams(vmem_limit_bytes=24 * 2**20),
+        scratch_shapes=fetch_scratch(large),
+        compiler_params=pltpu.CompilerParams(vmem_limit_bytes=48 * 2**20),
         cost_estimate=pl.CostEstimate(flops=2 * 10**9, bytes_accessed=4 * 2**20, transcendentals=0),
         name="prepare",
-    )(
-        live_atoms,
-        neighbour_count.reshape(1, atom_n),
-        neighbours,
-        radial_weight,
-        species_embed,
-        env_weight[0].T,
-        latent_weight[0],
-        readout[None, :],
-    )
+    )(live_atoms, *small, *large)
     return out[:3], out[3:]
 
 
@@ -268,18 +309,16 @@
     ext_n = atom_n + ghost_n * len(DIRECTIONS)
     own_kind = own_kind_ref[...]
     from_owners = [in_ref[place_ref[k]] for k in range(len(DIRECTIONS))]
-    sends = [owner[8:16, :ghost_n].astype(jnp.int32) for owner in from_owners]
-    picks = [one_hot(sends[k][k : k + 1], atom_n) for k in range(len(DIRECTIONS))]
-    ghosts = jnp.concatenate(
-        [sum_parts(mm(split3(owner[0:8]), pick)) for owner, pick in zip(from_owners, picks)], axis=1
-    )
+    ghosts = jnp.concatenate([owner[:, :ghost_n] for owner in from_owners], axis=1)
     ghost_kind = ghosts[3:4].astype(jnp.int32)
     if second_call:
         half_ref, send_ref, all_ref, half_two_ref, end_ref, own_out_ref, out_ref = refs
         on_ghosts = []
         for k in range(len(DIRECTIONS)):
-            whole = domain_force(all_ref, place_ref[k], around_ref, k * 8, sends[k], atom_n)
-            on_ghosts.append(sum_parts(mm(split3(padded_rows(whole, 8)), picks[k]))[0:3])
+            sends = from_owners[k][:, ghost_n : 2 * ghost_n].astype(jnp.int32)
+            whole = domain_force(all_ref, place_ref[k], around_ref, k * 8, sends, atom_n)
+            picked = mm(split3(padded_rows(whole, 8)), one_hot(sends[k : k + 1], atom_n))
+            on_ghosts.append(sum_parts(picked)[0:3])
         _, ghost_pos = step_on(
             ghosts[0:3], ghosts[4:7], ghost_kind, jnp.concatenate(on_ghosts, axis=1)
         )
@@ -415,7 +454,11 @@
         own_out_ref[...] = own
         put(out_ref, place_ref, -on_neigh[:, atom_n:])
     else:
-        out_ref[...] = jnp.concatenate([own, -on_neigh[:, atom_n:]], axis=1)
+        ghost_all = ext_n - atom_n
+        upper = jnp.concatenate([-on_neigh[:, atom_n:], jnp.zeros((3, TILE[1] - ghost_all), F32)], axis=1)
+        lower = jnp.concatenate([own, jnp.zeros((3, TILE[1] - atom_n), F32)], axis=1)
+        tile = jnp.concatenate([upper, lower, jnp.zeros((TILE[0] - 6, TILE[1]), F32)], axis=0)
+        out_ref[...] = jnp.broadcast_to(tile[None], out_ref.shape)
 
 
 def pair_forces(places, pairs, own_pos, own_kind, weights, incoming, ghost_n, second=()):
@@ -431,7 +474,7 @@
         out_shape = [jax.ShapeDtypeStruct((3, atom_n), F32)] * 3
         out_shape.append(jax.ShapeDtypeStruct((devices, 3, ghost_n), F32))
     else:
-        out_shape = [jax.ShapeDtypeStruct((3, ext_n), F32)]
+        out_shape = [jax.ShapeDtypeStruct((devices, *TILE), F32)]
     pair_rows = blocks * lanes
     return pl.pallas_call(
         functools.partial(force_kernel, second_call=bool(second), out_ghost_n=ghost_n),
@@ -459,13 +502,22 @@
     )(*operands)
 
 
-def small_call(kernel, name, smem_n, operands, out_shape):
+def fetch_scratch(operands):
+    return [pltpu.VMEM(operand.shape, operand.dtype) for operand in operands] + [
+        pltpu.SemaphoreType.DMA((len(operands),))
+    ]
+
+
+def small_call(kernel, name, smem_n, operands, out_shape, fetched=False):
+    others = operands[smem_n:]
+    place = pl.BlockSpec(memory_space=pl.ANY) if fetched else VMEM
     return pl.pallas_call(
         kernel,
         out_shape=out_shape,
-        in_specs=[SMEM] * smem_n + [VMEM] * (len(operands) - smem_n),
+        in_specs=[SMEM] * smem_n + [place] * len(others),
         out_specs=[VMEM] * len(out_shape),
-        compiler_params=pltpu.CompilerParams(vmem_limit_bytes=16 * 2**20),
+        scratch_shapes=fetch_scratch(others) if fetched else [],
+        compiler_params=pltpu.CompilerParams(vmem_limit_bytes=48 * 2**20),
         name=name,
     )(*operands)
 
@@ -475,10 +527,6 @@
     gx = (lax.axis_index("gx") + jnp.asarray(shift_gx, jnp.int32) + gx_n) % gx_n
     yz = (lax.axis_index("yz") + jnp.asarray(shift_yz, jnp.int32) + yz_n) % yz_n
     return gx * yz_n + yz
-
-
-def gather_all(block):
-    return lax.all_gather(block, ("gx", "yz"))
 
 
 def exchange(blocks):
@@ -502,6 +550,7 @@
 ):
     atom_n = positions.shape[1]
     ghost_n = send_list.shape[1]
+    devices = lax.axis_size("gx") * lax.axis_size("yz")
     ahead = devices_at([a for a, _ in DIRECTIONS], [b for _, b in DIRECTIONS])
     sources = [(-a, -b) for a, b in DIRECTIONS] + [(0, 0)]
     behind = devices_at([a for a, _ in sources], [b for _, b in sources])
@@ -514,17 +563,18 @@
     moved, half, sent = small_call(
         start_kernel,
         "start",
-        0,
-        [positions, velocities, forces_start, kinds, send_list],
-        [atoms, atoms, jax.ShapeDtypeStruct((16, atom_n), F32)],
-    )
-    got = gather_all(sent)
+        1,
+        [ahead, positions, velocities, forces_start, kinds, send_list],
+        [atoms, atoms, jax.ShapeDtypeStruct((devices, *TILE), F32)],
+        fetched=True,
+    )
+    got = exchange(sent)
     pairs, weights = prepare(
         live_atoms, neighbour_count, neighbours, radial_weight, species_embed, env_weight, latent_weight, readout
     )
     places = (behind, around)
     (sent,) = pair_forces(places, pairs, moved, kinds, weights, got, ghost_n)
-    every = gather_all(sent)
+    every = exchange(sent)
     half_two, positions_end, own, sent = pair_forces(
         places, pairs, moved, kinds, weights, got, ghost_n, (half, send_list, every)
     )

time: 189 us -> 86.5 us (0.46)
  blocking collectives: 140 us -> 19.4 us
  Pallas kernels: 27.6 us -> 53.3 us
  waiting for transfers between devices: 7.45 us -> 2.88 us
  starting transfers between devices: 9.9 us -> 7.3 us
    all_gather x2 -> x0, blocking collectives: 140 us -> none  [gather_all(): return lax.all_gather(block, ('gx', 'yz'))]
    pallas_call x2, Pallas kernels: 23.4 us -> 47.4 us  [pair_forces(): pl.pallas_call(functools.partial(force_kernel, second_call=bool(second),...]
    all_to_all x0 -> x2, blocking collectives: none -> 19.4 us  [exchange(): return lax.all_to_all(blocks, ('gx', 'yz'), 0, 0, tiled=True)]
    all_to_all x1, waiting for transfers between devices: 7.45 us -> 2.88 us  [exchange(): return lax.all_to_all(blocks, ('gx', 'yz'), 0, 0, tiled=True)]
    all_to_all x1, starting transfers between devices: 9.9 us -> 7.3 us  [exchange(): return lax.all_to_all(blocks, ('gx', 'yz'), 0, 0, tiled=True)]
  transfers between devices with their start and end apart: 1 -> 1, of which waited for: 1 -> 1; matrix products, arithmetic and copies ran while one was open for 0% -> 0% of each run, Pallas kernels for 0% -> 3%
where the time goes in v3:
time: 86.5 us; the launch traced here: 87.5 us
  Pallas kernels  53.3 us (62%)
  blocking collectives  19.4 us (22%)
  starting transfers between devices  7.3 us (8%)
  local copies, waits for them, and re-layouts  3.02 us (3%)
  waiting for transfers between devices  2.88 us (3%)
  between operations  1.55 us (2%)
    pallas_call x2, Pallas kernels, pair_forces(): pl.pallas_call(functools.partial(force_kernel, second_call=bool(second),...  47.4 us
    all_to_all x2, blocking collectives, exchange(): return lax.all_to_all(blocks, ('gx', 'yz'), 0, 0, tiled=True)  19.4 us
    all_to_all x1, starting transfers between devices, exchange(): return lax.all_to_all(blocks, ('gx', 'yz'), 0, 0, tiled=True)  7.3 us
    unnamed x36, local copies, waits for them, and re-layouts  3.02 us
    pallas_call x1, Pallas kernels, prepare(): pl.pallas_call(prepare_kernel, out_shape=[jax.ShapeDtypeStruct(*shape) fo...  3.01 us
    all_to_all x1, waiting for transfers between devices, exchange(): return lax.all_to_all(blocks, ('gx', 'yz'), 0, 0, tiled=True)  2.88 us
    pallas_call x2, Pallas kernels, small_call(): pl.pallas_call(kernel, out_shape=out_shape, in_specs=[SMEM] * smem_n + [p...  2.87 us
  transfers between devices with their start and end apart: 1, of which 1 were waited for; matrix products, arithmetic and copies ran while one was open for 0% of the time, Pallas kernels for 3%

profile of v3, /device:TPU:0, one launch (start us, length us, event | category | flops | bytes accessed | tf_op | source)
XLA Modules:
  0.0 87.5 jit_solution(12222055591575274915)
XLA Ops:
  0.6 0.0 copy-start.4
  0.6 0.0 copy-start.16
  0.7 0.0 copy-start.17
  0.7 0.0 copy-start.3
  0.7 0.0 copy-start
  0.7 0.6 copy-done.16
  1.3 0.0 copy-done.17
  1.3 0.0 copy-start.2
  1.3 0.0 copy-start.1
  1.4 0.0 copy-done.4
  1.4 0.0 copy-done.3
  1.4 0.0 copy-done
  1.4 0.6 copy-done.2
  2.0 0.0 copy-done.1
  2.0 1.5 %start.1 = (f32[3,48]{1,0:T(4,128)S(1)}, f32[3,48]{1,0:T(4,128)S(1)}, f32[32,8,128]{2,1,0:T(8,128)}) custom-call(s32[8]{0:T(128)S(1)} %fusion.2.place_ref, f32[3,48]{1,0:T(4,128)S(1)} %copy-done.2, f32[3,48]{1,0:T(4,128)S(1)} %copy-done.3, f32[3,48]{1,0:T(4,128)S(1)} %copy-done.4, s32[1,48]{1,0:T(1,128)S(1)} %bitcast.6, s32[8,12]{1,0:T(8,128)S(1)} %copy-done), custom_call_target="tpu_custom_call" | custom-call | tf_op jit(solution)/shard_map/start/pallas_call | solution.py:514
  3.6 0.0 copy-start.11
  3.6 0.0 copy-start.14
  3.6 0.0 copy-start.15
  3.6 0.0 copy-start.6
  3.6 0.0 copy-start.7
  3.6 0.0 copy-start.8
  3.6 7.3 %all-to-all-start = ((f32[32,8,128]{2,1,0:T(8,128)}), f32[32,8,128]{2,1,0:T(8,128)S(1)}, u32[]{:S(2)}, u32[]{:S(2)}) async-start(f32[32,8,128]{2,1,0:T(8,128)} %get-tuple-element.33), calls=%async_computation | async-start | bytes 262144 | tf_op jit(solution)/shard_map/all_to_all | solution.py:533
  10.9 0.0 copy-start.9
  11.6 0.0 copy-done.11
  11.6 0.0 copy-done.14
  11.6 0.0 copy-done.15
  11.7 0.0 copy-start.10
  11.7 0.0 copy-done.6
  11.7 0.0 copy-done.7
  11.7 0.0 copy-done.8
  11.7 0.0 copy-done.9
  11.7 0.6 copy-done.10
  12.3 0.0 copy-start.5
  12.3 1.1 %copy-done.5 = bf16[1,576,512]{2,1,0:T(8,128)(2,1)S(1)} copy-done((bf16[1,576,512]{2,1,0:T(8,128)(2,1)S(1)}, bf16[1,576,512]{2,1,0:T(8,128)(2,1)}, u32[]{:S(2)}) %copy-start.5) | copy-done | bytes 589848
  13.4 0.0 copy-start.12
  13.4 0.0 copy-start.13
  13.4 3.0 %prepare.1 = (s32[6,1024]{1,0:T(8,128)S(1)}, s32[6,1024]{1,0:T(8,128)S(1)}, s32[1]{0:T(128)}, bf16[512,32]{1,0:T(8,128)(2,1)S(1)}, bf16[592,512]{1,0:T(8,128)(2,...) custom-call(s32[1]{0:T(128)S(6)} %copy.22.live_ref, ...), custom_call_target="tpu_custom_call" | custom-call | flops 2000000000 | bytes 4194304 | tf_op jit(solution)/shard_map/prepare/pallas_call | solution.py:266
  16.4 0.0 copy-done.12
  16.4 0.0 copy-done.13
  16.5 2.9 %all-to-all-done.in_ref = f32[32,8,128]{2,1,0:T(8,128)S(1)} async-done(((f32[32,8,128]{2,1,0:T(8,128)}), f32[32,8,128]{2,1,0:T(8,128)S(1)}, u32[]{:S(2)}, u32[]{:S(2)}) %all-to-all-start) | async-done | bytes 131104 | tf_op jit(solution)/shard_map/all_to_all | solution.py:533
  19.3 22.9 %pair_forces.2 = f32[32,8,128]{2,1,0:T(8,128)S(1)} custom-call(s32[9]{0:T(128)S(1)} %fusion.place_ref, s32[1]{0:T(128)} %get-tuple-element.22.total_ref, s32[72]{0:T(128)S(1)} %fusion.1.around_ref, s32[6,1024]{1,0:T(8,128)S(1)} %get-tuple-element.23.neigh_ref, s32[6,1024]{1,0:T(8,128)S(1)} %get-tuple-element.24.centre_ref, ...), custom_call_target="tpu_custom_call" | custom-call | flops 8493465600 | bytes 4194304 | tf_op jit(solution)/shard_map/pair_forces/pallas_call | solution.py:479
  42.2 10.2 %all_to_all.15.refs_2_ = f32[32,8,128]{2,1,0:T(8,128)S(1)} all-to-all(f32[32,8,128]{2,1,0:T(8,128)S(1)} %pair_forces.2), channel_id=1, replica_groups=mesh['gx'=8,'yz'=4] {'gx','yz'}, dimensions={0} | all-to-all | bytes 262144 | tf_op jit(solution)/shard_map/all_to_all | solution.py:533
  52.5 24.5 %pair_forces.3 = (f32[3,48]{1,0:T(4,128)S(1)}, f32[3,48]{1,0:T(4,128)}, f32[3,48]{1,0:T(4,128)S(1)}, f32[32,3,12]{2,1,0:T(4,128)S(1)}) custom-call(s32[9]{0:T(128)S(1)} %fusion.place_ref, s32[1]{0:T(128)} %get-tuple-element.22.total_ref, s32[72]{0:T(128)S(1)} %fusion.1.around_ref, s32[6,1024]{1,0:T(8,128)S(1)} %get-tuple-element.23.neigh_ref, ...), custom_call_target="tpu_custom_call" | custom-call | flops 8493465600 | bytes 4194304 | tf_op jit(solution)/shard_map/pair_forces/pallas_call | solution.py:479
  77.0 9.2 %all_to_all.16.in_ref = f32[32,3,12]{2,1,0:T(4,128)S(1)} all-to-all(f32[32,3,12]{2,1,0:T(4,128)S(1)} %get-tuple-element.38), channel_id=1, replica_groups=mesh['gx'=8,'yz'=4] {'gx','yz'}, dimensions={0} | all-to-all | bytes 9216 | tf_op jit(solution)/shard_map/all_to_all | solution.py:533
  86.2 1.3 %last.1 = (f32[3,48]{1,0:T(4,128)}, f32[3,48]{1,0:T(4,128)}) custom-call(s32[8]{0:T(128)S(1)} %fusion.2.place_ref, f32[3,48]{1,0:T(4,128)S(1)} %get-tuple-element.36.own_ref, s32[8,12]{1,0:T(8,128)S(1)} %copy-done, f32[3,48]{1,0:T(4,128)S(1)} %get-tuple-element.37.half_two_ref, s32[1,48]{1,0:T(1,128)S(1)} %bitcast.9, f32[32,3,12]{2,1,0:T(4,128)S(1)} %all_to_all.16.in_ref), custom_call_target="tpu_custom_call" | custom-call | tf_op jit(solution)/shard_map/last/pallas_call | solution.py:514
  (4 shorter events, 0.0 us)
Async XLA Ops:
  0.6 0.7 copy-start.4
  0.6 0.7 copy-start.16
  0.7 0.7 copy-start.17
  0.7 0.7 copy-start.3
  0.7 0.7 copy-start
  1.3 0.7 copy-start.2
  1.3 0.7 copy-start.1
  3.6 8.1 %copy-start.11 = (bf16[512]{0:T(512)(128)(2,1)S(1)}, bf16[512]{0:T(512)(128)(2,1)}, u32[]{:S(2)}) copy-start(bf16[512]{0:T(512)(128)(2,1)} %param.31) | copy-start | bytes 3076
  3.6 8.1 %copy-start.14 = (s32[9]{0:T(128)S(1)}, s32[9]{0:T(128)}, u32[]{:S(2)}) copy-start(s32[9]{0:T(128)} %constant.82.clone) | copy-start | bytes 112
  3.6 8.1 %copy-start.15 = (s32[9]{0:T(128)S(1)}, s32[9]{0:T(128)}, u32[]{:S(2)}) copy-start(s32[9]{0:T(128)} %constant.81.clone) | copy-start | bytes 112
  3.6 8.1 %copy-start.6 = (bf16[1,512,64]{1,2,0:T(8,128)(2,1)S(1)}, bf16[1,512,64]{1,2,0:T(8,128)(2,1)}, u32[]{:S(2)}) copy-start(bf16[1,512,64]{1,2,0:T(8,128)(2,1)} %param.29) | copy-start | bytes 196612
  3.6 8.1 %copy-start.7 = (s32[48,128]{1,0:T(8,128)S(1)}, s32[48,128]{1,0:T(8,128)}, u32[]{:S(2)}) copy-start(s32[48,128]{1,0:T(8,128)} %slots_hbm.1) | copy-start | bytes 73732
  3.6 8.1 %copy-start.8 = (bf16[2,8,512]{2,1,0:T(8,128)(2,1)S(1)}, bf16[2,8,512]{2,1,0:T(8,128)(2,1)}, u32[]{:S(2)}) copy-start(bf16[2,8,512]{2,1,0:T(8,128)(2,1)} %embed_ref.1) | copy-start | bytes 49156
  3.6 15.7 %all-to-all-start = ((f32[32,8,128]{2,1,0:T(8,128)}), f32[32,8,128]{2,1,0:T(8,128)S(1)}, u32[]{:S(2)}, u32[]{:S(2)}) async-start(f32[32,8,128]{2,1,0:T(8,128)} %get-tuple-element.33), calls=%async_computation | async-start | bytes 262144 | tf_op jit(solution)/shard_map/all_to_all | solution.py:533
  10.9 0.8 copy-start.9
  11.7 0.7 copy-start.10
  12.3 1.1 %copy-start.5 = (bf16[1,576,512]{2,1,0:T(8,128)(2,1)S(1)}, bf16[1,576,512]{2,1,0:T(8,128)(2,1)}, u32[]{:S(2)}) copy-start(bf16[1,576,512]{2,1,0:T(8,128)(2,1)} %param.30) | copy-start | bytes 1769476
  13.4 3.0 %copy-start.12 = (s32[72]{0:T(128)S(1)}, s32[72]{0:T(128)}, u32[]{:S(2)}) copy-start(s32[72]{0:T(128)} %constant.84.clone) | copy-start | bytes 868
  13.4 3.0 %copy-start.13 = (s32[72]{0:T(128)S(1)}, s32[72]{0:T(128)}, u32[]{:S(2)}) copy-start(s32[72]{0:T(128)} %constant.83.clone) | copy-start | bytes 868

commit v4 on v2

--- a/solution.py
+++ b/solution.py
@@ -16,6 +16,7 @@
 
 LANES = 1024
 DIRECTIONS = ((-1, -1), (-1, 0), (-1, 1), (0, -1), (0, 1), (1, -1), (1, 0), (1, 1))
+TILE = (4, 128)
 BASIS_PAD = 16
 
 F32 = jnp.float32
@@ -67,15 +68,27 @@
     return jnp.concatenate([rows[k : k + 1] for k in range(len(DIRECTIONS))], axis=1)
 
 
-def put(out_ref, place_ref, blocks):
+def device_at(shift_gx, shift_yz):
+    gx_n, yz_n = lax.axis_size("gx"), lax.axis_size("yz")
+    gx = lax.rem(lax.axis_index("gx") + (shift_gx % gx_n), gx_n)
+    yz = lax.rem(lax.axis_index("yz") + (shift_yz % yz_n), yz_n)
+    return gx * yz_n + yz
+
+
+def towards(sign):
+    return [device_at(sign * a, sign * b) for a, b in DIRECTIONS]
+
+
+def put(out_ref, blocks):
+    places = towards(-1)
     ghost_n = blocks.shape[1] // len(DIRECTIONS)
     out_ref[...] = jnp.zeros_like(out_ref)
     for k in range(len(DIRECTIONS)):
-        out_ref[place_ref[k]] = blocks[:, k * ghost_n : (k + 1) * ghost_n]
-
-
-def take(in_ref, place_ref):
-    return jnp.concatenate([in_ref[place_ref[k]] for k in range(len(DIRECTIONS))], axis=1)
+        out_ref[places[k]] = blocks[:, k * ghost_n : (k + 1) * ghost_n]
+
+
+def take(in_ref):
+    return jnp.concatenate([in_ref[place] for place in towards(1)], axis=1)
 
 
 def inverse_mass(species):
@@ -87,15 +100,21 @@
 
 def start_kernel(pos_ref, vel_ref, force_ref, species_ref, send_ref, moved_ref, half_ref, out_ref):
     species = species_ref[...]
-    inverse = inverse_mass(species)
-    half = vel_ref[...] + 0.5 * STEP * inverse * force_ref[...]
+    half = vel_ref[...] + 0.5 * STEP * inverse_mass(species) * force_ref[...]
     moved = pos_ref[...] + STEP * half
     half_ref[...] = half
     moved_ref[...] = moved
     spare = jnp.zeros((1, species.shape[1]), F32)
-    sends = send_ref[...].astype(F32)
-    sends = jnp.concatenate([sends, jnp.zeros((8, species.shape[1] - sends.shape[1]), F32)], axis=1)
-    out_ref[...] = jnp.concatenate([moved, species.astype(F32), half, spare, sends], axis=0)
+    sources = split3(jnp.concatenate([moved, species.astype(F32), half, spare], axis=0))
+    sends = send_ref[...]
+    picked = sum_parts(mm(sources, one_hot(by_direction(sends), species.shape[1])))
+    sent = sends.astype(F32)
+    ghost_n = sent.shape[1]
+    rest = jnp.zeros((TILE[0], TILE[1] - 4 * ghost_n), F32)
+    out_ref[...] = jnp.zeros_like(out_ref)
+    for k, place in enumerate(towards(1)):
+        block = picked[:, k * ghost_n : (k + 1) * ghost_n]
+        out_ref[place] = jnp.concatenate([block[:4], block[4:], sent[:4], sent[4:], rest], axis=1)
 
 
 def total_force(own, back, sends):
@@ -103,13 +122,26 @@
     return own + sum_parts(mm_nt(split3(padded_rows(back, 8)), pick))[0:3]
 
 
-def domain_force(all_ref, owner, around_ref, first, sends, atom_n):
+def forces_tile(own, on_ghosts):
+    room = TILE[1] - on_ghosts.shape[1]
+    upper = jnp.concatenate([on_ghosts, own[:, :room]], axis=1)
+    last = [own[c : c + 1, room:] for c in range(3)]
+    last.append(jnp.zeros((1, TILE[1] - 3 * (own.shape[1] - room)), F32))
+    return jnp.concatenate([upper, jnp.concatenate(last, axis=1)], axis=0)
+
+
+def domain_force(all_ref, shift_gx, shift_yz, sends, atom_n):
     ghost_n = sends.shape[1]
     back = []
-    for k in range(len(DIRECTIONS)):
-        start = atom_n + k * ghost_n
-        back.append(all_ref[around_ref[first + k]][:, start : start + ghost_n])
-    return total_force(all_ref[owner][:, :atom_n], jnp.concatenate(back, axis=1), sends)
+    for k, (a, b) in enumerate(DIRECTIONS):
+        place = device_at(shift_gx + a, shift_yz + b)
+        back.append(all_ref[place][0:3, k * ghost_n : (k + 1) * ghost_n])
+    tile = all_ref[device_at(shift_gx, shift_yz)]
+    room = TILE[1] - len(DIRECTIONS) * ghost_n
+    over = atom_n - room
+    last = jnp.concatenate([tile[3:4, c * over : (c + 1) * over] for c in range(3)], axis=0)
+    own = jnp.concatenate([tile[0:3, TILE[1] - room :], last], axis=1)
+    return total_force(own, jnp.concatenate(back, axis=1), sends)
 
 
 def step_on(moved, half, kinds, forces):
@@ -118,21 +150,21 @@
     return half_two, moved + STEP * half_two
 
 
-def last_kernel(place_ref, own_ref, send_ref, half_two_ref, species_ref, in_ref, vel_ref, force_ref):
-    forces = total_force(own_ref[...], take(in_ref, place_ref), send_ref[...])
+def last_kernel(own_ref, send_ref, half_two_ref, species_ref, in_ref, vel_ref, force_ref):
+    forces = total_force(own_ref[...], take(in_ref), send_ref[...])
     force_ref[...] = forces
     vel_ref[...] = half_two_ref[...] + 0.5 * STEP * inverse_mass(species_ref[...]) * forces
 
 
 def prepare_kernel(
     live_ref,
+    radial_ref,
+    embed_ref,
+    readout_ref,
     count_ref,
     slots_ref,
-    radial_ref,
-    embed_ref,
     env_t_ref,
     latent_ref,
-    readout_ref,
     neigh_ref,
     centre_ref,
     total_ref,
@@ -147,7 +179,6 @@
     features, latent = env_t_ref.shape
     slots_t = mm_nt(identity(slots_ref.shape[1]), slots_ref[...].astype(F32).astype(BF16)).astype(BF16)
     list_pairs(live_ref, count_ref, slots_t, neigh_ref, centre_ref, total_ref)
-
     eye = identity(latent)
     half = BF16(0.5)
     latent_w = latent_ref[...]
@@ -171,7 +202,7 @@
     slot_n = slots_t.shape[0]
     blocks, lanes = neigh_ref.shape
     atom_row = lax.broadcasted_iota(jnp.int32, (1, atom_n), 1)
-    used = jnp.where(atom_row < live_ref[0], count_ref[...], 0).astype(F32)
+    used = jnp.where(atom_row < live_ref[...], count_ref[...], 0).astype(F32)
     row_i = lax.broadcasted_iota(jnp.int32, (atom_n, atom_n), 0)
     col_i = lax.broadcasted_iota(jnp.int32, (atom_n, atom_n), 1)
     end = jnp.sum(jnp.where(col_i <= row_i, used, 0.0), axis=1, keepdims=True)
@@ -214,24 +245,25 @@
         ((latent, 128), F32),
         ((BASIS_PAD, latent), BF16),
     )
+    operands = [
+        live_atoms.reshape(1, 1),
+        radial_weight,
+        species_embed,
+        readout[None, :],
+        neighbour_count.reshape(1, atom_n),
+        neighbours,
+        env_weight[0].T,
+        latent_weight[0],
+    ]
     out = pl.pallas_call(
         prepare_kernel,
         out_shape=[jax.ShapeDtypeStruct(*shape) for shape in shapes],
-        in_specs=[SMEM] + [VMEM] * 7,
+        in_specs=[VMEM] * len(operands),
         out_specs=[VMEM, VMEM, SMEM] + [VMEM] * 7,
         compiler_params=pltpu.CompilerParams(vmem_limit_bytes=24 * 2**20),
         cost_estimate=pl.CostEstimate(flops=2 * 10**9, bytes_accessed=4 * 2**20, transcendentals=0),
         name="prepare",
-    )(
-        live_atoms,
-        neighbour_count.reshape(1, atom_n),
-        neighbours,
-        radial_weight,
-        species_embed,
-        env_weight[0].T,
-        latent_weight[0],
-        readout[None, :],
-    )
+    )(*operands)
     return out[:3], out[3:]
 
 
@@ -242,9 +274,7 @@
 
 
 def force_kernel(
-    place_ref,
     total_ref,
-    around_ref,
     neigh_ref,
     centre_ref,
     moved_ref,
@@ -267,24 +297,29 @@
     ghost_n = out_ghost_n
     ext_n = atom_n + ghost_n * len(DIRECTIONS)
     own_kind = own_kind_ref[...]
-    from_owners = [in_ref[place_ref[k]] for k in range(len(DIRECTIONS))]
-    sends = [owner[8:16, :ghost_n].astype(jnp.int32) for owner in from_owners]
-    picks = [one_hot(sends[k][k : k + 1], atom_n) for k in range(len(DIRECTIONS))]
+    from_owners = [in_ref[place] for place in towards(-1)]
     ghosts = jnp.concatenate(
-        [sum_parts(mm(split3(owner[0:8]), pick)) for owner, pick in zip(from_owners, picks)], axis=1
+        [
+            jnp.concatenate([owner[:, n * ghost_n : (n + 1) * ghost_n] for owner in from_owners], axis=1)
+            for n in range(2)
+        ],
+        axis=0,
     )
     ghost_kind = ghosts[3:4].astype(jnp.int32)
     if second_call:
         half_ref, send_ref, all_ref, half_two_ref, end_ref, own_out_ref, out_ref = refs
         on_ghosts = []
-        for k in range(len(DIRECTIONS)):
-            whole = domain_force(all_ref, place_ref[k], around_ref, k * 8, sends[k], atom_n)
-            on_ghosts.append(sum_parts(mm(split3(padded_rows(whole, 8)), picks[k]))[0:3])
+        for k, (a, b) in enumerate(DIRECTIONS):
+            sends = jnp.concatenate(
+                [from_owners[k][:, n * ghost_n : (n + 1) * ghost_n] for n in (2, 3)], axis=0
+            ).astype(jnp.int32)
+            whole = domain_force(all_ref, -a, -b, sends, atom_n)
+            picked = mm(split3(padded_rows(whole, 8)), one_hot(sends[k : k + 1], atom_n))
+            on_ghosts.append(sum_parts(picked)[0:3])
         _, ghost_pos = step_on(
             ghosts[0:3], ghosts[4:7], ghost_kind, jnp.concatenate(on_ghosts, axis=1)
         )
-        here = len(DIRECTIONS)
-        whole = domain_force(all_ref, place_ref[here], around_ref, here * 8, send_ref[...], atom_n)
+        whole = domain_force(all_ref, 0, 0, send_ref[...], atom_n)
         half_two, own_pos = step_on(moved_ref[...], half_ref[...], own_kind, whole)
         half_two_ref[...] = half_two
         end_ref[...] = own_pos
@@ -413,30 +448,30 @@
     own = on_centre - on_neigh[:, :atom_n]
     if second_call:
         own_out_ref[...] = own
-        put(out_ref, place_ref, -on_neigh[:, atom_n:])
+        put(out_ref, -on_neigh[:, atom_n:])
     else:
-        out_ref[...] = jnp.concatenate([own, -on_neigh[:, atom_n:]], axis=1)
-
-
-def pair_forces(places, pairs, own_pos, own_kind, weights, incoming, ghost_n, second=()):
-    place, around = places
+        tile = forces_tile(own, -on_neigh[:, atom_n:])
+        out_ref[...] = jnp.broadcast_to(tile[None], out_ref.shape)
+
+
+def pair_forces(pairs, own_pos, own_kind, weights, incoming, ghost_n, second=()):
     neigh, centre, total = pairs
     blocks, lanes = neigh.shape
     latent, features = weights[2].shape
     atom_n = own_pos.shape[1]
     devices = incoming.shape[0]
     ext_n = atom_n + ghost_n * len(DIRECTIONS)
-    operands = [place, total, around, neigh, centre, own_pos, own_kind, *weights, incoming, *second]
+    operands = [total, neigh, centre, own_pos, own_kind, *weights, incoming, *second]
     if second:
         out_shape = [jax.ShapeDtypeStruct((3, atom_n), F32)] * 3
         out_shape.append(jax.ShapeDtypeStruct((devices, 3, ghost_n), F32))
     else:
-        out_shape = [jax.ShapeDtypeStruct((3, ext_n), F32)]
+        out_shape = [jax.ShapeDtypeStruct((devices, *TILE), F32)]
     pair_rows = blocks * lanes
     return pl.pallas_call(
         functools.partial(force_kernel, second_call=bool(second), out_ghost_n=ghost_n),
         out_shape=out_shape,
-        in_specs=[SMEM] * 3 + [VMEM] * (len(operands) - 3),
+        in_specs=[SMEM] + [VMEM] * (len(operands) - 1),
         out_specs=[VMEM] * len(out_shape),
         scratch_shapes=[
             pltpu.VMEM((blocks, ext_n + atom_n, lanes), BF16),
@@ -459,26 +494,15 @@
     )(*operands)
 
 
-def small_call(kernel, name, smem_n, operands, out_shape):
+def small_call(kernel, name, operands, out_shape):
     return pl.pallas_call(
         kernel,
         out_shape=out_shape,
-        in_specs=[SMEM] * smem_n + [VMEM] * (len(operands) - smem_n),
+        in_specs=[VMEM] * len(operands),
         out_specs=[VMEM] * len(out_shape),
         compiler_params=pltpu.CompilerParams(vmem_limit_bytes=16 * 2**20),
         name=name,
     )(*operands)
-
-
-def devices_at(shift_gx, shift_yz):
-    gx_n, yz_n = lax.axis_size("gx"), lax.axis_size("yz")
-    gx = (lax.axis_index("gx") + jnp.asarray(shift_gx, jnp.int32) + gx_n) % gx_n
-    yz = (lax.axis_index("yz") + jnp.asarray(shift_yz, jnp.int32) + yz_n) % yz_n
-    return gx * yz_n + yz
-
-
-def gather_all(block):
-    return lax.all_gather(block, ("gx", "yz"))
 
 
 def exchange(blocks):
@@ -502,35 +526,28 @@
 ):
     atom_n = positions.shape[1]
     ghost_n = send_list.shape[1]
-    ahead = devices_at([a for a, _ in DIRECTIONS], [b for _, b in DIRECTIONS])
-    sources = [(-a, -b) for a, b in DIRECTIONS] + [(0, 0)]
-    behind = devices_at([a for a, _ in sources], [b for _, b in sources])
-    around = devices_at(
-        [a + c for a, _ in sources for c, _ in DIRECTIONS], [b + d for _, b in sources for _, d in DIRECTIONS]
-    )
+    devices = lax.axis_size("gx") * lax.axis_size("yz")
     kinds = species.reshape(1, atom_n)
     atoms = jax.ShapeDtypeStruct((3, atom_n), F32)
 
     moved, half, sent = small_call(
         start_kernel,
         "start",
-        0,
         [positions, velocities, forces_start, kinds, send_list],
-        [atoms, atoms, jax.ShapeDtypeStruct((16, atom_n), F32)],
-    )
-    got = gather_all(sent)
+        [atoms, atoms, jax.ShapeDtypeStruct((devices, *TILE), F32)],
+    )
+    got = exchange(sent)
     pairs, weights = prepare(
         live_atoms, neighbour_count, neighbours, radial_weight, species_embed, env_weight, latent_weight, readout
     )
-    places = (behind, around)
-    (sent,) = pair_forces(places, pairs, moved, kinds, weights, got, ghost_n)
-    every = gather_all(sent)
+    (sent,) = pair_forces(pairs, moved, kinds, weights, got, ghost_n)
+    every = exchange(sent)
     half_two, positions_end, own, sent = pair_forces(
-        places, pairs, moved, kinds, weights, got, ghost_n, (half, send_list, every)
+        pairs, moved, kinds, weights, got, ghost_n, (half, send_list, every)
     )
     back = exchange(sent)
     velocities_end, forces_end = small_call(
-        last_kernel, "last", 1, [ahead, own, send_list, half_two, kinds, back], [atoms, atoms]
+        last_kernel, "last", [own, send_list, half_two, kinds, back], [atoms, atoms]
     )
     return (positions_end, velocities_end, forces_end)
 

time: 189 us -> 87.8 us (0.46)
  blocking collectives: 140 us -> 35.6 us
  Pallas kernels: 27.6 us -> 35.6 us
  waiting for transfers between devices: 7.45 us -> 2.2 us
  local copies, waits for them, and re-layouts: 2.4 us -> 5.08 us
  starting transfers between devices: 9.9 us -> 7.3 us
    all_gather x2 -> x0, blocking collectives: 140 us -> none  [gather_all(): return lax.all_gather(block, ('gx', 'yz'))]
    all_to_all x0 -> x2, blocking collectives: none -> 35.6 us  [exchange(): return lax.all_to_all(blocks, ('gx', 'yz'), 0, 0, tiled=True)]
    pallas_call x2, Pallas kernels: 23.4 us -> 31 us  [pair_forces(): pl.pallas_call(functools.partial(force_kernel, second_call=bool(second),...]
    all_to_all x1, waiting for transfers between devices: 7.45 us -> 2.2 us  [exchange(): return lax.all_to_all(blocks, ('gx', 'yz'), 0, 0, tiled=True)]
    unnamed x36 -> x26, local copies, waits for them, and re-layouts: 2.4 us -> 5.08 us
    all_to_all x1, starting transfers between devices: 9.9 us -> 7.3 us  [exchange(): return lax.all_to_all(blocks, ('gx', 'yz'), 0, 0, tiled=True)]
  transfers between devices with their start and end apart: 1 -> 1, of which waited for: 1 -> 1; matrix products, arithmetic and copies ran while one was open for 0% -> 0% of each run, Pallas kernels for 0% -> 3%
where the time goes in v4:
time: 87.8 us; the launch traced here: 87.1 us
  Pallas kernels  35.6 us (41%)
  blocking collectives  35.6 us (41%)
  starting transfers between devices  7.3 us (8%)
  local copies, waits for them, and re-layouts  5.08 us (6%)
  waiting for transfers between devices  2.2 us (3%)
  between operations  1.41 us (2%)
    all_to_all x2, blocking collectives, exchange(): return lax.all_to_all(blocks, ('gx', 'yz'), 0, 0, tiled=True)  35.6 us
    pallas_call x2, Pallas kernels, pair_forces(): pl.pallas_call(functools.partial(force_kernel, second_call=bool(second),...  31 us
    all_to_all x1, starting transfers between devices, exchange(): return lax.all_to_all(blocks, ('gx', 'yz'), 0, 0, tiled=True)  7.3 us
    unnamed x26, local copies, waits for them, and re-layouts  5.08 us
    pallas_call x1, Pallas kernels, prepare(): pl.pallas_call(prepare_kernel, out_shape=[jax.ShapeDtypeStruct(*shape) fo...  2.87 us
    all_to_all x1, waiting for transfers between devices, exchange(): return lax.all_to_all(blocks, ('gx', 'yz'), 0, 0, tiled=True)  2.2 us
  transfers between devices with their start and end apart: 1, of which 1 were waited for; matrix products, arithmetic and copies ran while one was open for 0% of the time, Pallas kernels for 3%

profile of v4, /device:TPU:0, one launch (start us, length us, event | category | flops | bytes accessed | tf_op | source)
XLA Modules:
  0.0 87.1 jit_solution(1031673676804099913)
XLA Ops:
  0.6 0.0 copy-start.2
  0.6 0.6 copy-done.2
  1.3 0.0 copy-start
  1.3 0.7 copy-done
  2.0 0.0 copy-start.3
  2.0 0.7 copy-done.3
  2.7 0.0 copy-start.4
  2.7 0.7 copy-done.4
  3.3 0.0 copy-start.5
  3.3 0.7 copy-done.5
  4.0 0.9 %start.1 = (f32[3,48]{1,0:T(4,128)S(1)}, f32[3,48]{1,0:T(4,128)S(1)}, f32[32,4,128]{2,1,0:T(4,128)}) custom-call(f32[3,48]{1,0:T(4,128)S(1)} %copy-done.3, f32[3,48]{1,0:T(4,128)S(1)} %copy-done.4, f32[3,48]{1,0:T(4,128)S(1)} %copy-done.5, s32[1,48]{1,0:T(1,128)S(1)} %bitcast.8, s32[8,12]{1,0:T(8,128)S(1)} %copy-done), custom_call_target="tpu_custom_call" | custom-call | tf_op jit(solution)/shard_map/start/pallas_call | solution.py:498
  4.9 0.0 copy-start.12
  4.9 0.0 copy-start.7
  5.0 0.0 copy-start.8
  5.0 0.0 copy-start.9
  5.0 7.3 %all-to-all-start = ((f32[32,4,128]{2,1,0:T(4,128)}), f32[32,4,128]{2,1,0:T(4,128)S(1)}, u32[]{:S(2)}, u32[]{:S(2)}) async-start(f32[32,4,128]{2,1,0:T(4,128)} %get-tuple-element.33), calls=%async_computation | async-start | bytes 131072 | tf_op jit(solution)/shard_map/all_to_all | solution.py:509
  12.3 0.0 copy-start.10
  12.9 0.0 copy-done.12
  13.0 0.0 copy-start.11
  13.0 0.0 copy-done.7
  13.0 0.0 copy-done.8
  13.0 0.0 copy-done.9
  13.0 0.0 copy-done.10
  13.0 0.6 copy-done.11
  13.6 0.0 copy-start.6
  13.6 1.1 %copy-done.6 = bf16[1,576,512]{2,1,0:T(8,128)(2,1)S(1)} copy-done((bf16[1,576,512]{2,1,0:T(8,128)(2,1)S(1)}, bf16[1,576,512]{2,1,0:T(8,128)(2,1)}, u32[]{:S(2)}) %copy-start.6) | copy-done | bytes 589848
  14.7 2.9 %prepare.1 = (s32[6,1024]{1,0:T(8,128)S(1)}, s32[6,1024]{1,0:T(8,128)S(1)}, s32[1]{0:T(128)}, bf16[512,32]{1,0:T(8,128)(2,1)S(1)}, bf16[592,512]{1,0:T(8,128)(2,...) custom-call(s32[1,1]{1,0:T(1,128)} %bitcast.7.live_ref, ...), custom_call_target="tpu_custom_call" | custom-call | flops 2000000000 | bytes 4194304 | tf_op jit(solution)/shard_map/prepare/pallas_call | solution.py:258
  17.6 2.2 %all-to-all-done.in_ref = f32[32,4,128]{2,1,0:T(4,128)S(1)} async-done(((f32[32,4,128]{2,1,0:T(4,128)}), f32[32,4,128]{2,1,0:T(4,128)S(1)}, u32[]{:S(2)}, u32[]{:S(2)}) %all-to-all-start) | async-done | bytes 65568 | tf_op jit(solution)/shard_map/all_to_all | solution.py:509
  19.8 14.6 %pair_forces.2 = f32[32,4,128]{2,1,0:T(4,128)S(1)} custom-call(s32[1]{0:T(128)} %get-tuple-element.22.total_ref, s32[6,1024]{1,0:T(8,128)S(1)} %get-tuple-element.23.neigh_ref, s32[6,1024]{1,0:T(8,128)S(1)} %get-tuple-element.24.centre_ref, f32[3,48]{1,0:T(4,128)S(1)} %get-tuple-element.25.moved_ref, s32[1,48]{1,0:T(1,128)S(1)} %bitcast.9, ...), custom_call_target="tpu_custom_call" | custom-call | flops 8493465600 | bytes 4194304 | tf_op jit(solution)/shard_map/pair_forces/pallas_call | solution.py:471
  34.4 0.0 copy-start.1
  34.4 18.5 %all_to_all.15.refs_2_ = f32[32,4,128]{2,1,0:T(4,128)S(1)} all-to-all(f32[32,4,128]{2,1,0:T(4,128)S(1)} %pair_forces.2), channel_id=1, replica_groups=mesh['gx'=8,'yz'=4] {'gx','yz'}, dimensions={0} | all-to-all | bytes 131072 | tf_op jit(solution)/shard_map/all_to_all | solution.py:509
  52.9 0.0 copy-done.1
  52.9 16.3 %pair_forces.3 = (f32[3,48]{1,0:T(4,128)S(1)}, f32[3,48]{1,0:T(4,128)}, f32[3,48]{1,0:T(4,128)S(1)}, f32[32,3,12]{2,1,0:T(4,128)S(1)}) custom-call(s32[1]{0:T(128)} %get-tuple-element.22.total_ref, s32[6,1024]{1,0:T(8,128)S(1)} %get-tuple-element.23.neigh_ref, s32[6,1024]{1,0:T(8,128)S(1)} %get-tuple-element.24.centre_ref, ...), custom_call_target="tpu_custom_call" | custom-call | flops 8493465600 | bytes 4194304 | tf_op jit(solution)/shard_map/pair_forces/pallas_call | solution.py:471
  69.3 17.0 %all_to_all.16.in_ref = f32[32,3,12]{2,1,0:T(4,128)S(1)} all-to-all(f32[32,3,12]{2,1,0:T(4,128)S(1)} %get-tuple-element.38), channel_id=1, replica_groups=mesh['gx'=8,'yz'=4] {'gx','yz'}, dimensions={0} | all-to-all | bytes 9216 | tf_op jit(solution)/shard_map/all_to_all | solution.py:509
  86.3 0.8 last.1
  (1 shorter events, 0.0 us)
Async XLA Ops:
  0.6 0.7 copy-start.2
  1.3 0.7 copy-start
  2.0 0.7 copy-start.3
  2.7 0.7 copy-start.4
  3.3 0.7 copy-start.5
  4.9 8.0 %copy-start.12 = (bf16[512]{0:T(512)(128)(2,1)S(1)}, bf16[512]{0:T(512)(128)(2,1)}, u32[]{:S(2)}) copy-start(bf16[512]{0:T(512)(128)(2,1)} %param.25) | copy-start | bytes 3076
  4.9 8.0 %copy-start.7 = (bf16[1,512,64]{1,2,0:T(8,128)(2,1)S(1)}, bf16[1,512,64]{1,2,0:T(8,128)(2,1)}, u32[]{:S(2)}) copy-start(bf16[1,512,64]{1,2,0:T(8,128)(2,1)} %param.23) | copy-start | bytes 196612
  5.0 8.0 %copy-start.8 = (s32[48,128]{1,0:T(8,128)S(1)}, s32[48,128]{1,0:T(8,128)}, u32[]{:S(2)}) copy-start(s32[48,128]{1,0:T(8,128)} %slots_ref.1) | copy-start | bytes 73732
  5.0 8.0 %copy-start.9 = (bf16[2,8,512]{2,1,0:T(8,128)(2,1)S(1)}, bf16[2,8,512]{2,1,0:T(8,128)(2,1)}, u32[]{:S(2)}) copy-start(bf16[2,8,512]{2,1,0:T(8,128)(2,1)} %embed_ref.1) | copy-start | bytes 49156
  5.0 14.8 %all-to-all-start = ((f32[32,4,128]{2,1,0:T(4,128)}), f32[32,4,128]{2,1,0:T(4,128)S(1)}, u32[]{:S(2)}, u32[]{:S(2)}) async-start(f32[32,4,128]{2,1,0:T(4,128)} %get-tuple-element.33), calls=%async_computation | async-start | bytes 131072 | tf_op jit(solution)/shard_map/all_to_all | solution.py:509
  12.3 0.7 copy-start.10
  13.0 0.7 copy-start.11
  13.6 1.1 %copy-start.6 = (bf16[1,576,512]{2,1,0:T(8,128)(2,1)S(1)}, bf16[1,576,512]{2,1,0:T(8,128)(2,1)}, u32[]{:S(2)}) copy-start(bf16[1,576,512]{2,1,0:T(8,128)(2,1)} %param.24) | copy-start | bytes 1769476
  34.4 18.5 %copy-start.1 = (s32[8,12]{1,0:T(8,128)S(1)}, s32[8,12]{1,0:T(8,128)}, u32[]{:S(2)}) copy-start(s32[8,12]{1,0:T(8,128)} %send_ref.3) | copy-start | bytes 1156

commit v5 on v4

--- a/solution.py
+++ b/solution.py
@@ -98,8 +98,23 @@
     return inverse
 
 
-def start_kernel(pos_ref, vel_ref, force_ref, species_ref, send_ref, moved_ref, half_ref, out_ref):
+def start_kernel(
+    ahead_ref,
+    pos_ref,
+    vel_ref,
+    force_ref,
+    species_ref,
+    live_ref,
+    count_ref,
+    send_ref,
+    moved_ref,
+    half_ref,
+    used_ref,
+    out_ref,
+):
     species = species_ref[...]
+    slot = lax.broadcasted_iota(jnp.int32, species.shape, 1)
+    used_ref[...] = jnp.where(slot < live_ref[...].reshape(1, 1), count_ref[...], 0).astype(F32)
     half = vel_ref[...] + 0.5 * STEP * inverse_mass(species) * force_ref[...]
     moved = pos_ref[...] + STEP * half
     half_ref[...] = half
@@ -112,9 +127,9 @@
     ghost_n = sent.shape[1]
     rest = jnp.zeros((TILE[0], TILE[1] - 4 * ghost_n), F32)
     out_ref[...] = jnp.zeros_like(out_ref)
-    for k, place in enumerate(towards(1)):
+    for k in range(len(DIRECTIONS)):
         block = picked[:, k * ghost_n : (k + 1) * ghost_n]
-        out_ref[place] = jnp.concatenate([block[:4], block[4:], sent[:4], sent[4:], rest], axis=1)
+        out_ref[ahead_ref[k]] = jnp.concatenate([block[:4], block[4:], sent[:4], sent[4:], rest], axis=1)
 
 
 def total_force(own, back, sends):
@@ -156,18 +171,12 @@
     vel_ref[...] = half_two_ref[...] + 0.5 * STEP * inverse_mass(species_ref[...]) * forces
 
 
-def prepare_kernel(
-    live_ref,
+def weights_kernel(
     radial_ref,
     embed_ref,
     readout_ref,
-    count_ref,
-    slots_ref,
     env_t_ref,
     latent_ref,
-    neigh_ref,
-    centre_ref,
-    total_ref,
     into_ref,
     on_hidden_ref,
     on_inner_ref,
@@ -176,9 +185,7 @@
     readout_t_ref,
     radial_back_ref,
 ):
-    features, latent = env_t_ref.shape
-    slots_t = mm_nt(identity(slots_ref.shape[1]), slots_ref[...].astype(F32).astype(BF16)).astype(BF16)
-    list_pairs(live_ref, count_ref, slots_t, neigh_ref, centre_ref, total_ref)
+    latent = latent_ref.shape[1]
     eye = identity(latent)
     half = BF16(0.5)
     latent_w = latent_ref[...]
@@ -197,12 +204,11 @@
     into_ref[...] = mm_nt(eye, into).astype(BF16)
 
 
-def list_pairs(live_ref, count_ref, slots_t, neigh_ref, centre_ref, total_ref):
-    atom_n = count_ref.shape[1]
-    slot_n = slots_t.shape[0]
+def list_kernel(used_ref, slots_ref, neigh_ref, centre_ref, total_ref):
+    atom_n, slot_n = slots_ref.shape
     blocks, lanes = neigh_ref.shape
-    atom_row = lax.broadcasted_iota(jnp.int32, (1, atom_n), 1)
-    used = jnp.where(atom_row < live_ref[...], count_ref[...], 0).astype(F32)
+    slots_t = mm_nt(identity(slot_n), slots_ref[...].astype(F32).astype(BF16)).astype(BF16)
+    used = used_ref[...]
     row_i = lax.broadcasted_iota(jnp.int32, (atom_n, atom_n), 0)
     col_i = lax.broadcasted_iota(jnp.int32, (atom_n, atom_n), 1)
     end = jnp.sum(jnp.where(col_i <= row_i, used, 0.0), axis=1, keepdims=True)
@@ -229,14 +235,23 @@
     lax.fori_loop(0, blocks, one_block, 0)
 
 
-def prepare(live_atoms, neighbour_count, neighbours, radial_weight, species_embed, env_weight, latent_weight, readout):
-    atom_n, slot_n = neighbours.shape
+def list_pairs(used, neighbours):
+    blocks = pl.cdiv(neighbours.size, LANES)
+    pairs = jax.ShapeDtypeStruct((blocks, LANES), jnp.int32)
+    return pl.pallas_call(
+        list_kernel,
+        out_shape=[pairs, pairs, jax.ShapeDtypeStruct((1,), jnp.int32)],
+        in_specs=[VMEM] * 2,
+        out_specs=[VMEM, VMEM, SMEM],
+        compiler_params=pltpu.CompilerParams(vmem_limit_bytes=16 * 2**20),
+        cost_estimate=pl.CostEstimate(flops=10**9, bytes_accessed=2**16, transcendentals=0),
+        name="list_pairs",
+    )(used, neighbours)
+
+
+def prepare_weights(radial_weight, species_embed, env_weight, latent_weight, readout):
     latent, features = env_weight.shape[1:]
-    blocks = pl.cdiv(atom_n * slot_n, LANES)
     shapes = (
-        ((blocks, LANES), jnp.int32),
-        ((blocks, LANES), jnp.int32),
-        ((1,), jnp.int32),
         ((latent, 2 * SPECIES + BASIS_PAD), BF16),
         ((latent + features + BASIS_PAD, latent), BF16),
         ((latent, features), BF16),
@@ -245,26 +260,16 @@
         ((latent, 128), F32),
         ((BASIS_PAD, latent), BF16),
     )
-    operands = [
-        live_atoms.reshape(1, 1),
-        radial_weight,
-        species_embed,
-        readout[None, :],
-        neighbour_count.reshape(1, atom_n),
-        neighbours,
-        env_weight[0].T,
-        latent_weight[0],
-    ]
-    out = pl.pallas_call(
-        prepare_kernel,
+    operands = [radial_weight, species_embed, readout[None, :], env_weight[0].T, latent_weight[0]]
+    return pl.pallas_call(
+        weights_kernel,
         out_shape=[jax.ShapeDtypeStruct(*shape) for shape in shapes],
         in_specs=[VMEM] * len(operands),
-        out_specs=[VMEM, VMEM, SMEM] + [VMEM] * 7,
+        out_specs=[VMEM] * len(shapes),
         compiler_params=pltpu.CompilerParams(vmem_limit_bytes=24 * 2**20),
-        cost_estimate=pl.CostEstimate(flops=2 * 10**9, bytes_accessed=4 * 2**20, transcendentals=0),
-        name="prepare",
+        cost_estimate=pl.CostEstimate(flops=10**9, bytes_accessed=4 * 2**20, transcendentals=0),
+        name="prepare_weights",
     )(*operands)
-    return out[:3], out[3:]
 
 
 def silu_pair(half_in):
@@ -494,15 +499,22 @@
     )(*operands)
 
 
-def small_call(kernel, name, operands, out_shape):
+def small_call(kernel, name, operands, out_shape, smem_n=0):
     return pl.pallas_call(
         kernel,
         out_shape=out_shape,
-        in_specs=[VMEM] * len(operands),
+        in_specs=[SMEM] * smem_n + [VMEM] * (len(operands) - smem_n),
         out_specs=[VMEM] * len(out_shape),
         compiler_params=pltpu.CompilerParams(vmem_limit_bytes=16 * 2**20),
         name=name,
     )(*operands)
+
+
+def devices_at(shift_gx, shift_yz):
+    gx_n, yz_n = lax.axis_size("gx"), lax.axis_size("yz")
+    gx = (lax.axis_index("gx") + jnp.asarray(shift_gx, jnp.int32) + gx_n) % gx_n
+    yz = (lax.axis_index("yz") + jnp.asarray(shift_yz, jnp.int32) + yz_n) % yz_n
+    return gx * yz_n + yz
 
 
 def exchange(blocks):
@@ -527,19 +539,29 @@
     atom_n = positions.shape[1]
     ghost_n = send_list.shape[1]
     devices = lax.axis_size("gx") * lax.axis_size("yz")
+    atoms = jax.ShapeDtypeStruct((3, atom_n), F32)
+
     kinds = species.reshape(1, atom_n)
-    atoms = jax.ShapeDtypeStruct((3, atom_n), F32)
-
-    moved, half, sent = small_call(
+    ahead = devices_at([a for a, _ in DIRECTIONS], [b for _, b in DIRECTIONS])
+    moved, half, used, sent = small_call(
         start_kernel,
         "start",
-        [positions, velocities, forces_start, kinds, send_list],
-        [atoms, atoms, jax.ShapeDtypeStruct((devices, *TILE), F32)],
+        [
+            ahead,
+            positions,
+            velocities,
+            forces_start,
+            kinds,
+            live_atoms,
+            neighbour_count.reshape(1, atom_n),
+            send_list,
+        ],
+        [atoms, atoms, jax.ShapeDtypeStruct((1, atom_n), F32), jax.ShapeDtypeStruct((devices, *TILE), F32)],
+        smem_n=1,
     )
     got = exchange(sent)
-    pairs, weights = prepare(
-        live_atoms, neighbour_count, neighbours, radial_weight, species_embed, env_weight, latent_weight, readout
-    )
+    pairs = list_pairs(used, neighbours)
+    weights = prepare_weights(radial_weight, species_embed, env_weight, latent_weight, readout)
     (sent,) = pair_forces(pairs, moved, kinds, weights, got, ghost_n)
     every = exchange(sent)
     half_two, positions_end, own, sent = pair_forces(

time: 87.8 us -> 83.3 us (0.949)
  Pallas kernels: 35.6 us -> 26.8 us
  blocking collectives: 35.6 us -> 41.5 us
  local copies, waits for them, and re-layouts: 5.08 us -> 0.7 us
  waiting for transfers between devices: 2.2 us -> 4.39 us
    pallas_call x2, Pallas kernels: 31 us -> 21.6 us  [pair_forces(): pl.pallas_call(functools.partial(force_kernel, second_call=bool(second),...]
    all_to_all x2, blocking collectives: 35.6 us -> 41.5 us  [exchange(): return lax.all_to_all(blocks, ('gx', 'yz'), 0, 0, tiled=True)]
    unnamed x26 -> x28, local copies, waits for them, and re-layouts: 5.08 us -> 0.7 us
    all_to_all x1, waiting for transfers between devices: 2.2 us -> 4.39 us  [exchange(): return lax.all_to_all(blocks, ('gx', 'yz'), 0, 0, tiled=True)]
    pallas_call x3 -> x4, Pallas kernels: 4.6 us -> 5.21 us  [the longest x2 2.25 us: small_call(): pl.pallas_call(kernel, out_shape=out_shape, in_specs=[SMEM] * smem_n + [V...]
  transfers between devices with their start and end apart: 1 -> 1, of which waited for: 1 -> 1; matrix products, arithmetic and copies ran while one was open for 0% -> 0% of each run, Pallas kernels for 3% -> 4%
where the time goes in v5:
time: 83.3 us; the launch traced here: 82.3 us
  blocking collectives  41.5 us (50%)
  Pallas kernels  26.8 us (32%)
  starting transfers between devices  7.3 us (9%)
  waiting for transfers between devices  4.39 us (5%)
  between operations  1.55 us (2%)
    all_to_all x2, blocking collectives, exchange(): return lax.all_to_all(blocks, ('gx', 'yz'), 0, 0, tiled=True)  41.5 us
    pallas_call x2, Pallas kernels, pair_forces(): pl.pallas_call(functools.partial(force_kernel, second_call=bool(second),...  21.6 us
    all_to_all x1, starting transfers between devices, exchange(): return lax.all_to_all(blocks, ('gx', 'yz'), 0, 0, tiled=True)  7.3 us
    all_to_all x1, waiting for transfers between devices, exchange(): return lax.all_to_all(blocks, ('gx', 'yz'), 0, 0, tiled=True)  4.39 us
    pallas_call x2, Pallas kernels, small_call(): pl.pallas_call(kernel, out_shape=out_shape, in_specs=[SMEM] * smem_n + [V...  2.25 us
    pallas_call x1, Pallas kernels, list_pairs(): pl.pallas_call(list_kernel, out_shape=[pairs, pairs, jax.ShapeDtypeStruct...  1.93 us
  transfers between devices with their start and end apart: 1, of which 1 were waited for; matrix products, arithmetic and copies ran while one was open for 0% of the time, Pallas kernels for 4%

profile of v5, /device:TPU:0, one launch (start us, length us, event | category | flops | bytes accessed | tf_op | source)
XLA Modules:
  0.0 82.3 jit_solution(11697336347882617029)
XLA Ops:
  0.6 0.0 copy-start.13
  0.6 0.0 copy-start.4
  0.7 0.0 copy-start.12
  0.7 0.0 copy-start.3
  0.7 0.0 copy-start
  1.4 0.0 copy-done.13
  1.4 0.0 copy-done.12
  1.4 0.0 copy-start.2
  1.4 0.0 copy-start.1
  1.4 0.0 copy-start.5
  1.4 0.0 copy-done.4
  1.5 0.0 copy-done.3
  1.5 0.0 copy-done
  1.5 0.6 copy-done.2
  2.1 0.0 copy-done.1
  2.1 0.0 copy-done.5
  2.1 1.4 %start.1 = (f32[3,48]{1,0:T(4,128)S(1)}, f32[3,48]{1,0:T(4,128)S(1)}, f32[1,48]{1,0:T(1,128)S(1)}, f32[32,4,128]{2,1,0:T(4,128)}) custom-call(s32[8]{0:T(128)S(1)} %fusion.ahead_ref, f32[3,48]{1,0:T(4,128)S(1)} %copy-done.2, f32[3,48]{1,0:T(4,128)S(1)} %copy-done.3, f32[3,48]{1,0:T(4,128)S(1)} %copy-done.4, s32[1,48]{1,0:T(1,128)S(1)} %bitcast.6, ...), custom_call_target="tpu_custom_call" | custom-call | tf_op jit(solution)/shard_map/start/pallas_call | solution.py:503
  3.5 0.0 copy-start.8
  3.5 7.3 %all-to-all-start = ((f32[32,4,128]{2,1,0:T(4,128)}), f32[32,4,128]{2,1,0:T(4,128)S(1)}, u32[]{:S(2)}, u32[]{:S(2)}) async-start(f32[32,4,128]{2,1,0:T(4,128)} %get-tuple-element.35), calls=%async_computation | async-start | bytes 131072 | tf_op jit(solution)/shard_map/all_to_all | solution.py:521
  10.9 0.0 copy-done.8
  10.9 0.0 copy-start.11
  10.9 0.0 copy-start.6
  10.9 0.0 copy-start.7
  10.9 0.0 copy-start.9
  10.9 0.0 copy-start.10
  10.9 1.9 %list_pairs.1 = (s32[6,1024]{1,0:T(8,128)S(1)}, s32[6,1024]{1,0:T(8,128)S(1)}, s32[1]{0:T(128)}) custom-call(f32[1,48]{1,0:T(1,128)S(1)} %get-tuple-element.23.used_ref, s32[48,128]{1,0:T(8,128)S(1)} %copy-done.8), custom_call_target="tpu_custom_call" | custom-call | flops 1000000000 | bytes 65536 | tf_op jit(solution)/shard_map/list_pairs/pallas_call | solution.py:241
  12.9 0.0 copy-done.11
  12.9 0.0 copy-done.6
  12.9 0.0 copy-done.7
  12.9 0.0 copy-done.9
  12.9 0.0 copy-done.10
  12.9 1.0 %prepare_weights.1 = (bf16[512,32]{1,0:T(8,128)(2,1)S(1)}, bf16[592,512]{1,0:T(8,128)(2,1)S(1)}, bf16[512,64]{1,0:T(8,128)(2,1)S(1)}, bf16[576,512]{1,0:T(8,128)...) custom-call(bf16[8,512]{1,0:T(8,128)(2,1)S(1)} %copy-done.10, ...), custom_call_target="tpu_custom_call" | custom-call | flops 1000000000 | bytes 4194304 | tf_op jit(solution)/shard_map/prepare_weights/pallas_call | solution.py:264
  14.0 4.4 %all-to-all-done.in_ref = f32[32,4,128]{2,1,0:T(4,128)S(1)} async-done(((f32[32,4,128]{2,1,0:T(4,128)}), f32[32,4,128]{2,1,0:T(4,128)S(1)}, u32[]{:S(2)}, u32[]{:S(2)}) %all-to-all-start) | async-done | bytes 65568 | tf_op jit(solution)/shard_map/all_to_all | solution.py:521
  18.3 10.0 %pair_forces.2 = f32[32,4,128]{2,1,0:T(4,128)S(1)} custom-call(s32[1]{0:T(128)} %get-tuple-element.24.total_ref, s32[6,1024]{1,0:T(8,128)S(1)} %get-tuple-element.25.neigh_ref, s32[6,1024]{1,0:T(8,128)S(1)} %get-tuple-element.26.centre_ref, f32[3,48]{1,0:T(4,128)S(1)} %get-tuple-element.27.moved_ref, s32[1,48]{1,0:T(1,128)S(1)} %bitcast.7, ...), custom_call_target="tpu_custom_call" | custom-call | flops 8493465600 | bytes 4194304 | tf_op jit(solution)/shard_map/pair_forces/pallas_call | solution.py:476
  28.3 20.7 %all_to_all.15.refs_2_ = f32[32,4,128]{2,1,0:T(4,128)S(1)} all-to-all(f32[32,4,128]{2,1,0:T(4,128)S(1)} %pair_forces.2), channel_id=1, replica_groups=mesh['gx'=8,'yz'=4] {'gx','yz'}, dimensions={0} | all-to-all | bytes 131072 | tf_op jit(solution)/shard_map/all_to_all | solution.py:521
  49.0 11.6 %pair_forces.3 = (f32[3,48]{1,0:T(4,128)S(1)}, f32[3,48]{1,0:T(4,128)}, f32[3,48]{1,0:T(4,128)S(1)}, f32[32,3,12]{2,1,0:T(4,128)S(1)}) custom-call(s32[1]{0:T(128)} %get-tuple-element.24.total_ref, s32[6,1024]{1,0:T(8,128)S(1)} %get-tuple-element.25.neigh_ref, s32[6,1024]{1,0:T(8,128)S(1)} %get-tuple-element.26.centre_ref, ...), custom_call_target="tpu_custom_call" | custom-call | flops 8493465600 | bytes 4194304 | tf_op jit(solution)/shard_map/pair_forces/pallas_call | solution.py:476
  60.7 20.8 %all_to_all.16.in_ref = f32[32,3,12]{2,1,0:T(4,128)S(1)} all-to-all(f32[32,3,12]{2,1,0:T(4,128)S(1)} %get-tuple-element.40), channel_id=1, replica_groups=mesh['gx'=8,'yz'=4] {'gx','yz'}, dimensions={0} | all-to-all | bytes 9216 | tf_op jit(solution)/shard_map/all_to_all | solution.py:521
  81.5 0.8 last.1
  (2 shorter events, 0.0 us)
Async XLA Ops:
  0.6 0.7 copy-start.13
  0.6 0.8 copy-start.4
  0.7 0.7 copy-start.12
  0.7 0.8 copy-start.3
  0.7 0.8 copy-start
  1.4 0.7 copy-start.2
  1.4 0.7 copy-start.1
  1.4 0.7 copy-start.5
  3.5 7.3 %copy-start.8 = (s32[48,128]{1,0:T(8,128)S(1)}, s32[48,128]{1,0:T(8,128)}, u32[]{:S(2)}) copy-start(s32[48,128]{1,0:T(8,128)} %slots_ref.1) | copy-start | bytes 73732
  3.5 14.8 %all-to-all-start = ((f32[32,4,128]{2,1,0:T(4,128)}), f32[32,4,128]{2,1,0:T(4,128)S(1)}, u32[]{:S(2)}, u32[]{:S(2)}) async-start(f32[32,4,128]{2,1,0:T(4,128)} %get-tuple-element.35), calls=%async_computation | async-start | bytes 131072 | tf_op jit(solution)/shard_map/all_to_all | solution.py:521
  10.9 2.0 %copy-start.11 = (bf16[512]{0:T(512)(128)(2,1)S(1)}, bf16[512]{0:T(512)(128)(2,1)}, u32[]{:S(2)}) copy-start(bf16[512]{0:T(512)(128)(2,1)} %param.27) | copy-start | bytes 3076
  10.9 2.0 %copy-start.6 = (bf16[1,576,512]{2,1,0:T(8,128)(2,1)S(1)}, bf16[1,576,512]{2,1,0:T(8,128)(2,1)}, u32[]{:S(2)}) copy-start(bf16[1,576,512]{2,1,0:T(8,128)(2,1)} %param.26) | copy-start | bytes 1769476
  10.9 2.0 %copy-start.7 = (bf16[1,512,64]{1,2,0:T(8,128)(2,1)S(1)}, bf16[1,512,64]{1,2,0:T(8,128)(2,1)}, u32[]{:S(2)}) copy-start(bf16[1,512,64]{1,2,0:T(8,128)(2,1)} %param.25) | copy-start | bytes 196612
  10.9 2.0 %copy-start.9 = (bf16[2,8,512]{2,1,0:T(8,128)(2,1)S(1)}, bf16[2,8,512]{2,1,0:T(8,128)(2,1)}, u32[]{:S(2)}) copy-start(bf16[2,8,512]{2,1,0:T(8,128)(2,1)} %embed_ref.1) | copy-start | bytes 49156
  10.9 2.0 %copy-start.10 = (bf16[8,512]{1,0:T(8,128)(2,1)S(1)}, bf16[8,512]{1,0:T(8,128)(2,1)}, u32[]{:S(2)}) copy-start(bf16[8,512]{1,0:T(8,128)(2,1)} %radial_ref.1) | copy-start | bytes 24580

commit v6 on v5

--- a/solution.py
+++ b/solution.py
@@ -15,6 +15,8 @@
 MASSES = (1.008, 12.011, 14.007, 15.999, 32.06, 22.99, 35.45, 30.97)
 
 LANES = 1024
+TAIL = 640
+LISTED = 2
 DIRECTIONS = ((-1, -1), (-1, 0), (-1, 1), (0, -1), (0, 1), (1, -1), (1, 0), (1, 1))
 TILE = (4, 128)
 BASIS_PAD = 16
@@ -217,7 +219,7 @@
     total_ref[0] = total.astype(jnp.int32)
     lane = lax.broadcasted_iota(jnp.int32, (1, lanes), 1)
 
-    def one_block(block, carry):
+    def one_block(block):
         place = (lane + block * lanes).astype(F32)
         past = end <= place
         centre = jnp.sum(jnp.where(past, 1.0, 0.0), axis=0, keepdims=True)
@@ -230,13 +232,18 @@
         valid = place < total
         neigh_ref[pl.ds(block, 1), :] = jnp.where(valid, neigh.astype(jnp.int32), -1)
         centre_ref[pl.ds(block, 1), :] = jnp.where(valid, centre_id, -1)
+
+    def some_blocks(step, carry):
+        for more in range(LISTED):
+            one_block(step * LISTED + more)
         return carry
 
-    lax.fori_loop(0, blocks, one_block, 0)
+    group = LISTED * lanes
+    lax.fori_loop(0, (total.astype(jnp.int32) + group - 1) // group, some_blocks, 0)
 
 
 def list_pairs(used, neighbours):
-    blocks = pl.cdiv(neighbours.size, LANES)
+    blocks = pl.cdiv(neighbours.size, LANES * LISTED) * LISTED
     pairs = jax.ShapeDtypeStruct((blocks, LANES), jnp.int32)
     return pl.pallas_call(
         list_kernel,
@@ -335,7 +342,8 @@
     pos = jnp.concatenate([own_pos, ghost_pos], axis=1)
     basis_n = SPECIES
     latent, features = on_inner_ref.shape
-    count = (total_ref[0] + lanes - 1) // lanes
+    total = total_ref[0]
+    full = (total + lanes - 1 - TAIL) // lanes
     scale = COUPLING * SLOTS ** (-0.5)
 
     pos8 = padded_rows(pos, 8) * (1.0 / RADIUS)
@@ -363,75 +371,81 @@
     dc_s[...] = jnp.zeros_like(dc_s)
     f_s[...] = jnp.zeros_like(f_s)
 
-    def geometry(block):
-        vec = u_s[block]
+    def each_block(one):
+        def step(block, carry):
+            one(block, lanes)
+            return carry
+
+        lax.fori_loop(0, full, step, 0)
+        pl.when(total > full * lanes)(functools.partial(one, full, TAIL))
+
+    def geometry(block, width):
+        vec = u_s[block, :, :width]
         square = jnp.sum(vec * vec, axis=0, keepdims=True)
         inside = jnp.maximum(1.0 - square, 0.0)
-        inside = jnp.where(centre_ref[pl.ds(block, 1), :] >= 0, inside, 0.0)
-        apart = square - mids
+        inside = jnp.where(centre_ref[pl.ds(block, 1), :width] >= 0, inside, 0.0)
+        apart = square - mids[:, :width]
         return vec, inside, apart, jnp.exp(-sharp * apart * apart)
 
-    def first(block, carry):
-        hot_j = one_hot(neigh_ref[pl.ds(block, 1), :], ext_n)
-        hot_c = one_hot(centre_ref[pl.ds(block, 1), :], atom_n)
+    def first(block, width):
+        hot_j = one_hot(neigh_ref[pl.ds(block, 1), :width], ext_n)
+        hot_c = one_hot(centre_ref[pl.ds(block, 1), :width], atom_n)
         hot = jnp.concatenate([hot_j, hot_c], axis=0)
-        hot_s[block] = hot
-        u_s[block] = sum_parts(mm(pos_parts, hot))
-        vec, inside, _, basis = geometry(block)
+        hot_s[block, :, :width] = hot
+        u_s[block, :, :width] = sum_parts(mm(pos_parts, hot))
+        vec, inside, _, basis = geometry(block, width)
         use = jnp.concatenate([hot_c * vec[k : k + 1].astype(BF16) for k in range(3)], axis=0)
-        use_s[block] = use
+        use_s[block, :, :width] = use
         pre = mm(weight_in, jnp.concatenate([hot, basis.astype(BF16)], axis=0))
         hidden, slope = silu_pair(pre)
-        slope_s[block] = slope.astype(BF16)
+        slope_s[block, :, :width] = slope.astype(BF16)
         taken = mm(on_hidden_ref[...], hidden.astype(BF16))
-        part_s[block] = taken[:latent]
+        part_s[block, :, :width] = taken[:latent]
         raw = taken[latent : latent + features]
-        raw_s[block] = raw
-        energy_s[block] = taken[latent + features : latent + features + 8]
+        raw_s[block, :, :width] = raw
+        energy_s[block, :, :width] = taken[latent + features : latent + features + 8]
         c_s[...] += mm_nt((raw * (inside * inside)).astype(BF16), use)
-        return carry
-
-    lax.fori_loop(0, count, first, 0)
+
+    each_block(first)
     c_all = c_s[...] * scale
     c_b = c_all.astype(BF16)
 
-    def second(block, carry):
-        _, inside, _, _ = geometry(block)
-        use = use_s[block]
+    def second(block, width):
+        _, inside, _, _ = geometry(block, width)
+        use = use_s[block, :, :width]
         env = inside * inside
-        weight = raw_s[block] * env
+        weight = raw_s[block, :, :width] * env
         inner = weight * mm(c_b, use)
-        later = part_s[block] + mm(on_inner_ref[...], inner.astype(BF16))
+        later = part_s[block, :, :width] + mm(on_inner_ref[...], inner.astype(BF16))
         gain, bent = silu_pair(later)
-        readout = jnp.concatenate([readout_ref[...]] * (lanes // 128), axis=1)
-        energy_s[block] += jnp.sum(gain * readout, axis=0, keepdims=True)
+        readout = jnp.concatenate([readout_ref[...]] * (width // 128), axis=1)
+        energy_s[block, :, :width] += jnp.sum(gain * readout, axis=0, keepdims=True)
         taken = mm(on_bent_ref[...], bent.astype(BF16))
-        part_s[block] = taken[:latent]
+        part_s[block, :, :width] = taken[:latent]
         a_in = taken[latent:] * env
-        ain_s[block] = a_in
+        ain_s[block, :, :width] = a_in
         dc_s[...] += mm_nt((a_in * weight).astype(BF16), use)
-        return carry
-
-    lax.fori_loop(0, count, second, 0)
+
+    each_block(second)
     c_dc = jnp.concatenate([c_all, dc_s[...] * scale], axis=0).astype(BF16)
     both = jnp.concatenate([c_all.T, dc_s[...].T * scale], axis=1).astype(BF16)
 
-    def third(block, carry):
-        vec, inside, apart, basis = geometry(block)
-        use = use_s[block]
-        hot = hot_s[block]
+    def third(block, width):
+        vec, inside, apart, basis = geometry(block, width)
+        use = use_s[block, :, :width]
+        hot = hot_s[block, :, :width]
         env = inside * inside
-        raw = raw_s[block]
+        raw = raw_s[block, :, :width]
         weight = raw * env
-        a_in = ain_s[block]
+        a_in = ain_s[block, :, :width]
         along = mm(c_dc, use)
         d_weight = a_in * along[:features] + along[features:]
-        d_env = jnp.sum(d_weight * raw, axis=0, keepdims=True) + energy_s[block][0:1]
-        ones = jnp.ones((BASIS_PAD, lanes), BF16)
-        d_hidden = part_s[block] + mm(
+        d_env = jnp.sum(d_weight * raw, axis=0, keepdims=True) + energy_s[block, :, :width][0:1]
+        ones = jnp.ones((BASIS_PAD, width), BF16)
+        d_hidden = part_s[block, :, :width] + mm(
             on_weight_ref[...], jnp.concatenate([d_weight.astype(BF16), ones], axis=0)
         )
-        d_pre = (d_hidden * slope_s[block].astype(F32)).astype(BF16)
+        d_pre = (d_hidden * slope_s[block, :, :width].astype(F32)).astype(BF16)
         d_basis = mm(radial_back_ref[...], d_pre)
         d_square = env * jnp.sum(d_basis * basis * apart, axis=0, keepdims=True) * (-2.0 * sharp)
         d_square = d_square - 2.0 * inside * d_env
@@ -441,12 +455,11 @@
             jnp.sum(d_all[k * atom_n : (k + 1) * atom_n] * hot_c, axis=0, keepdims=True)
             for k in range(3)
         ]
-        d_vec = jnp.concatenate(picked + [jnp.zeros((5, lanes), F32)], axis=0)
+        d_vec = jnp.concatenate(picked + [jnp.zeros((5, width), F32)], axis=0)
         d_vec = (d_vec + 2.0 * d_square * vec) * (1.0 / RADIUS)
         f_s[...] += mm_nt(split3(d_vec), hot)
-        return carry
-
-    lax.fori_loop(0, count, third, 0)
+
+    each_block(third)
     summed = f_s[0:8] + f_s[8:16] + f_s[16:24]
     on_centre = summed[0:3, ext_n:]
     on_neigh = summed[0:3, :ext_n]

time: 83.3 us -> 81 us (0.972)
  blocking collectives: 41.5 us -> 32.7 us
  Pallas kernels: 26.8 us -> 33.4 us
    all_to_all x2, blocking collectives: 41.5 us -> 32.7 us  [exchange(): return lax.all_to_all(blocks, ('gx', 'yz'), 0, 0, tiled=True)]
    pallas_call x2, Pallas kernels: 21.6 us -> 28.8 us  [pair_forces(): pl.pallas_call(functools.partial(force_kernel, second_call=bool(second),...]
  transfers between devices with their start and end apart: 1 -> 1, of which waited for: 1 -> 1; matrix products, arithmetic and copies ran while one was open for 0% -> 0% of each run, Pallas kernels for 4% -> 3%
where the time goes in v6:
time: 81 us; the launch traced here: 80.6 us
  Pallas kernels  33.4 us (41%)
  blocking collectives  32.7 us (40%)
  starting transfers between devices  7.3 us (9%)
  waiting for transfers between devices  4.97 us (6%)
  between operations  1.55 us (2%)
    all_to_all x2, blocking collectives, exchange(): return lax.all_to_all(blocks, ('gx', 'yz'), 0, 0, tiled=True)  32.7 us
    pallas_call x2, Pallas kernels, pair_forces(): pl.pallas_call(functools.partial(force_kernel, second_call=bool(second),...  28.8 us
    all_to_all x1, starting transfers between devices, exchange(): return lax.all_to_all(blocks, ('gx', 'yz'), 0, 0, tiled=True)  7.3 us
    all_to_all x1, waiting for transfers between devices, exchange(): return lax.all_to_all(blocks, ('gx', 'yz'), 0, 0, tiled=True)  4.97 us
    pallas_call x2, Pallas kernels, small_call(): pl.pallas_call(kernel, out_shape=out_shape, in_specs=[SMEM] * smem_n + [V...  2.25 us
  transfers between devices with their start and end apart: 1, of which 1 were waited for; matrix products, arithmetic and copies ran while one was open for 0% of the time, Pallas kernels for 3%

profile of v6, /device:TPU:0, one launch (start us, length us, event | category | flops | bytes accessed | tf_op | source)
XLA Modules:
  0.0 80.6 jit_solution(16960240687940309716)
XLA Ops:
  0.6 0.0 copy-start.13
  0.6 0.0 copy-start.4
  0.7 0.0 copy-start.12
  0.7 0.0 copy-start.3
  0.7 0.0 copy-start
  1.4 0.0 copy-done.13
  1.4 0.0 copy-done.12
  1.4 0.0 copy-start.2
  1.4 0.0 copy-start.1
  1.4 0.0 copy-start.5
  1.4 0.0 copy-done.4
  1.5 0.0 copy-done.3
  1.5 0.0 copy-done
  1.5 0.6 copy-done.2
  2.1 0.0 copy-done.1
  2.1 0.0 copy-done.5
  2.1 1.4 %start.1 = (f32[3,48]{1,0:T(4,128)S(1)}, f32[3,48]{1,0:T(4,128)S(1)}, f32[1,48]{1,0:T(1,128)S(1)}, f32[32,4,128]{2,1,0:T(4,128)}) custom-call(s32[8]{0:T(128)S(1)} %fusion.ahead_ref, f32[3,48]{1,0:T(4,128)S(1)} %copy-done.2, f32[3,48]{1,0:T(4,128)S(1)} %copy-done.3, f32[3,48]{1,0:T(4,128)S(1)} %copy-done.4, s32[1,48]{1,0:T(1,128)S(1)} %bitcast.6, ...), custom_call_target="tpu_custom_call" | custom-call | tf_op jit(solution)/shard_map/start/pallas_call | solution.py:516
  3.5 0.0 copy-start.8
  3.5 7.3 %all-to-all-start = ((f32[32,4,128]{2,1,0:T(4,128)}), f32[32,4,128]{2,1,0:T(4,128)S(1)}, u32[]{:S(2)}, u32[]{:S(2)}) async-start(f32[32,4,128]{2,1,0:T(4,128)} %get-tuple-element.35), calls=%async_computation | async-start | bytes 131072 | tf_op jit(solution)/shard_map/all_to_all | solution.py:534
  10.9 0.0 copy-done.8
  10.9 0.0 copy-start.11
  10.9 0.0 copy-start.6
  10.9 0.0 copy-start.7
  10.9 0.0 copy-start.9
  10.9 0.0 copy-start.10
  10.9 1.4 %list_pairs.1 = (s32[6,1024]{1,0:T(8,128)S(1)}, s32[6,1024]{1,0:T(8,128)S(1)}, s32[1]{0:T(128)}) custom-call(f32[1,48]{1,0:T(1,128)S(1)} %get-tuple-element.23.used_ref, s32[48,128]{1,0:T(8,128)S(1)} %copy-done.8), custom_call_target="tpu_custom_call" | custom-call | flops 1000000000 | bytes 65536 | tf_op jit(solution)/shard_map/list_pairs/pallas_call | solution.py:248
  12.3 0.0 copy-done.11
  12.3 0.0 copy-done.6
  12.3 0.0 copy-done.7
  12.3 0.0 copy-done.9
  12.3 0.0 copy-done.10
  12.4 1.0 %prepare_weights.1 = (bf16[512,32]{1,0:T(8,128)(2,1)S(1)}, bf16[592,512]{1,0:T(8,128)(2,1)S(1)}, bf16[512,64]{1,0:T(8,128)(2,1)S(1)}, bf16[576,512]{1,0:T(8,128)...) custom-call(bf16[8,512]{1,0:T(8,128)(2,1)S(1)} %copy-done.10, ...), custom_call_target="tpu_custom_call" | custom-call | flops 1000000000 | bytes 4194304 | tf_op jit(solution)/shard_map/prepare_weights/pallas_call | solution.py:271
  13.4 5.0 %all-to-all-done.in_ref = f32[32,4,128]{2,1,0:T(4,128)S(1)} async-done(((f32[32,4,128]{2,1,0:T(4,128)}), f32[32,4,128]{2,1,0:T(4,128)S(1)}, u32[]{:S(2)}, u32[]{:S(2)}) %all-to-all-start) | async-done | bytes 65568 | tf_op jit(solution)/shard_map/all_to_all | solution.py:534
  18.3 13.4 %pair_forces.2 = f32[32,4,128]{2,1,0:T(4,128)S(1)} custom-call(s32[1]{0:T(128)} %get-tuple-element.24.total_ref, s32[6,1024]{1,0:T(8,128)S(1)} %get-tuple-element.25.neigh_ref, s32[6,1024]{1,0:T(8,128)S(1)} %get-tuple-element.26.centre_ref, f32[3,48]{1,0:T(4,128)S(1)} %get-tuple-element.27.moved_ref, s32[1,48]{1,0:T(1,128)S(1)} %bitcast.7, ...), custom_call_target="tpu_custom_call" | custom-call | flops 8493465600 | bytes 4194304 | tf_op jit(solution)/shard_map/pair_forces/pallas_call | solution.py:489
  31.8 16.3 %all_to_all.15.refs_2_ = f32[32,4,128]{2,1,0:T(4,128)S(1)} all-to-all(f32[32,4,128]{2,1,0:T(4,128)S(1)} %pair_forces.2), channel_id=1, replica_groups=mesh['gx'=8,'yz'=4] {'gx','yz'}, dimensions={0} | all-to-all | bytes 131072 | tf_op jit(solution)/shard_map/all_to_all | solution.py:534
  48.1 15.3 %pair_forces.3 = (f32[3,48]{1,0:T(4,128)S(1)}, f32[3,48]{1,0:T(4,128)}, f32[3,48]{1,0:T(4,128)S(1)}, f32[32,3,12]{2,1,0:T(4,128)S(1)}) custom-call(s32[1]{0:T(128)} %get-tuple-element.24.total_ref, s32[6,1024]{1,0:T(8,128)S(1)} %get-tuple-element.25.neigh_ref, s32[6,1024]{1,0:T(8,128)S(1)} %get-tuple-element.26.centre_ref, ...), custom_call_target="tpu_custom_call" | custom-call | flops 8493465600 | bytes 4194304 | tf_op jit(solution)/shard_map/pair_forces/pallas_call | solution.py:489
  63.4 16.4 %all_to_all.16.in_ref = f32[32,3,12]{2,1,0:T(4,128)S(1)} all-to-all(f32[32,3,12]{2,1,0:T(4,128)S(1)} %get-tuple-element.40), channel_id=1, replica_groups=mesh['gx'=8,'yz'=4] {'gx','yz'}, dimensions={0} | all-to-all | bytes 9216 | tf_op jit(solution)/shard_map/all_to_all | solution.py:534
  79.8 0.8 last.1
  (2 shorter events, 0.0 us)
Async XLA Ops:
  0.6 0.7 copy-start.13
  0.6 0.8 copy-start.4
  0.7 0.7 copy-start.12
  0.7 0.8 copy-start.3
  0.7 0.8 copy-start
  1.4 0.7 copy-start.2
  1.4 0.7 copy-start.1
  1.4 0.7 copy-start.5
  3.5 7.3 %copy-start.8 = (s32[48,128]{1,0:T(8,128)S(1)}, s32[48,128]{1,0:T(8,128)}, u32[]{:S(2)}) copy-start(s32[48,128]{1,0:T(8,128)} %slots_ref.1) | copy-start | bytes 73732
  3.5 14.8 %all-to-all-start = ((f32[32,4,128]{2,1,0:T(4,128)}), f32[32,4,128]{2,1,0:T(4,128)S(1)}, u32[]{:S(2)}, u32[]{:S(2)}) async-start(f32[32,4,128]{2,1,0:T(4,128)} %get-tuple-element.35), calls=%async_computation | async-start | bytes 131072 | tf_op jit(solution)/shard_map/all_to_all | solution.py:534
  10.9 1.4 %copy-start.11 = (bf16[512]{0:T(512)(128)(2,1)S(1)}, bf16[512]{0:T(512)(128)(2,1)}, u32[]{:S(2)}) copy-start(bf16[512]{0:T(512)(128)(2,1)} %param.27) | copy-start | bytes 3076
  10.9 1.4 %copy-start.6 = (bf16[1,576,512]{2,1,0:T(8,128)(2,1)S(1)}, bf16[1,576,512]{2,1,0:T(8,128)(2,1)}, u32[]{:S(2)}) copy-start(bf16[1,576,512]{2,1,0:T(8,128)(2,1)} %param.26) | copy-start | bytes 1769476
  10.9 1.4 %copy-start.7 = (bf16[1,512,64]{1,2,0:T(8,128)(2,1)S(1)}, bf16[1,512,64]{1,2,0:T(8,128)(2,1)}, u32[]{:S(2)}) copy-start(bf16[1,512,64]{1,2,0:T(8,128)(2,1)} %param.25) | copy-start | bytes 196612
  10.9 1.4 %copy-start.9 = (bf16[2,8,512]{2,1,0:T(8,128)(2,1)S(1)}, bf16[2,8,512]{2,1,0:T(8,128)(2,1)}, u32[]{:S(2)}) copy-start(bf16[2,8,512]{2,1,0:T(8,128)(2,1)} %embed_ref.1) | copy-start | bytes 49156
  10.9 1.4 %copy-start.10 = (bf16[8,512]{1,0:T(8,128)(2,1)S(1)}, bf16[8,512]{1,0:T(8,128)(2,1)}, u32[]{:S(2)}) copy-start(bf16[8,512]{1,0:T(8,128)(2,1)} %radial_ref.1) | copy-start | bytes 24580

commit v7 on v6

--- a/solution.py
+++ b/solution.py
@@ -15,7 +15,8 @@
 MASSES = (1.008, 12.011, 14.007, 15.999, 32.06, 22.99, 35.45, 30.97)
 
 LANES = 1024
-TAIL = 640
+TAIL = 768
+GROUP = 256
 LISTED = 2
 DIRECTIONS = ((-1, -1), (-1, 0), (-1, 1), (0, -1), (0, 1), (1, -1), (1, 0), (1, 1))
 TILE = (4, 128)
@@ -387,6 +388,14 @@
         apart = square - mids[:, :width]
         return vec, inside, apart, jnp.exp(-sharp * apart * apart)
 
+    def staggered(width, begin, finish):
+        spans = [slice(at, min(at + GROUP, width)) for at in range(0, width, GROUP)]
+        held = begin(spans[0])
+        for span, later in zip(spans, spans[1:] + [None]):
+            coming = None if later is None else begin(later)
+            finish(span, held)
+            held = coming
+
     def first(block, width):
         hot_j = one_hot(neigh_ref[pl.ds(block, 1), :width], ext_n)
         hot_c = one_hot(centre_ref[pl.ds(block, 1), :width], atom_n)
@@ -396,14 +405,23 @@
         vec, inside, _, basis = geometry(block, width)
         use = jnp.concatenate([hot_c * vec[k : k + 1].astype(BF16) for k in range(3)], axis=0)
         use_s[block, :, :width] = use
-        pre = mm(weight_in, jnp.concatenate([hot, basis.astype(BF16)], axis=0))
-        hidden, slope = silu_pair(pre)
-        slope_s[block, :, :width] = slope.astype(BF16)
-        taken = mm(on_hidden_ref[...], hidden.astype(BF16))
-        part_s[block, :, :width] = taken[:latent]
-        raw = taken[latent : latent + features]
-        raw_s[block, :, :width] = raw
-        energy_s[block, :, :width] = taken[latent + features : latent + features + 8]
+        given = jnp.concatenate([hot, basis.astype(BF16)], axis=0)
+        raws = []
+
+        def begin(span):
+            return mm(weight_in, given[:, span])
+
+        def finish(span, pre):
+            hidden, slope = silu_pair(pre)
+            slope_s[block, :, span] = slope.astype(BF16)
+            taken = mm(on_hidden_ref[...], hidden.astype(BF16))
+            part_s[block, :, span] = taken[:latent]
+            raws.append(taken[latent : latent + features])
+            raw_s[block, :, span] = raws[-1]
+            energy_s[block, :, span] = taken[latent + features : latent + features + 8]
+
+        staggered(width, begin, finish)
+        raw = jnp.concatenate(raws, axis=1)
         c_s[...] += mm_nt((raw * (inside * inside)).astype(BF16), use)
 
     each_block(first)
@@ -415,15 +433,23 @@
         use = use_s[block, :, :width]
         env = inside * inside
         weight = raw_s[block, :, :width] * env
-        inner = weight * mm(c_b, use)
-        later = part_s[block, :, :width] + mm(on_inner_ref[...], inner.astype(BF16))
-        gain, bent = silu_pair(later)
-        readout = jnp.concatenate([readout_ref[...]] * (width // 128), axis=1)
-        energy_s[block, :, :width] += jnp.sum(gain * readout, axis=0, keepdims=True)
-        taken = mm(on_bent_ref[...], bent.astype(BF16))
-        part_s[block, :, :width] = taken[:latent]
-        a_in = taken[latent:] * env
-        ain_s[block, :, :width] = a_in
+        inner = (weight * mm(c_b, use)).astype(BF16)
+        readout = jnp.concatenate([readout_ref[...]] * (GROUP // 128), axis=1)
+        a_ins = []
+
+        def begin(span):
+            return part_s[block, :, span] + mm(on_inner_ref[...], inner[:, span])
+
+        def finish(span, later):
+            gain, bent = silu_pair(later)
+            energy_s[block, :, span] += jnp.sum(gain * readout, axis=0, keepdims=True)
+            taken = mm(on_bent_ref[...], bent.astype(BF16))
+            part_s[block, :, span] = taken[:latent]
+            a_ins.append(taken[latent:] * env[:, span])
+            ain_s[block, :, span] = a_ins[-1]
+
+        staggered(width, begin, finish)
+        a_in = jnp.concatenate(a_ins, axis=1)
         dc_s[...] += mm_nt((a_in * weight).astype(BF16), use)
 
     each_block(second)
@@ -440,13 +466,20 @@
         a_in = ain_s[block, :, :width]
         along = mm(c_dc, use)
         d_weight = a_in * along[:features] + along[features:]
-        d_env = jnp.sum(d_weight * raw, axis=0, keepdims=True) + energy_s[block, :, :width][0:1]
+        d_env = jnp.sum(d_weight * raw, axis=0, keepdims=True) + energy_s[block, 0:1, :width]
         ones = jnp.ones((BASIS_PAD, width), BF16)
-        d_hidden = part_s[block, :, :width] + mm(
-            on_weight_ref[...], jnp.concatenate([d_weight.astype(BF16), ones], axis=0)
-        )
-        d_pre = (d_hidden * slope_s[block, :, :width].astype(F32)).astype(BF16)
-        d_basis = mm(radial_back_ref[...], d_pre)
+        given = jnp.concatenate([d_weight.astype(BF16), ones], axis=0)
+        d_bases = []
+
+        def begin(span):
+            return part_s[block, :, span] + mm(on_weight_ref[...], given[:, span])
+
+        def finish(span, d_hidden):
+            d_pre = (d_hidden * slope_s[block, :, span].astype(F32)).astype(BF16)
+            d_bases.append(mm(radial_back_ref[...], d_pre))
+
+        staggered(width, begin, finish)
+        d_basis = jnp.concatenate(d_bases, axis=1)
         d_square = env * jnp.sum(d_basis * basis * apart, axis=0, keepdims=True) * (-2.0 * sharp)
         d_square = d_square - 2.0 * inside * d_env
         d_all = mm(both, jnp.concatenate([a_in * weight, weight], axis=0).astype(BF16))

time: 81 us -> 83.5 us (1.031)
  blocking collectives: 32.7 us -> 43.1 us
  Pallas kernels: 33.4 us -> 25.4 us
    all_to_all x2, blocking collectives: 32.7 us -> 43.1 us  [exchange(): return lax.all_to_all(blocks, ('gx', 'yz'), 0, 0, tiled=True)]
    pallas_call x2, Pallas kernels: 28.8 us -> 21.1 us  [pair_forces(): pl.pallas_call(functools.partial(force_kernel, second_call=bool(second),...]
  transfers between devices with their start and end apart: 1 -> 1, of which waited for: 1 -> 1; matrix products, arithmetic and copies ran while one was open for 0% -> 0% of each run, Pallas kernels for 3% -> 2%
where the time goes in v7:
time: 83.5 us; the launch traced here: 83.4 us
  blocking collectives  43.1 us (52%)
  Pallas kernels  25.4 us (30%)
  starting transfers between devices  7.3 us (9%)
  waiting for transfers between devices  5.31 us (6%)
  between operations  1.55 us (2%)
    all_to_all x2, blocking collectives, exchange(): return lax.all_to_all(blocks, ('gx', 'yz'), 0, 0, tiled=True)  43.1 us
    pallas_call x2, Pallas kernels, pair_forces(): pl.pallas_call(functools.partial(force_kernel, second_call=bool(second),...  21.1 us
    all_to_all x1, starting transfers between devices, exchange(): return lax.all_to_all(blocks, ('gx', 'yz'), 0, 0, tiled=True)  7.3 us
    all_to_all x1, waiting for transfers between devices, exchange(): return lax.all_to_all(blocks, ('gx', 'yz'), 0, 0, tiled=True)  5.31 us
    pallas_call x2, Pallas kernels, small_call(): pl.pallas_call(kernel, out_shape=out_shape, in_specs=[SMEM] * smem_n + [V...  2.25 us
  transfers between devices with their start and end apart: 1, of which 1 were waited for; matrix products, arithmetic and copies ran while one was open for 0% of the time, Pallas kernels for 2%

profile of v7, /device:TPU:0, one launch (start us, length us, event | category | flops | bytes accessed | tf_op | source)
XLA Modules:
  0.0 83.4 jit_solution(8499789922273055460)
XLA Ops:
  0.6 0.0 copy-start.13
  0.6 0.0 copy-start.4
  0.7 0.0 copy-start.12
  0.7 0.0 copy-start.3
  0.7 0.0 copy-start
  1.4 0.0 copy-done.13
  1.4 0.0 copy-done.12
  1.4 0.0 copy-start.2
  1.4 0.0 copy-start.1
  1.4 0.0 copy-start.5
  1.4 0.0 copy-done.4
  1.5 0.0 copy-done.3
  1.5 0.0 copy-done
  1.5 0.6 copy-done.2
  2.1 0.0 copy-done.1
  2.1 0.0 copy-done.5
  2.1 1.4 %start.1 = (f32[3,48]{1,0:T(4,128)S(1)}, f32[3,48]{1,0:T(4,128)S(1)}, f32[1,48]{1,0:T(1,128)S(1)}, f32[32,4,128]{2,1,0:T(4,128)}) custom-call(s32[8]{0:T(128)S(1)} %fusion.ahead_ref, f32[3,48]{1,0:T(4,128)S(1)} %copy-done.2, f32[3,48]{1,0:T(4,128)S(1)} %copy-done.3, f32[3,48]{1,0:T(4,128)S(1)} %copy-done.4, s32[1,48]{1,0:T(1,128)S(1)} %bitcast.6, ...), custom_call_target="tpu_custom_call" | custom-call | tf_op jit(solution)/shard_map/start/pallas_call | solution.py:549
  3.5 0.0 copy-start.8
  3.5 7.3 %all-to-all-start = ((f32[32,4,128]{2,1,0:T(4,128)}), f32[32,4,128]{2,1,0:T(4,128)S(1)}, u32[]{:S(2)}, u32[]{:S(2)}) async-start(f32[32,4,128]{2,1,0:T(4,128)} %get-tuple-element.35), calls=%async_computation | async-start | bytes 131072 | tf_op jit(solution)/shard_map/all_to_all | solution.py:567
  10.9 0.0 copy-done.8
  10.9 0.0 copy-start.11
  10.9 0.0 copy-start.6
  10.9 0.0 copy-start.7
  10.9 0.0 copy-start.9
  10.9 0.0 copy-start.10
  10.9 1.0 %list_pairs.1 = (s32[6,1024]{1,0:T(8,128)S(1)}, s32[6,1024]{1,0:T(8,128)S(1)}, s32[1]{0:T(128)}) custom-call(f32[1,48]{1,0:T(1,128)S(1)} %get-tuple-element.23.used_ref, s32[48,128]{1,0:T(8,128)S(1)} %copy-done.8), custom_call_target="tpu_custom_call" | custom-call | flops 1000000000 | bytes 65536 | tf_op jit(solution)/shard_map/list_pairs/pallas_call | solution.py:249
  11.9 0.0 copy-done.11
  12.0 0.0 copy-done.6
  12.0 0.0 copy-done.7
  12.0 0.0 copy-done.9
  12.0 0.0 copy-done.10
  12.0 1.0 %prepare_weights.1 = (bf16[512,32]{1,0:T(8,128)(2,1)S(1)}, bf16[592,512]{1,0:T(8,128)(2,1)S(1)}, bf16[512,64]{1,0:T(8,128)(2,1)S(1)}, bf16[576,512]{1,0:T(8,128)...) custom-call(bf16[8,512]{1,0:T(8,128)(2,1)S(1)} %copy-done.10, ...), custom_call_target="tpu_custom_call" | custom-call | flops 1000000000 | bytes 4194304 | tf_op jit(solution)/shard_map/prepare_weights/pallas_call | solution.py:272
  13.0 5.3 %all-to-all-done.in_ref = f32[32,4,128]{2,1,0:T(4,128)S(1)} async-done(((f32[32,4,128]{2,1,0:T(4,128)}), f32[32,4,128]{2,1,0:T(4,128)S(1)}, u32[]{:S(2)}, u32[]{:S(2)}) %all-to-all-start) | async-done | bytes 65568 | tf_op jit(solution)/shard_map/all_to_all | solution.py:567
  18.3 9.6 %pair_forces.2 = f32[32,4,128]{2,1,0:T(4,128)S(1)} custom-call(s32[1]{0:T(128)} %get-tuple-element.24.total_ref, s32[6,1024]{1,0:T(8,128)S(1)} %get-tuple-element.25.neigh_ref, s32[6,1024]{1,0:T(8,128)S(1)} %get-tuple-element.26.centre_ref, f32[3,48]{1,0:T(4,128)S(1)} %get-tuple-element.27.moved_ref, s32[1,48]{1,0:T(1,128)S(1)} %bitcast.7, ...), custom_call_target="tpu_custom_call" | custom-call | flops 8493465600 | bytes 4194304 | tf_op jit(solution)/shard_map/pair_forces/pallas_call | solution.py:522
  28.0 21.5 %all_to_all.15.refs_2_ = f32[32,4,128]{2,1,0:T(4,128)S(1)} all-to-all(f32[32,4,128]{2,1,0:T(4,128)S(1)} %pair_forces.2), channel_id=1, replica_groups=mesh['gx'=8,'yz'=4] {'gx','yz'}, dimensions={0} | all-to-all | bytes 131072 | tf_op jit(solution)/shard_map/all_to_all | solution.py:567
  49.5 11.5 %pair_forces.3 = (f32[3,48]{1,0:T(4,128)S(1)}, f32[3,48]{1,0:T(4,128)}, f32[3,48]{1,0:T(4,128)S(1)}, f32[32,3,12]{2,1,0:T(4,128)S(1)}) custom-call(s32[1]{0:T(128)} %get-tuple-element.24.total_ref, s32[6,1024]{1,0:T(8,128)S(1)} %get-tuple-element.25.neigh_ref, s32[6,1024]{1,0:T(8,128)S(1)} %get-tuple-element.26.centre_ref, ...), custom_call_target="tpu_custom_call" | custom-call | flops 8493465600 | bytes 4194304 | tf_op jit(solution)/shard_map/pair_forces/pallas_call | solution.py:522
  61.0 21.6 %all_to_all.16.in_ref = f32[32,3,12]{2,1,0:T(4,128)S(1)} all-to-all(f32[32,3,12]{2,1,0:T(4,128)S(1)} %get-tuple-element.40), channel_id=1, replica_groups=mesh['gx'=8,'yz'=4] {'gx','yz'}, dimensions={0} | all-to-all | bytes 9216 | tf_op jit(solution)/shard_map/all_to_all | solution.py:567
  82.6 0.8 last.1
  (2 shorter events, 0.0 us)
Async XLA Ops:
  0.6 0.7 copy-start.13
  0.6 0.8 copy-start.4
  0.7 0.7 copy-start.12
  0.7 0.8 copy-start.3
  0.7 0.8 copy-start
  1.4 0.7 copy-start.2
  1.4 0.7 copy-start.1
  1.4 0.7 copy-start.5
  3.5 7.3 %copy-start.8 = (s32[48,128]{1,0:T(8,128)S(1)}, s32[48,128]{1,0:T(8,128)}, u32[]{:S(2)}) copy-start(s32[48,128]{1,0:T(8,128)} %slots_ref.1) | copy-start | bytes 73732
  3.5 14.8 %all-to-all-start = ((f32[32,4,128]{2,1,0:T(4,128)}), f32[32,4,128]{2,1,0:T(4,128)S(1)}, u32[]{:S(2)}, u32[]{:S(2)}) async-start(f32[32,4,128]{2,1,0:T(4,128)} %get-tuple-element.35), calls=%async_computation | async-start | bytes 131072 | tf_op jit(solution)/shard_map/all_to_all | solution.py:567
  10.9 1.1 %copy-start.11 = (bf16[512]{0:T(512)(128)(2,1)S(1)}, bf16[512]{0:T(512)(128)(2,1)}, u32[]{:S(2)}) copy-start(bf16[512]{0:T(512)(128)(2,1)} %param.27) | copy-start | bytes 3076
  10.9 1.1 %copy-start.6 = (bf16[1,576,512]{2,1,0:T(8,128)(2,1)S(1)}, bf16[1,576,512]{2,1,0:T(8,128)(2,1)}, u32[]{:S(2)}) copy-start(bf16[1,576,512]{2,1,0:T(8,128)(2,1)} %param.26) | copy-start | bytes 1769476
  10.9 1.1 %copy-start.7 = (bf16[1,512,64]{1,2,0:T(8,128)(2,1)S(1)}, bf16[1,512,64]{1,2,0:T(8,128)(2,1)}, u32[]{:S(2)}) copy-start(bf16[1,512,64]{1,2,0:T(8,128)(2,1)} %param.25) | copy-start | bytes 196612
  10.9 1.1 %copy-start.9 = (bf16[2,8,512]{2,1,0:T(8,128)(2,1)S(1)}, bf16[2,8,512]{2,1,0:T(8,128)(2,1)}, u32[]{:S(2)}) copy-start(bf16[2,8,512]{2,1,0:T(8,128)(2,1)} %embed_ref.1) | copy-start | bytes 49156
  10.9 1.1 %copy-start.10 = (bf16[8,512]{1,0:T(8,128)(2,1)S(1)}, bf16[8,512]{1,0:T(8,128)(2,1)}, u32[]{:S(2)}) copy-start(bf16[8,512]{1,0:T(8,128)(2,1)} %radial_ref.1) | copy-start | bytes 24580

commit v8 on v6

--- a/solution.py
+++ b/solution.py
@@ -15,7 +15,7 @@
 MASSES = (1.008, 12.011, 14.007, 15.999, 32.06, 22.99, 35.45, 30.97)
 
 LANES = 1024
-TAIL = 640
+TAIL = 768
 LISTED = 2
 DIRECTIONS = ((-1, -1), (-1, 0), (-1, 1), (0, -1), (0, 1), (1, -1), (1, 0), (1, 1))
 TILE = (4, 128)
@@ -39,6 +39,20 @@
     mid = rest.astype(BF16)
     low = (rest - mid.astype(F32)).astype(BF16)
     return jnp.concatenate([high.astype(F32), mid.astype(F32), low.astype(F32)], axis=0).astype(BF16)
+
+
+def lane_table(values):
+    rows, lanes = values.shape
+    return jnp.concatenate([values, jnp.zeros((rows, 128 - lanes), F32)], axis=1)
+
+
+def look_up(table, ids):
+    inside = jnp.minimum(jnp.maximum(ids, 0), 127)
+    found = []
+    for at in range(0, ids.shape[1], 128):
+        index = jnp.broadcast_to(inside[:, at : at + 128], table.shape)
+        found.append(jnp.take_along_axis(table, index, axis=1, mode="promise_in_bounds"))
+    return jnp.concatenate(found, axis=1)
 
 
 def one_hot(ids, rows):
@@ -320,34 +334,34 @@
     ghost_kind = ghosts[3:4].astype(jnp.int32)
     if second_call:
         half_ref, send_ref, all_ref, half_two_ref, end_ref, own_out_ref, out_ref = refs
-        on_ghosts = []
+        sends, wholes = [], []
         for k, (a, b) in enumerate(DIRECTIONS):
-            sends = jnp.concatenate(
-                [from_owners[k][:, n * ghost_n : (n + 1) * ghost_n] for n in (2, 3)], axis=0
-            ).astype(jnp.int32)
-            whole = domain_force(all_ref, -a, -b, sends, atom_n)
-            picked = mm(split3(padded_rows(whole, 8)), one_hot(sends[k : k + 1], atom_n))
-            on_ghosts.append(sum_parts(picked)[0:3])
+            rows = [from_owners[k][:, n * ghost_n : (n + 1) * ghost_n] for n in (2, 3)]
+            sends.append(jnp.concatenate(rows, axis=0).astype(jnp.int32))
+            wholes.append(domain_force(all_ref, -a, -b, sends[k], atom_n))
+        own_whole = domain_force(all_ref, 0, 0, send_ref[...], atom_n)
+        on_ghosts = [
+            sum_parts(mm(split3(padded_rows(whole, 8)), one_hot(sends[k][k : k + 1], atom_n)))[0:3]
+            for k, whole in enumerate(wholes)
+        ]
         _, ghost_pos = step_on(
             ghosts[0:3], ghosts[4:7], ghost_kind, jnp.concatenate(on_ghosts, axis=1)
         )
-        whole = domain_force(all_ref, 0, 0, send_ref[...], atom_n)
-        half_two, own_pos = step_on(moved_ref[...], half_ref[...], own_kind, whole)
+        half_two, own_pos = step_on(moved_ref[...], half_ref[...], own_kind, own_whole)
         half_two_ref[...] = half_two
         end_ref[...] = own_pos
     else:
         (out_ref,) = refs
         own_pos, ghost_pos = moved_ref[...], ghosts[0:3]
     kind = jnp.concatenate([own_kind, ghost_kind], axis=1)
-    pos = jnp.concatenate([own_pos, ghost_pos], axis=1)
     basis_n = SPECIES
     latent, features = on_inner_ref.shape
     total = total_ref[0]
     full = (total + lanes - 1 - TAIL) // lanes
     scale = COUPLING * SLOTS ** (-0.5)
 
-    pos8 = padded_rows(pos, 8) * (1.0 / RADIUS)
-    pos_parts = split3(jnp.concatenate([pos8, -pos8[:, :atom_n]], axis=1))
+    own_table = lane_table(padded_rows(own_pos, 8) * (1.0 / RADIUS))
+    ghost_table = lane_table(padded_rows(ghost_pos, 8) * (1.0 / RADIUS))
     row8 = lax.broadcasted_iota(jnp.int32, (SPECIES, ext_n), 0)
     kinds = jnp.where(row8 == kind, 1.0, 0.0)
     basis_in = identity(BASIS_PAD).astype(F32)
@@ -388,11 +402,15 @@
         return vec, inside, apart, jnp.exp(-sharp * apart * apart)
 
     def first(block, width):
-        hot_j = one_hot(neigh_ref[pl.ds(block, 1), :width], ext_n)
-        hot_c = one_hot(centre_ref[pl.ds(block, 1), :width], atom_n)
-        hot = jnp.concatenate([hot_j, hot_c], axis=0)
+        neigh = neigh_ref[pl.ds(block, 1), :width]
+        centre = centre_ref[pl.ds(block, 1), :width]
+        hot_c = one_hot(centre, atom_n)
+        hot = jnp.concatenate([one_hot(neigh, ext_n), hot_c], axis=0)
         hot_s[block, :, :width] = hot
-        u_s[block, :, :width] = sum_parts(mm(pos_parts, hot))
+        there = jnp.where(
+            neigh < atom_n, look_up(own_table, neigh), look_up(ghost_table, neigh - atom_n)
+        )
+        u_s[block, :, :width] = there - look_up(own_table, centre)
         vec, inside, _, basis = geometry(block, width)
         use = jnp.concatenate([hot_c * vec[k : k + 1].astype(BF16) for k in range(3)], axis=0)
         use_s[block, :, :width] = use

time: 81 us -> 80.7 us (level); the launches traced: 80.6 us -> 81.8 us
  Pallas kernels: 33.4 us -> 49.2 us
  blocking collectives: 32.7 us -> 18.4 us
    pallas_call x2, Pallas kernels: 28.8 us -> 44.2 us  [pair_forces(): pl.pallas_call(functools.partial(force_kernel, second_call=bool(second),...]
    all_to_all x2, blocking collectives: 32.7 us -> 18.4 us  [exchange(): return lax.all_to_all(blocks, ('gx', 'yz'), 0, 0, tiled=True)]
where the time goes in v8:
time: 80.7 us; the launch traced here: 81.8 us
  Pallas kernels  49.2 us (61%)
  blocking collectives  18.4 us (23%)
  starting transfers between devices  7.3 us (9%)
  waiting for transfers between devices  4.61 us (6%)
  between operations  1.55 us (2%)
    pallas_call x2, Pallas kernels, pair_forces(): pl.pallas_call(functools.partial(force_kernel, second_call=bool(second),...  44.2 us
    all_to_all x2, blocking collectives, exchange(): return lax.all_to_all(blocks, ('gx', 'yz'), 0, 0, tiled=True)  18.4 us
    all_to_all x1, starting transfers between devices, exchange(): return lax.all_to_all(blocks, ('gx', 'yz'), 0, 0, tiled=True)  7.3 us
    all_to_all x1, waiting for transfers between devices, exchange(): return lax.all_to_all(blocks, ('gx', 'yz'), 0, 0, tiled=True)  4.61 us
    pallas_call x2, Pallas kernels, small_call(): pl.pallas_call(kernel, out_shape=out_shape, in_specs=[SMEM] * smem_n + [V...  2.25 us
    pallas_call x1, Pallas kernels, list_pairs(): pl.pallas_call(list_kernel, out_shape=[pairs, pairs, jax.ShapeDtypeStruct...  1.71 us
  transfers between devices with their start and end apart: 1, of which 1 were waited for; matrix products, arithmetic and copies ran while one was open for 0% of the time, Pallas kernels for 3%

profile of v8, /device:TPU:0, one launch (start us, length us, event | category | flops | bytes accessed | tf_op | source)
XLA Modules:
  0.0 81.8 jit_solution(6967149826994536036)
XLA Ops:
  0.6 0.0 copy-start.13
  0.6 0.0 copy-start.4
  0.7 0.0 copy-start.12
  0.7 0.0 copy-start.3
  0.7 0.0 copy-start
  1.4 0.0 copy-done.13
  1.4 0.0 copy-done.12
  1.4 0.0 copy-start.2
  1.4 0.0 copy-start.1
  1.4 0.0 copy-start.5
  1.4 0.0 copy-done.4
  1.5 0.0 copy-done.3
  1.5 0.0 copy-done
  1.5 0.6 copy-done.2
  2.1 0.0 copy-done.1
  2.1 0.0 copy-done.5
  2.1 1.4 %start.1 = (f32[3,48]{1,0:T(4,128)S(1)}, f32[3,48]{1,0:T(4,128)S(1)}, f32[1,48]{1,0:T(1,128)S(1)}, f32[32,4,128]{2,1,0:T(4,128)}) custom-call(s32[8]{0:T(128)S(1)} %fusion.ahead_ref, f32[3,48]{1,0:T(4,128)S(1)} %copy-done.2, f32[3,48]{1,0:T(4,128)S(1)} %copy-done.3, f32[3,48]{1,0:T(4,128)S(1)} %copy-done.4, s32[1,48]{1,0:T(1,128)S(1)} %bitcast.6, ...), custom_call_target="tpu_custom_call" | custom-call | tf_op jit(solution)/shard_map/start/pallas_call | solution.py:534
  3.5 0.0 copy-start.8
  3.5 7.3 %all-to-all-start = ((f32[32,4,128]{2,1,0:T(4,128)}), f32[32,4,128]{2,1,0:T(4,128)S(1)}, u32[]{:S(2)}, u32[]{:S(2)}) async-start(f32[32,4,128]{2,1,0:T(4,128)} %get-tuple-element.35), calls=%async_computation | async-start | bytes 131072 | tf_op jit(solution)/shard_map/all_to_all | solution.py:552
  10.9 0.0 copy-done.8
  10.9 0.0 copy-start.11
  10.9 0.0 copy-start.6
  10.9 0.0 copy-start.7
  10.9 0.0 copy-start.9
  10.9 0.0 copy-start.10
  10.9 1.7 %list_pairs.1 = (s32[6,1024]{1,0:T(8,128)S(1)}, s32[6,1024]{1,0:T(8,128)S(1)}, s32[1]{0:T(128)}) custom-call(f32[1,48]{1,0:T(1,128)S(1)} %get-tuple-element.23.used_ref, s32[48,128]{1,0:T(8,128)S(1)} %copy-done.8), custom_call_target="tpu_custom_call" | custom-call | flops 1000000000 | bytes 65536 | tf_op jit(solution)/shard_map/list_pairs/pallas_call | solution.py:262
  12.6 0.0 copy-done.11
  12.7 0.0 copy-done.6
  12.7 0.0 copy-done.7
  12.7 0.0 copy-done.9
  12.7 0.0 copy-done.10
  12.7 1.0 %prepare_weights.1 = (bf16[512,32]{1,0:T(8,128)(2,1)S(1)}, bf16[592,512]{1,0:T(8,128)(2,1)S(1)}, bf16[512,64]{1,0:T(8,128)(2,1)S(1)}, bf16[576,512]{1,0:T(8,128)...) custom-call(bf16[8,512]{1,0:T(8,128)(2,1)S(1)} %copy-done.10, ...), custom_call_target="tpu_custom_call" | custom-call | flops 1000000000 | bytes 4194304 | tf_op jit(solution)/shard_map/prepare_weights/pallas_call | solution.py:285
  13.7 4.6 %all-to-all-done.in_ref = f32[32,4,128]{2,1,0:T(4,128)S(1)} async-done(((f32[32,4,128]{2,1,0:T(4,128)}), f32[32,4,128]{2,1,0:T(4,128)S(1)}, u32[]{:S(2)}, u32[]{:S(2)}) %all-to-all-start) | async-done | bytes 65568 | tf_op jit(solution)/shard_map/all_to_all | solution.py:552
  18.3 21.6 %pair_forces.2 = f32[32,4,128]{2,1,0:T(4,128)S(1)} custom-call(s32[1]{0:T(128)} %get-tuple-element.24.total_ref, s32[6,1024]{1,0:T(8,128)S(1)} %get-tuple-element.25.neigh_ref, s32[6,1024]{1,0:T(8,128)S(1)} %get-tuple-element.26.centre_ref, f32[3,48]{1,0:T(4,128)S(1)} %get-tuple-element.27.moved_ref, s32[1,48]{1,0:T(1,128)S(1)} %bitcast.7, ...), custom_call_target="tpu_custom_call" | custom-call | flops 8493465600 | bytes 4194304 | tf_op jit(solution)/shard_map/pair_forces/pallas_call | solution.py:507
  40.0 9.2 %all_to_all.15.refs_2_ = f32[32,4,128]{2,1,0:T(4,128)S(1)} all-to-all(f32[32,4,128]{2,1,0:T(4,128)S(1)} %pair_forces.2), channel_id=1, replica_groups=mesh['gx'=8,'yz'=4] {'gx','yz'}, dimensions={0} | all-to-all | bytes 131072 | tf_op jit(solution)/shard_map/all_to_all | solution.py:552
  49.2 22.6 %pair_forces.3 = (f32[3,48]{1,0:T(4,128)S(1)}, f32[3,48]{1,0:T(4,128)}, f32[3,48]{1,0:T(4,128)S(1)}, f32[32,3,12]{2,1,0:T(4,128)S(1)}) custom-call(s32[1]{0:T(128)} %get-tuple-element.24.total_ref, s32[6,1024]{1,0:T(8,128)S(1)} %get-tuple-element.25.neigh_ref, s32[6,1024]{1,0:T(8,128)S(1)} %get-tuple-element.26.centre_ref, ...), custom_call_target="tpu_custom_call" | custom-call | flops 8493465600 | bytes 4194304 | tf_op jit(solution)/shard_map/pair_forces/pallas_call | solution.py:507
  71.8 9.2 %all_to_all.16.in_ref = f32[32,3,12]{2,1,0:T(4,128)S(1)} all-to-all(f32[32,3,12]{2,1,0:T(4,128)S(1)} %get-tuple-element.40), channel_id=1, replica_groups=mesh['gx'=8,'yz'=4] {'gx','yz'}, dimensions={0} | all-to-all | bytes 9216 | tf_op jit(solution)/shard_map/all_to_all | solution.py:552
  80.9 0.8 last.1
  (2 shorter events, 0.0 us)
Async XLA Ops:
  0.6 0.7 copy-start.13
  0.6 0.8 copy-start.4
  0.7 0.7 copy-start.12
  0.7 0.8 copy-start.3
  0.7 0.8 copy-start
  1.4 0.7 copy-start.2
  1.4 0.7 copy-start.1
  1.4 0.7 copy-start.5
  3.5 7.3 %copy-start.8 = (s32[48,128]{1,0:T(8,128)S(1)}, s32[48,128]{1,0:T(8,128)}, u32[]{:S(2)}) copy-start(s32[48,128]{1,0:T(8,128)} %slots_ref.1) | copy-start | bytes 73732
  3.5 14.8 %all-to-all-start = ((f32[32,4,128]{2,1,0:T(4,128)}), f32[32,4,128]{2,1,0:T(4,128)S(1)}, u32[]{:S(2)}, u32[]{:S(2)}) async-start(f32[32,4,128]{2,1,0:T(4,128)} %get-tuple-element.35), calls=%async_computation | async-start | bytes 131072 | tf_op jit(solution)/shard_map/all_to_all | solution.py:552
  10.9 1.8 %copy-start.11 = (bf16[512]{0:T(512)(128)(2,1)S(1)}, bf16[512]{0:T(512)(128)(2,1)}, u32[]{:S(2)}) copy-start(bf16[512]{0:T(512)(128)(2,1)} %param.27) | copy-start | bytes 3076
  10.9 1.8 %copy-start.6 = (bf16[1,576,512]{2,1,0:T(8,128)(2,1)S(1)}, bf16[1,576,512]{2,1,0:T(8,128)(2,1)}, u32[]{:S(2)}) copy-start(bf16[1,576,512]{2,1,0:T(8,128)(2,1)} %param.26) | copy-start | bytes 1769476
  10.9 1.8 %copy-start.7 = (bf16[1,512,64]{1,2,0:T(8,128)(2,1)S(1)}, bf16[1,512,64]{1,2,0:T(8,128)(2,1)}, u32[]{:S(2)}) copy-start(bf16[1,512,64]{1,2,0:T(8,128)(2,1)} %param.25) | copy-start | bytes 196612
  10.9 1.8 %copy-start.9 = (bf16[2,8,512]{2,1,0:T(8,128)(2,1)S(1)}, bf16[2,8,512]{2,1,0:T(8,128)(2,1)}, u32[]{:S(2)}) copy-start(bf16[2,8,512]{2,1,0:T(8,128)(2,1)} %embed_ref.1) | copy-start | bytes 49156
  10.9 1.8 %copy-start.10 = (bf16[8,512]{1,0:T(8,128)(2,1)S(1)}, bf16[8,512]{1,0:T(8,128)(2,1)}, u32[]{:S(2)}) copy-start(bf16[8,512]{1,0:T(8,128)(2,1)} %radial_ref.1) | copy-start | bytes 24580

commit v9 on v8

--- a/solution.py
+++ b/solution.py
@@ -60,7 +60,6 @@
     return jnp.where(row_ids == ids, 1.0, 0.0).astype(BF16)
 
 
-SMEM = pl.BlockSpec(memory_space=pltpu.SMEM)
 VMEM = pl.BlockSpec(memory_space=pltpu.VMEM)
 
 
@@ -115,7 +114,7 @@
 
 
 def start_kernel(
-    ahead_ref,
+    _,
     pos_ref,
     vel_ref,
     force_ref,
@@ -143,9 +142,9 @@
     ghost_n = sent.shape[1]
     rest = jnp.zeros((TILE[0], TILE[1] - 4 * ghost_n), F32)
     out_ref[...] = jnp.zeros_like(out_ref)
-    for k in range(len(DIRECTIONS)):
+    for k, place in enumerate(towards(1)):
         block = picked[:, k * ghost_n : (k + 1) * ghost_n]
-        out_ref[ahead_ref[k]] = jnp.concatenate([block[:4], block[4:], sent[:4], sent[4:], rest], axis=1)
+        out_ref[place] = jnp.concatenate([block[:4], block[4:], sent[:4], sent[4:], rest], axis=1)
 
 
 def total_force(own, back, sends):
@@ -220,7 +219,7 @@
     into_ref[...] = mm_nt(eye, into).astype(BF16)
 
 
-def list_kernel(used_ref, slots_ref, neigh_ref, centre_ref, total_ref):
+def list_kernel(used_ref, slots_ref, neigh_ref, centre_ref):
     atom_n, slot_n = slots_ref.shape
     blocks, lanes = neigh_ref.shape
     slots_t = mm_nt(identity(slot_n), slots_ref[...].astype(F32).astype(BF16)).astype(BF16)
@@ -230,7 +229,6 @@
     end = jnp.sum(jnp.where(col_i <= row_i, used, 0.0), axis=1, keepdims=True)
     own = jnp.sum(jnp.where(col_i == row_i, used, 0.0), axis=1, keepdims=True)
     total = jnp.sum(used)
-    total_ref[0] = total.astype(jnp.int32)
     lane = lax.broadcasted_iota(jnp.int32, (1, lanes), 1)
 
     def one_block(block):
@@ -261,9 +259,9 @@
     pairs = jax.ShapeDtypeStruct((blocks, LANES), jnp.int32)
     return pl.pallas_call(
         list_kernel,
-        out_shape=[pairs, pairs, jax.ShapeDtypeStruct((1,), jnp.int32)],
+        out_shape=[pairs, pairs],
         in_specs=[VMEM] * 2,
-        out_specs=[VMEM, VMEM, SMEM],
+        out_specs=[VMEM] * 2,
         compiler_params=pltpu.CompilerParams(vmem_limit_bytes=16 * 2**20),
         cost_estimate=pl.CostEstimate(flops=10**9, bytes_accessed=2**16, transcendentals=0),
         name="list_pairs",
@@ -300,7 +298,7 @@
 
 
 def force_kernel(
-    total_ref,
+    used_ref,
     neigh_ref,
     centre_ref,
     moved_ref,
@@ -356,7 +354,7 @@
     kind = jnp.concatenate([own_kind, ghost_kind], axis=1)
     basis_n = SPECIES
     latent, features = on_inner_ref.shape
-    total = total_ref[0]
+    total = jnp.sum(used_ref[...]).astype(jnp.int32)
     full = (total + lanes - 1 - TAIL) // lanes
     scale = COUPLING * SLOTS ** (-0.5)
 
@@ -457,6 +455,12 @@
         weight = raw * env
         a_in = ain_s[block, :, :width]
         along = mm(c_dc, use)
+        d_all = mm(both, jnp.concatenate([a_in * weight, weight], axis=0).astype(BF16))
+        hot_c = hot[ext_n:].astype(F32)
+        picked = [
+            jnp.sum(d_all[k * atom_n : (k + 1) * atom_n] * hot_c, axis=0, keepdims=True)
+            for k in range(3)
+        ]
         d_weight = a_in * along[:features] + along[features:]
         d_env = jnp.sum(d_weight * raw, axis=0, keepdims=True) + energy_s[block, :, :width][0:1]
         ones = jnp.ones((BASIS_PAD, width), BF16)
@@ -467,12 +471,6 @@
         d_basis = mm(radial_back_ref[...], d_pre)
         d_square = env * jnp.sum(d_basis * basis * apart, axis=0, keepdims=True) * (-2.0 * sharp)
         d_square = d_square - 2.0 * inside * d_env
-        d_all = mm(both, jnp.concatenate([a_in * weight, weight], axis=0).astype(BF16))
-        hot_c = hot[ext_n:].astype(F32)
-        picked = [
-            jnp.sum(d_all[k * atom_n : (k + 1) * atom_n] * hot_c, axis=0, keepdims=True)
-            for k in range(3)
-        ]
         d_vec = jnp.concatenate(picked + [jnp.zeros((5, width), F32)], axis=0)
         d_vec = (d_vec + 2.0 * d_square * vec) * (1.0 / RADIUS)
         f_s[...] += mm_nt(split3(d_vec), hot)
@@ -491,13 +489,13 @@
 
 
 def pair_forces(pairs, own_pos, own_kind, weights, incoming, ghost_n, second=()):
-    neigh, centre, total = pairs
+    used, neigh, centre = pairs
     blocks, lanes = neigh.shape
     latent, features = weights[2].shape
     atom_n = own_pos.shape[1]
     devices = incoming.shape[0]
     ext_n = atom_n + ghost_n * len(DIRECTIONS)
-    operands = [total, neigh, centre, own_pos, own_kind, *weights, incoming, *second]
+    operands = [used, neigh, centre, own_pos, own_kind, *weights, incoming, *second]
     if second:
         out_shape = [jax.ShapeDtypeStruct((3, atom_n), F32)] * 3
         out_shape.append(jax.ShapeDtypeStruct((devices, 3, ghost_n), F32))
@@ -507,7 +505,7 @@
     return pl.pallas_call(
         functools.partial(force_kernel, second_call=bool(second), out_ghost_n=ghost_n),
         out_shape=out_shape,
-        in_specs=[SMEM] + [VMEM] * (len(operands) - 1),
+        in_specs=[VMEM] * len(operands),
         out_specs=[VMEM] * len(out_shape),
         scratch_shapes=[
             pltpu.VMEM((blocks, ext_n + atom_n, lanes), BF16),
@@ -530,11 +528,11 @@
     )(*operands)
 
 
-def small_call(kernel, name, operands, out_shape, smem_n=0):
+def small_call(kernel, name, operands, out_shape):
     return pl.pallas_call(
         kernel,
         out_shape=out_shape,
-        in_specs=[SMEM] * smem_n + [VMEM] * (len(operands) - smem_n),
+        in_specs=[VMEM] * len(operands),
         out_specs=[VMEM] * len(out_shape),
         compiler_params=pltpu.CompilerParams(vmem_limit_bytes=16 * 2**20),
         name=name,
@@ -578,7 +576,7 @@
         start_kernel,
         "start",
         [
-            ahead,
+            ahead[None, :],
             positions,
             velocities,
             forces_start,
@@ -588,10 +586,9 @@
             send_list,
         ],
         [atoms, atoms, jax.ShapeDtypeStruct((1, atom_n), F32), jax.ShapeDtypeStruct((devices, *TILE), F32)],
-        smem_n=1,
     )
     got = exchange(sent)
-    pairs = list_pairs(used, neighbours)
+    pairs = (used, *list_pairs(used, neighbours))
     weights = prepare_weights(radial_weight, species_embed, env_weight, latent_weight, readout)
     (sent,) = pair_forces(pairs, moved, kinds, weights, got, ghost_n)
     every = exchange(sent)

time: 80.7 us -> 80 us (level)
  Pallas kernels: 49.2 us -> 30.8 us
  blocking collectives: 18.4 us -> 34.5 us
    pallas_call x2, Pallas kernels: 44.2 us -> 27.2 us  [pair_forces(): pl.pallas_call(functools.partial(force_kernel, second_call=bool(second),...]
    all_to_all x2, blocking collectives: 18.4 us -> 34.5 us  [exchange(): return lax.all_to_all(blocks, ('gx', 'yz'), 0, 0, tiled=True)]
    pallas_call x3, Pallas kernels: 3.96 us -> 2.56 us  [the longest x2 1.71 us: small_call(): pl.pallas_call(kernel, out_shape=out_shape, in_specs=[VMEM] * len(operand...]
  transfers between devices with their start and end apart: 1 -> 1, of which waited for: 1 -> 1; matrix products, arithmetic and copies ran while one was open for 0% -> 0% of each run, Pallas kernels for 3% -> 2%
where the time goes in v9:
time: 80 us; the launch traced here: 80.3 us
  blocking collectives  34.5 us (43%)
  Pallas kernels  30.8 us (38%)
  starting transfers between devices  7.3 us (9%)
  waiting for transfers between devices  5.37 us (7%)
  between operations  1.52 us (2%)
  local copies, waits for them, and re-layouts  0.85 us (1%)
    all_to_all x2, blocking collectives, exchange(): return lax.all_to_all(blocks, ('gx', 'yz'), 0, 0, tiled=True)  34.5 us
    pallas_call x2, Pallas kernels, pair_forces(): pl.pallas_call(functools.partial(force_kernel, second_call=bool(second),...  27.2 us
    all_to_all x1, starting transfers between devices, exchange(): return lax.all_to_all(blocks, ('gx', 'yz'), 0, 0, tiled=True)  7.3 us
    all_to_all x1, waiting for transfers between devices, exchange(): return lax.all_to_all(blocks, ('gx', 'yz'), 0, 0, tiled=True)  5.37 us
    pallas_call x2, Pallas kernels, small_call(): pl.pallas_call(kernel, out_shape=out_shape, in_specs=[VMEM] * len(operand...  1.71 us
  transfers between devices with their start and end apart: 1, of which 1 were waited for; matrix products, arithmetic and copies ran while one was open for 0% of the time, Pallas kernels for 2%

profile of v9, /device:TPU:0, one launch (start us, length us, event | category | flops | bytes accessed | tf_op | source)
XLA Modules:
  0.0 80.3 jit_solution(13034328770297531337)
XLA Ops:
  0.6 0.0 copy-start.13
  0.6 0.0 copy-start.4
  0.7 0.0 copy-start.12
  0.7 0.0 copy-start.3
  0.7 0.0 copy-start
  1.4 0.0 copy-done.13
  1.4 0.0 copy-done.12
  1.4 0.0 copy-start.2
  1.4 0.0 copy-start.1
  1.4 0.0 copy-start.5
  1.4 0.0 copy-done.4
  1.5 0.0 copy-done.3
  1.5 0.0 copy-done
  1.5 0.6 copy-done.2
  2.1 0.0 copy-done.1
  2.1 0.0 copy-done.5
  2.1 0.9 %start.1 = (f32[3,48]{1,0:T(4,128)S(1)}, f32[3,48]{1,0:T(4,128)S(1)}, f32[1,48]{1,0:T(1,128)S(1)}, f32[32,4,128]{2,1,0:T(4,128)}) custom-call(s32[1,8]{1,0:T(1,128)S(1)} %fusion.4._, f32[3,48]{1,0:T(4,128)S(1)} %copy-done.2, f32[3,48]{1,0:T(4,128)S(1)} %copy-done.3, f32[3,48]{1,0:T(4,128)S(1)} %copy-done.4, s32[1,48]{1,0:T(1,128)S(1)} %bitcast.8, ...), custom_call_target="tpu_custom_call" | custom-call | tf_op jit(solution)/shard_map/start/pallas_call | solution.py:532
  3.0 0.0 copy-start.8
  3.0 7.3 %all-to-all-start = ((f32[32,4,128]{2,1,0:T(4,128)}), f32[32,4,128]{2,1,0:T(4,128)S(1)}, u32[]{:S(2)}, u32[]{:S(2)}) async-start(f32[32,4,128]{2,1,0:T(4,128)} %get-tuple-element.33), calls=%async_computation | async-start | bytes 131072 | tf_op jit(solution)/shard_map/all_to_all | solution.py:550
  10.3 0.0 copy-done.8
  10.3 0.0 copy-start.11
  10.3 0.0 copy-start.6
  10.4 0.0 copy-start.7
  10.4 0.0 copy-start.9
  10.4 0.0 copy-start.10
  10.4 0.8 %list_pairs.1 = (s32[6,1024]{1,0:T(8,128)S(1)}, s32[6,1024]{1,0:T(8,128)S(1)}) custom-call(f32[1,48]{1,0:T(1,128)S(1)} %get-tuple-element.22.used_ref, s32[48,128]{1,0:T(8,128)S(1)} %copy-done.8), custom_call_target="tpu_custom_call" | custom-call | flops 1000000000 | bytes 65536 | tf_op jit(solution)/shard_map/list_pairs/pallas_call | solution.py:260
  11.2 0.0 copy-done.11
  11.3 0.2 copy-done.6
  11.4 0.0 copy-done.7
  11.4 0.0 copy-done.9
  11.4 0.0 copy-done.10
  11.4 1.0 %prepare_weights.1 = (bf16[512,32]{1,0:T(8,128)(2,1)S(1)}, bf16[592,512]{1,0:T(8,128)(2,1)S(1)}, bf16[512,64]{1,0:T(8,128)(2,1)S(1)}, bf16[576,512]{1,0:T(8,128)...) custom-call(bf16[8,512]{1,0:T(8,128)(2,1)S(1)} %copy-done.10, ...), custom_call_target="tpu_custom_call" | custom-call | flops 1000000000 | bytes 4194304 | tf_op jit(solution)/shard_map/prepare_weights/pallas_call | solution.py:283
  12.4 5.4 %all-to-all-done.in_ref = f32[32,4,128]{2,1,0:T(4,128)S(1)} async-done(((f32[32,4,128]{2,1,0:T(4,128)}), f32[32,4,128]{2,1,0:T(4,128)S(1)}, u32[]{:S(2)}, u32[]{:S(2)}) %all-to-all-start) | async-done | bytes 65568 | tf_op jit(solution)/shard_map/all_to_all | solution.py:550
  17.8 13.2 %pair_forces.2 = f32[32,4,128]{2,1,0:T(4,128)S(1)} custom-call(f32[1,48]{1,0:T(1,128)S(1)} %get-tuple-element.22.used_ref, s32[6,1024]{1,0:T(8,128)S(1)} %get-tuple-element.23.neigh_ref, s32[6,1024]{1,0:T(8,128)S(1)} %get-tuple-element.24.centre_ref, f32[3,48]{1,0:T(4,128)S(1)} %get-tuple-element.25.moved_ref, s32[1,48]{1,0:T(1,128)S(1)} %bitcast.9, ...), custom_call_target="tpu_custom_call" | custom-call | flops 8493465600 | bytes 4194304 | tf_op jit(solution)/shard_map/pair_forces/pallas_call | solution.py:505
  31.0 17.2 %all_to_all.15.refs_2_ = f32[32,4,128]{2,1,0:T(4,128)S(1)} all-to-all(f32[32,4,128]{2,1,0:T(4,128)S(1)} %pair_forces.2), channel_id=1, replica_groups=mesh['gx'=8,'yz'=4] {'gx','yz'}, dimensions={0} | all-to-all | bytes 131072 | tf_op jit(solution)/shard_map/all_to_all | solution.py:550
  48.2 14.0 %pair_forces.3 = (f32[3,48]{1,0:T(4,128)S(1)}, f32[3,48]{1,0:T(4,128)}, f32[3,48]{1,0:T(4,128)S(1)}, f32[32,3,12]{2,1,0:T(4,128)S(1)}) custom-call(f32[1,48]{1,0:T(1,128)S(1)} %get-tuple-element.22.used_ref, s32[6,1024]{1,0:T(8,128)S(1)} %get-tuple-element.23.neigh_ref, s32[6,1024]{1,0:T(8,128)S(1)} %get-tuple-element.24.centre_ref, ...), custom_call_target="tpu_custom_call" | custom-call | flops 8493465600 | bytes 4194304 | tf_op jit(solution)/shard_map/pair_forces/pallas_call | solution.py:505
  62.2 17.3 %all_to_all.16.in_ref = f32[32,3,12]{2,1,0:T(4,128)S(1)} all-to-all(f32[32,3,12]{2,1,0:T(4,128)S(1)} %get-tuple-element.38), channel_id=1, replica_groups=mesh['gx'=8,'yz'=4] {'gx','yz'}, dimensions={0} | all-to-all | bytes 9216 | tf_op jit(solution)/shard_map/all_to_all | solution.py:550
  79.5 0.8 %last.1 = (f32[3,48]{1,0:T(4,128)}, f32[3,48]{1,0:T(4,128)}) custom-call(f32[3,48]{1,0:T(4,128)S(1)} %get-tuple-element.36.own_ref, s32[8,12]{1,0:T(8,128)S(1)} %copy-done, f32[3,48]{1,0:T(4,128)S(1)} %get-tuple-element.37.half_two_ref, s32[1,48]{1,0:T(1,128)S(1)} %bitcast.11, f32[32,3,12]{2,1,0:T(4,128)S(1)} %all_to_all.16.in_ref), custom_call_target="tpu_custom_call" | custom-call | tf_op jit(solution)/shard_map/last/pallas_call | solution.py:532
  (2 shorter events, 0.0 us)
Async XLA Ops:
  0.6 0.7 copy-start.13
  0.6 0.8 copy-start.4
  0.7 0.7 copy-start.12
  0.7 0.8 copy-start.3
  0.7 0.8 copy-start
  1.4 0.7 copy-start.2
  1.4 0.7 copy-start.1
  1.4 0.7 copy-start.5
  3.0 7.3 %copy-start.8 = (s32[48,128]{1,0:T(8,128)S(1)}, s32[48,128]{1,0:T(8,128)}, u32[]{:S(2)}) copy-start(s32[48,128]{1,0:T(8,128)} %slots_ref.1) | copy-start | bytes 73732
  3.0 14.8 %all-to-all-start = ((f32[32,4,128]{2,1,0:T(4,128)}), f32[32,4,128]{2,1,0:T(4,128)S(1)}, u32[]{:S(2)}, u32[]{:S(2)}) async-start(f32[32,4,128]{2,1,0:T(4,128)} %get-tuple-element.33), calls=%async_computation | async-start | bytes 131072 | tf_op jit(solution)/shard_map/all_to_all | solution.py:550
  10.3 0.9 %copy-start.11 = (bf16[512]{0:T(512)(128)(2,1)S(1)}, bf16[512]{0:T(512)(128)(2,1)}, u32[]{:S(2)}) copy-start(bf16[512]{0:T(512)(128)(2,1)} %param.27) | copy-start | bytes 3076
  10.3 1.1 %copy-start.6 = (bf16[1,576,512]{2,1,0:T(8,128)(2,1)S(1)}, bf16[1,576,512]{2,1,0:T(8,128)(2,1)}, u32[]{:S(2)}) copy-start(bf16[1,576,512]{2,1,0:T(8,128)(2,1)} %param.26) | copy-start | bytes 1769476
  10.4 1.1 %copy-start.7 = (bf16[1,512,64]{1,2,0:T(8,128)(2,1)S(1)}, bf16[1,512,64]{1,2,0:T(8,128)(2,1)}, u32[]{:S(2)}) copy-start(bf16[1,512,64]{1,2,0:T(8,128)(2,1)} %param.25) | copy-start | bytes 196612
  10.4 1.1 %copy-start.9 = (bf16[2,8,512]{2,1,0:T(8,128)(2,1)S(1)}, bf16[2,8,512]{2,1,0:T(8,128)(2,1)}, u32[]{:S(2)}) copy-start(bf16[2,8,512]{2,1,0:T(8,128)(2,1)} %embed_ref.1) | copy-start | bytes 49156
  10.4 1.0 %copy-start.10 = (bf16[8,512]{1,0:T(8,128)(2,1)S(1)}, bf16[8,512]{1,0:T(8,128)(2,1)}, u32[]{:S(2)}) copy-start(bf16[8,512]{1,0:T(8,128)(2,1)} %radial_ref.1) | copy-start | bytes 24580
